TPU v7x, 512 devices: a whole 4x4x16 slice. The times are simulated.
512 devices in a mesh: dp: 8 (over y, core), space: 64 (over x, z).
Axes of the slice: x: 4, y: 4, z: 16, core: 2. Of those that a mesh axis runs over, the one named last changes fastest.
Arguments:
- fine_features: bfloat16 [8, 1536, 4, 4, 256], P('dp', 'space'), may hold values from -6 to 6
- cotangent: bfloat16 [8, 1536, 4, 4, 256], P('dp', 'space'), may hold values from -0.01953125 to 0.01953125
- down_weight: bfloat16 [1728, 128], replicated, may hold values from -0.15625 to 0.15625
- coarse_weight: bfloat16 [3456, 128], replicated, may hold values from -0.109375 to 0.109375
- up_weight: bfloat16 [128, 512], replicated, may hold values from -0.5 to 0.5
- fine_neighbours: int32 [8, 1536, 7], P('dp', 'space'), may hold values from -1 to 1535, as said below
- children: int32 [8, 384, 8], P('dp', 'space'), may hold values from -1 to 1535, as said below
- parent_slots: int32 [8, 1536], P('dp', 'space'), may hold values from 0 to 3071, as said below
- coarse_neighbours: int32 [8, 384, 26], P('dp', 'space'), may hold values from -1 to 383, as said below
Outputs:
- decoded: bfloat16 [8, 1536, 4, 4, 256], P('dp', 'space')
- grad_down: float32 [221184], P('space')
- grad_coarse: float32 [442368], P('space')
- grad_up: float32 [65536], P('space')
Inputs may be any that keep to these rules, and one draw needn't show every extreme that they name: Bricks sit in a strip of the map with coordinates; fine_neighbours lists the occupied brick at the named lower offset. Every listed neighbour of fine brick f is lower than f and at least 24 * (f // 24 - 1). Each coarse brick has 3 to 5 children; children[t, c, o] = f exactly when parent_slots[t, f] = 8 c + o, and every fine brick is the child of one coarse brick. The children of coarse brick c lie from 24 * (c // 6) to 24 * (c // 6 + 1), both included. `parent_slots`: the parent of fine brick f is a coarse brick from 6 * (f // 24) to 6 * (f // 24 + 1) - 1, or the coarse brick 6 * (f // 24) - 1. `coarse_neighbours`: Symmetric: if the entry of c for offset (sx, sy, sz) is d, the entry of d for the opposite offset is c. Coarse brick c lies in cross-section c // 2 of the strip, and a listed neighbour of c for offset (sx, sy, sz) lies in cross-section c // 2 + sx.
All inputs are finite; a program needn't handle non-finite values.
Results may differ from a plain program's by a relative error of at most 0.0065.
The roundings to bfloat16 on the way count: a program that leaves them out, or rounds other values in their place, can miss the bound.
Values may be sent and summed in bfloat16 or wider, within the bound.
No kernel may reach another device: no remote copies, remote signals or barrier semaphores. Data moves between devices by JAX's collectives and lax.ppermute only.
A program may use at most 64 MiB of HBM per device.

v0:
```python
import jax
import jax.numpy as jnp
from jax import lax
from jax.sharding import PartitionSpec as P


def padded_2(x, sides, width):
    for axis, dim in sides:
        size, length = (lax.axis_size(axis), x.shape[dim])
        up = [(i, (i + 1) % size) for i in range(size - 1)]
        down = [(j, i) for i, j in up]
        last = lax.slice_in_dim(x, length - width, length, axis=dim)
        leading = lax.slice_in_dim(x, 0, width, axis=dim)
        before = lax.ppermute(last, axis, up)
        after = lax.ppermute(leading, axis, down)
        x = jnp.concatenate([before, x, after], axis=dim)
    return x


def from_behind(block, axis, distance):
    devices = range(lax.axis_size(axis))
    route = [(i - distance, i) for i in devices if i - distance in devices]
    return lax.ppermute(block, axis, route)


def silu_slope(inputs):
    squash = jax.nn.sigmoid(inputs)
    return squash * (1.0 + inputs * (1.0 - squash))


def edge_pick(offset_value, brick_edge):
    if offset_value < 0:
        return slice(brick_edge - 1, brick_edge)
    if offset_value > 0:
        return slice(0, 1)
    return slice(0, brick_edge)


def edge_place(offset_value, brick_edge):
    if offset_value < 0:
        return slice(0, 1)
    if offset_value > 0:
        return slice(brick_edge + 1, brick_edge + 2)
    return slice(1, brick_edge + 1)


def fine_planes(bricks):
    return jnp.stack([bricks[:, -1], bricks[:, :, -1], bricks[:, :, :, -1]], axis=1)


def fine_padded(bricks, planes_all, neighbours):
    brick_edge = bricks.shape[1]
    padded = jnp.pad(bricks, ((0, 0), (1, 0), (1, 0), (1, 0), (0, 0)))
    for bit_code in range(1, 8):
        shift_x = bit_code // 4
        shift_y = bit_code // 2 % 2
        shift_z = bit_code % 2
        picked = planes_all[neighbours[:, bit_code - 1]]
        if shift_x:
            values = picked[:, 0][
                :, edge_pick(-shift_y, brick_edge), edge_pick(-shift_z, brick_edge)
            ][:, None]
        elif shift_y:
            values = picked[:, 1][:, :, edge_pick(-shift_z, brick_edge)][:, :, None]
        else:
            values = picked[:, 2][:, :, :, None]
        place_x = slice(0, 1) if shift_x else slice(1, brick_edge + 1)
        place_y = slice(0, 1) if shift_y else slice(1, brick_edge + 1)
        place_z = slice(0, 1) if shift_z else slice(1, brick_edge + 1)
        padded = padded.at[:, place_x, place_y, place_z].set(values)
    return padded


def fine_columns(padded, half_edge):
    tap_list = []
    for tap_code in range(27):
        along_x = tap_code // 9
        along_y = tap_code // 3 % 3
        along_z = tap_code % 3
        tap_list.append(
            padded[
                :,
                along_x : along_x + 2 * half_edge - 1 : 2,
                along_y : along_y + 2 * half_edge - 1 : 2,
                along_z : along_z + 2 * half_edge - 1 : 2,
            ]
        )
    stacked = jnp.stack(tap_list, axis=4)
    return stacked.reshape(-1, 27 * stacked.shape[-1])


def octants_to_bricks(patches):
    brick_count = patches.shape[0]
    half_edge = patches.shape[2]
    channels = patches.shape[-1]
    arranged = patches.reshape(brick_count, 2, 2, 2, half_edge, half_edge, half_edge, channels)
    arranged = arranged.transpose(0, 1, 4, 2, 5, 3, 6, 7)
    return arranged.reshape(brick_count, 2 * half_edge, 2 * half_edge, 2 * half_edge, channels)


def bricks_to_octants(bricks):
    brick_count = bricks.shape[0]
    half_edge = bricks.shape[1] // 2
    channels = bricks.shape[-1]
    arranged = bricks.reshape(brick_count, 2, half_edge, 2, half_edge, 2, half_edge, channels)
    arranged = arranged.transpose(0, 1, 3, 5, 2, 4, 6, 7)
    return arranged.reshape(brick_count * 8, half_edge, half_edge, half_edge, channels)


def coarse_faces(bricks):
    return jnp.stack(
        [
            bricks[:, 0],
            bricks[:, -1],
            bricks[:, :, 0],
            bricks[:, :, -1],
            bricks[:, :, :, 0],
            bricks[:, :, :, -1],
        ],
        axis=1,
    )


def coarse_padded(bricks, faces_all, neighbours):
    brick_edge = bricks.shape[1]
    padded = jnp.pad(bricks, ((0, 0), (1, 1), (1, 1), (1, 1), (0, 0)))
    offset_codes = [offset_code for offset_code in range(27) if offset_code != 13]
    for column_index, offset_code in enumerate(offset_codes):
        off_x = offset_code // 9 - 1
        off_y = offset_code // 3 % 3 - 1
        off_z = offset_code % 3 - 1
        picked = faces_all[neighbours[:, column_index]]
        if off_x != 0:
            values = picked[:, 1 if off_x < 0 else 0][
                :, edge_pick(off_y, brick_edge), edge_pick(off_z, brick_edge)
            ][:, None]
        elif off_y != 0:
            values = picked[:, 3 if off_y < 0 else 2][:, :, edge_pick(off_z, brick_edge)][
                :, :, None
            ]
        else:
            values = picked[:, 5 if off_z < 0 else 4][:, :, :, None]
        padded = padded.at[
            :,
            edge_place(off_x, brick_edge),
            edge_place(off_y, brick_edge),
            edge_place(off_z, brick_edge),
        ].set(values)
    return padded


def pair_taps(padded, along_x, along_y, reverse):
    brick_edge = padded.shape[1] - 2
    pieces = []
    for along_z in range(3):
        if reverse:
            lows = (2 - along_x, 2 - along_y, 2 - along_z)
        else:
            lows = (along_x, along_y, along_z)
        pieces.append(
            padded[
                :,
                lows[0] : lows[0] + brick_edge,
                lows[1] : lows[1] + brick_edge,
                lows[2] : lows[2] + brick_edge,
            ]
        )
    gathered_taps = jnp.concatenate(pieces, axis=-1)
    return gathered_taps.reshape(-1, gathered_taps.shape[-1])


def coarse_forward(padded, weight):
    channels = weight.shape[0] // 27
    summed = None
    for pair_code in range(9):
        gathered_taps = pair_taps(padded, pair_code // 3, pair_code % 3, False)
        weight_rows = weight[pair_code * 3 * channels : (pair_code + 1) * 3 * channels]
        partial_value = jnp.dot(gathered_taps, weight_rows, preferred_element_type=jnp.float32)
        summed = partial_value if summed is None else summed + partial_value
    return summed


def coarse_weight_grad(padded, slope_rows):
    blocks = []
    for pair_code in range(9):
        gathered_taps = pair_taps(padded, pair_code // 3, pair_code % 3, False)
        blocks.append(
            lax.dot_general(
                gathered_taps,
                slope_rows,
                (((0,), (0,)), ((), ())),
                preferred_element_type=jnp.float32,
            )
        )
    return jnp.concatenate(blocks, axis=0)


def coarse_transpose(padded, weight):
    channels_in = weight.shape[0] // 27
    channels_out = weight.shape[1]
    summed = None
    for pair_code in range(9):
        gathered_taps = pair_taps(padded, pair_code // 3, pair_code % 3, True)
        weight_block = weight[pair_code * 3 * channels_in : (pair_code + 1) * 3 * channels_in]
        weight_block = (
            weight_block.reshape(3, channels_in, channels_out)
            .transpose(0, 2, 1)
            .reshape(3 * channels_out, channels_in)
        )
        partial_value = jnp.dot(gathered_taps, weight_block, preferred_element_type=jnp.float32)
        summed = partial_value if summed is None else summed + partial_value
    return summed


def wide_faces(faces_own, forward):
    count = faces_own.shape[0]
    if forward:
        return padded_2(faces_own, (("space", 0),), count)
    return padded_2(faces_own, (("space", 0),), count)


def parent_patches(octants, parent_list, place_index, forward):
    patch_count = octants.shape[0]
    half_edge = octants.shape[1]
    channels = octants.shape[-1]
    tail_octants = octants[patch_count - 8 :].reshape(8, half_edge, half_edge, half_edge * channels)
    if forward:
        arrived = from_behind(tail_octants, "space", 1)
    else:
        arrived = from_behind(tail_octants, "space", 1)
    patch_pool = jnp.concatenate(
        [arrived.reshape(8, half_edge, half_edge, half_edge, channels), octants], axis=0
    )
    offset_slot = (patch_count // 8 * place_index - 1) * 8
    return patch_pool[parent_list - offset_slot]


def body(
    fine_features,
    cotangent,
    down_weight,
    coarse_weight,
    up_weight,
    fine_neighbours,
    children,
    parent_slots,
    coarse_neighbours,
):
    place_index = lax.axis_index("space")
    brick_edge = fine_features.shape[2]
    half_edge = brick_edge // 2
    fine_width = down_weight.shape[0] // 27
    coarse_width = down_weight.shape[1]
    fine_count = fine_features.shape[1]
    coarse_count = children.shape[1]
    bricks = fine_features.reshape(fine_count, brick_edge, brick_edge, brick_edge, fine_width)
    own_planes = fine_planes(bricks).reshape(fine_count, 3, brick_edge, brick_edge * fine_width)
    prev_planes = from_behind(own_planes, "space", 1)
    zero_planes = jnp.zeros((1, 3, brick_edge, brick_edge * fine_width), jnp.bfloat16)
    planes_all = jnp.concatenate([prev_planes, own_planes, zero_planes], axis=0)
    planes_all = planes_all.reshape(2 * fine_count + 1, 3, brick_edge, brick_edge, fine_width)
    fine_nbr = fine_neighbours[0]
    local_fine = jnp.where(fine_nbr < 0, 2 * fine_count, fine_nbr - fine_count * (place_index - 1))
    padded_fine = fine_padded(bricks, planes_all, local_fine)
    columns = fine_columns(padded_fine, half_edge)
    pre_down = jnp.dot(columns, down_weight, preferred_element_type=jnp.float32)
    hidden = jax.nn.silu(pre_down).astype(jnp.bfloat16)
    patches = hidden.reshape(fine_count, half_edge, half_edge, half_edge * coarse_width)
    next_first = from_behind(patches[0:1], "space", -1)
    zero_patch = jnp.zeros((1, half_edge, half_edge, half_edge * coarse_width), jnp.bfloat16)
    patch_pool = jnp.concatenate([patches, next_first, zero_patch], axis=0)
    patch_pool = patch_pool.reshape(fine_count + 2, half_edge, half_edge, half_edge, coarse_width)
    child_list = children[0]
    child_local = jnp.where(child_list < 0, fine_count + 1, child_list - fine_count * place_index)
    coarse_in = octants_to_bricks(patch_pool[child_local])
    coarse_nbr = coarse_neighbours[0]
    local_coarse = jnp.where(
        coarse_nbr < 0, 3 * coarse_count, coarse_nbr - coarse_count * (place_index - 1)
    )
    zero_faces = jnp.zeros((1, 6, brick_edge, brick_edge * coarse_width), jnp.bfloat16)
    faces_own = coarse_faces(coarse_in).reshape(
        coarse_count, 6, brick_edge, brick_edge * coarse_width
    )
    faces_wide = wide_faces(faces_own, True)
    faces_all = jnp.concatenate([faces_wide, zero_faces], axis=0)
    faces_all = faces_all.reshape(3 * coarse_count + 1, 6, brick_edge, brick_edge, coarse_width)
    padded_in = coarse_padded(coarse_in, faces_all, local_coarse)
    pre_coarse = coarse_forward(padded_in, coarse_weight)
    coarse_out = jax.nn.silu(pre_coarse).astype(jnp.bfloat16)
    coarse_out = coarse_out.reshape(coarse_count, brick_edge, brick_edge, brick_edge, coarse_width)
    parent_list = parent_slots[0]
    up_input = parent_patches(bricks_to_octants(coarse_out), parent_list, place_index, True)
    up_rows = up_input.reshape(-1, coarse_width)
    up_out = jnp.dot(up_rows, up_weight, preferred_element_type=jnp.float32)
    up_grid = up_out.reshape(
        fine_count, half_edge, half_edge, half_edge, 2, 2, 2, fine_width
    ).transpose(0, 1, 4, 2, 5, 3, 6, 7)
    up_grid = up_grid.reshape(fine_count, brick_edge, brick_edge, brick_edge, fine_width)
    joined = up_grid + bricks.astype(jnp.float32)
    decoded = jax.nn.silu(joined).astype(jnp.bfloat16).reshape(fine_features.shape)
    cot_grid = cotangent.reshape(fine_count, brick_edge, brick_edge, brick_edge, fine_width).astype(
        jnp.float32
    )
    out_grad = (cot_grid * silu_slope(joined)).astype(jnp.bfloat16)
    out_rows = out_grad.reshape(
        fine_count, half_edge, 2, half_edge, 2, half_edge, 2, fine_width
    ).transpose(0, 1, 3, 5, 2, 4, 6, 7)
    out_rows = out_rows.reshape(-1, 8 * fine_width)
    grad_up = lax.dot_general(
        up_rows, out_rows, (((0,), (0,)), ((), ())), preferred_element_type=jnp.float32
    )
    patch_grad = lax.dot_general(
        out_rows, up_weight, (((1,), (1,)), ((), ())), preferred_element_type=jnp.float32
    ).astype(jnp.bfloat16)
    grad_patches = patch_grad.reshape(fine_count, half_edge, half_edge, half_edge * coarse_width)
    next_grad = from_behind(grad_patches[0:1], "space", -1)
    grad_pool = jnp.concatenate([grad_patches, next_grad, zero_patch], axis=0)
    grad_pool = grad_pool.reshape(fine_count + 2, half_edge, half_edge, half_edge, coarse_width)
    coarse_grad_out = octants_to_bricks(grad_pool[child_local])
    coarse_slope = (
        coarse_grad_out.reshape(-1, coarse_width).astype(jnp.float32) * silu_slope(pre_coarse)
    ).astype(jnp.bfloat16)
    grad_coarse = coarse_weight_grad(padded_in, coarse_slope)
    slope_bricks = coarse_slope.reshape(
        coarse_count, brick_edge, brick_edge, brick_edge, coarse_width
    )
    slope_faces = coarse_faces(slope_bricks).reshape(
        coarse_count, 6, brick_edge, brick_edge * coarse_width
    )
    slope_wide = wide_faces(slope_faces, False)
    slope_all = jnp.concatenate([slope_wide, zero_faces], axis=0)
    slope_all = slope_all.reshape(3 * coarse_count + 1, 6, brick_edge, brick_edge, coarse_width)
    padded_slope = coarse_padded(slope_bricks, slope_all, local_coarse)
    input_grad = coarse_transpose(padded_slope, coarse_weight).astype(jnp.bfloat16)
    input_bricks = input_grad.reshape(
        coarse_count, brick_edge, brick_edge, brick_edge, coarse_width
    )
    hidden_grad = parent_patches(bricks_to_octants(input_bricks), parent_list, place_index, False)
    down_slope = (
        hidden_grad.reshape(-1, coarse_width).astype(jnp.float32) * silu_slope(pre_down)
    ).astype(jnp.bfloat16)
    grad_down = lax.dot_general(
        columns, down_slope, (((0,), (0,)), ((), ())), preferred_element_type=jnp.float32
    )
    flat_down = grad_down.reshape(-1)
    flat_coarse = grad_coarse.reshape(-1)
    flat_up = grad_up.reshape(-1)
    whole_down, whole_coarse, whole_up = lax.psum(
        (flat_down, flat_coarse, flat_up), ("dp", "space")
    )
    space_count = lax.axis_size("space")
    share_down = lax.dynamic_slice_in_dim(
        whole_down,
        place_index * (flat_down.shape[0] // space_count),
        flat_down.shape[0] // space_count,
    )
    share_coarse = lax.dynamic_slice_in_dim(
        whole_coarse,
        place_index * (flat_coarse.shape[0] // space_count),
        flat_coarse.shape[0] // space_count,
    )
    share_up = lax.dynamic_slice_in_dim(
        whole_up, place_index * (flat_up.shape[0] // space_count), flat_up.shape[0] // space_count
    )
    return (decoded, share_down, share_coarse, share_up)


def solution(mesh):
    in_specs = (
        P("dp", "space", None, None, None),
        P("dp", "space", None, None, None),
        P(),
        P(),
        P(),
        P("dp", "space", None),
        P("dp", "space", None),
        P("dp", "space"),
        P("dp", "space", None),
    )
    out_specs = (P("dp", "space", None, None, None), P("space"), P("space"), P("space"))
    return jax.shard_map(body, mesh=mesh, in_specs=in_specs, out_specs=out_specs, check_vma=False)
```

profile of v0, /device:TPU:1, one launch (start us, length us, event | category | flops | bytes accessed | tf_op | source)
XLA Modules:
  0.0 734.9 jit_solution(11911529440482196568)
XLA Ops:
  7.2 1.8 copy_convert_fusion
  10.0 4.4 collective-permute-start
  23.6 7.6 %scatter.196 = bf16[24,5,5,5,64]{4,3,0,2,1:T(8,128)(2,1)S(1)} dynamic-update-slice(bf16[24,5,5,5,64]{4,3,0,2,1:T(8,128)(2,1)S(1)} %pad.247, bf16[24,4,4,1,64]{4,3,0,2,1:T(2,128)(2,1)S(1)} %copy.350, s32[]{:T(128)} %constant.1608.clone.1, s32[]{:T(128)} %constant.1614.clone.1, s32[]{:T(128)} %constant.1614.clone.1, s32[]{:T(128)} %constant.1608.clone.1, s32[]{:T(128)} %constant.1608.clone.1) | dynamic-update-slice | bytes 98308 | tf_op jit(solution)/shard_map/scatter | solution.py:70
  31.2 3.1 scatter.199
  34.3 1.7 scatter.200
  36.0 3.4 scatter.201
  39.4 1.9 scatter.204
  49.5 1.6 copy.360
  54.6 3.5 collective-permute-done.1
  61.1 4.7 collective-permute-start.2
  66.4 1.5 collective-permute-done.2
  88.8 1.5 scatter.229
  90.3 1.5 scatter.230
  93.3 1.7 fusion.59
  96.9 2.0 pad_maximum_fusion.7
  98.9 1.7 reshape.2974
  100.6 1.8 pad_maximum_fusion.8
  102.5 1.8 reshape.2975
  107.5 4.3 collective-permute-start.4
  115.5 1.6 copy.429
  117.1 1.6 copy.430
  118.7 1.6 copy.431
  128.7 1.7 collective-permute-start.5
  131.4 3.6 collective-permute-done.5
  138.4 5.2 collective-permute-start.6
  194.9 1.5 scatter.271
  199.5 1.6 fusion.57
  206.5 1.9 pad_maximum_fusion.16
  209.4 1.8 pad_maximum_fusion.17
  211.3 1.8 reshape.3031
  217.6 5.0 collective-permute-start.8
  227.9 495.8 %all-reduce.6.cloned.1.call-done = (f32[221184]{0:T(1024)}, f32[442368]{0:T(1024)}, f32[65536]{0:T(1024)}) async-done(((f32[221184]{0:T(1024)}, f32[442368]{0:T(1024)}, f32[65536]{0:T(1024)}), (f32[221184]{0:T(1024)}, f32[442368]{0:T(1024)}, f32[65536]{0:T(1024)})) %all-reduce.6.cloned.1.call-update) | async-done | bytes 2916368 | tf_op jit(solution)/shard_map/psum | solution.py:348
  (627 shorter events, 140.6 us)
Async XLA Ops:
  7.2 45.1 %copy-start = (bf16[1728,128]{1,0:T(8,128)(2,1)S(1)}, bf16[1728,128]{1,0:T(8,128)(2,1)}, u32[]{:S(2)}) copy-start(bf16[1728,128]{1,0:T(8,128)(2,1)} %param.129) | copy-start | bytes 1327108
  7.2 716.5 %all-reduce.6.cloned.1.call-start = ((), (), s32[]{:S(2)}) async-start(), calls=%async_computation | async-start | bytes 5832704 | tf_op jit(solution)/shard_map/psum | solution.py:348
  10.0 6.5 collective-permute-start
  15.4 55.3 %copy-start.40 = (s32[1024]{0:T(1024)}, s32[1024]{0:T(1024)S(1)}, u32[]{:S(2)}) copy-start(s32[1024]{0:T(1024)S(1)} %get-tuple-element.878) | copy-start | bytes 12292
  15.5 56.0 %copy-start.39 = (s32[1024]{0:T(1024)}, s32[1024]{0:T(1024)S(1)}, u32[]{:S(2)}) copy-start(s32[1024]{0:T(1024)S(1)} %get-tuple-element.877) | copy-start | bytes 12292
  15.5 56.7 %copy-start.42 = (s32[1024]{0:T(1024)}, s32[1024]{0:T(1024)S(1)}, u32[]{:S(2)}) copy-start(s32[1024]{0:T(1024)S(1)} %get-tuple-element.876) | copy-start | bytes 12292
  15.5 57.4 %copy-start.41 = (s32[1024]{0:T(1024)}, s32[1024]{0:T(1024)S(1)}, u32[]{:S(2)}) copy-start(s32[1024]{0:T(1024)S(1)} %get-tuple-element.875) | copy-start | bytes 12292
  15.5 58.1 %copy-start.44 = (s32[1024]{0:T(1024)}, s32[1024]{0:T(1024)S(1)}, u32[]{:S(2)}) copy-start(s32[1024]{0:T(1024)S(1)} %get-tuple-element.874) | copy-start | bytes 12292
  15.5 58.9 %copy-start.43 = (s32[1024]{0:T(1024)}, s32[1024]{0:T(1024)S(1)}, u32[]{:S(2)}) copy-start(s32[1024]{0:T(1024)S(1)} %get-tuple-element.873) | copy-start | bytes 12292
  15.5 59.6 %copy-start.46 = (s32[1024]{0:T(1024)}, s32[1024]{0:T(1024)S(1)}, u32[]{:S(2)}) copy-start(s32[1024]{0:T(1024)S(1)} %get-tuple-element.872) | copy-start | bytes 12292
  15.6 60.3 %copy-start.45 = (s32[1024]{0:T(1024)}, s32[1024]{0:T(1024)S(1)}, u32[]{:S(2)}) copy-start(s32[1024]{0:T(1024)S(1)} %get-tuple-element.871) | copy-start | bytes 12292
  15.6 61.0 %copy-start.48 = (s32[1024]{0:T(1024)}, s32[1024]{0:T(1024)S(1)}, u32[]{:S(2)}) copy-start(s32[1024]{0:T(1024)S(1)} %get-tuple-element.870) | copy-start | bytes 12292
  15.6 61.7 %copy-start.47 = (s32[1024]{0:T(1024)}, s32[1024]{0:T(1024)S(1)}, u32[]{:S(2)}) copy-start(s32[1024]{0:T(1024)S(1)} %get-tuple-element.869) | copy-start | bytes 12292
  15.6 62.4 %copy-start.50 = (s32[1024]{0:T(1024)}, s32[1024]{0:T(1024)S(1)}, u32[]{:S(2)}) copy-start(s32[1024]{0:T(1024)S(1)} %get-tuple-element.868) | copy-start | bytes 12292
  15.6 63.2 %copy-start.49 = (s32[1024]{0:T(1024)}, s32[1024]{0:T(1024)S(1)}, u32[]{:S(2)}) copy-start(s32[1024]{0:T(1024)S(1)} %get-tuple-element.867) | copy-start | bytes 12292
  15.7 63.9 %copy-start.52 = (s32[1024]{0:T(1024)}, s32[1024]{0:T(1024)S(1)}, u32[]{:S(2)}) copy-start(s32[1024]{0:T(1024)S(1)} %get-tuple-element.866) | copy-start | bytes 12292
  15.7 64.6 %copy-start.51 = (s32[1024]{0:T(1024)}, s32[1024]{0:T(1024)S(1)}, u32[]{:S(2)}) copy-start(s32[1024]{0:T(1024)S(1)} %get-tuple-element.865) | copy-start | bytes 12292
  15.7 65.3 %copy-start.54 = (s32[1024]{0:T(1024)}, s32[1024]{0:T(1024)S(1)}, u32[]{:S(2)}) copy-start(s32[1024]{0:T(1024)S(1)} %get-tuple-element.864) | copy-start | bytes 12292
  15.7 66.0 %copy-start.53 = (s32[1024]{0:T(1024)}, s32[1024]{0:T(1024)S(1)}, u32[]{:S(2)}) copy-start(s32[1024]{0:T(1024)S(1)} %get-tuple-element.863) | copy-start | bytes 12292
  15.7 66.7 %copy-start.56 = (s32[1024]{0:T(1024)}, s32[1024]{0:T(1024)S(1)}, u32[]{:S(2)}) copy-start(s32[1024]{0:T(1024)S(1)} %get-tuple-element.862) | copy-start | bytes 12292
  15.8 67.4 %copy-start.55 = (s32[1024]{0:T(1024)}, s32[1024]{0:T(1024)S(1)}, u32[]{:S(2)}) copy-start(s32[1024]{0:T(1024)S(1)} %get-tuple-element.861) | copy-start | bytes 12292
  16.3 67.6 %copy-start.58 = (s32[1024]{0:T(1024)}, s32[1024]{0:T(1024)S(1)}, u32[]{:S(2)}) copy-start(s32[1024]{0:T(1024)S(1)} %get-tuple-element.860) | copy-start | bytes 12292
  16.3 68.3 %copy-start.57 = (s32[1024]{0:T(1024)}, s32[1024]{0:T(1024)S(1)}, u32[]{:S(2)}) copy-start(s32[1024]{0:T(1024)S(1)} %get-tuple-element.859) | copy-start | bytes 12292
  53.2 4.9 collective-permute-start.1
  59.8 6.6 collective-permute-start.3
  61.1 6.8 collective-permute-start.2
  65.9 20.9 %copy-start.61 = (s32[1024]{0:T(1024)}, s32[1024]{0:T(1024)S(1)}, u32[]{:S(2)}) copy-start(s32[1024]{0:T(1024)S(1)} %get-tuple-element.856) | copy-start | bytes 12292
  107.5 17.5 %collective-permute-start.4 = (bf16[8,2,2,256]{3,0,2,1:T(8,128)(2,1)S(1)}, bf16[8,2,2,256]{3,0,2,1:T(8,128)(2,1)S(1)}, u32[]{:S(2)}, u32[]{:S(2)}) collective-permute-start(bf16[8,2,2,256]{3,0,2,1:T(8,128)(2,1)S(1)} %bitcast.517), channel_id=1, source_target_pairs={{0,1},{1,2},{2,3},{3,4},{4,5},{5,6},{6,7},{7,8},{8,9},{9,10},{10,1... | collective-permute-start | bytes 49160 | tf_op jit(solution)/shard_map/ppermute | solution.py:23
  128.7 6.3 collective-permute-start.5
  137.0 10.2 %collective-permute-start.7 = (bf16[6,6,4,512]{3,2,0,1:T(4,128)(2,1)S(1)}, bf16[6,6,4,512]{3,2,0,1:T(4,128)(2,1)S(1)}, u32[]{:S(2)}, u32[]{:S(2)}) collective-permute-start(bf16[6,6,4,512]{3,2,0,1:T(4,128)(2,1)S(1)} %constant_dynamic-update-slice_fusion.36), channel_id=1, source_target_pairs={{1,0},{2,1},{3,2},{4,3},{5,4},{6,5},{7,6},{8,7},{9,8},{10,9},{11,1... | collective-permute-start | bytes 442376 | tf_op jit(solution)/shard_map/ppermute | solution.py:15
  138.4 8.8 %collective-permute-start.6 = (bf16[6,6,4,512]{3,2,0,1:T(4,128)(2,1)S(1)}, bf16[6,6,4,512]{3,2,0,1:T(4,128)(2,1)S(1)}, u32[]{:S(2)}, u32[]{:S(2)}) collective-permute-start(bf16[6,6,4,512]{3,2,0,1:T(4,128)(2,1)S(1)} %constant_dynamic-update-slice_fusion.36), channel_id=1, source_target_pairs={{0,1},{1,2},{2,3},{3,4},{4,5},{5,6},{6,7},{7,8},{8,9},{9,10},{10,1... | collective-permute-start | bytes 442376 | tf_op jit(solution)/shard_map/ppermute | solution.py:14
  217.6 6.1 collective-permute-start.8
  (50 other events, 300.2 us)
Sparse Core Ops, SparseCore 0:
  226.1 497.5 all-reduce.5
where the time goes:
time: 745 us; the launch traced here: 735 us
  waiting for transfers between devices  505 us (68%)
  local copies, waits for them, and re-layouts  151 us (20%)
  starting transfers between devices  29.4 us (4%)
  between operations  18 us (2%)
  other arithmetic  17.7 us (2%)
  matrix products  14 us (2%)
    psum x1, waiting for transfers between devices, body(): lax.psum((flat_down, flat_coarse, flat_up), ('dp', 'space'))  496 us
    gather x52, local copies, waits for them, and re-layouts, coarse_padded(): picked = faces_all[neighbours[:, column_index]]  50 us
    scatter x7, local copies, waits for them, and re-layouts, fine_padded(): padded = padded.at[:, place_x, place_y, place_z].set(values)  18.1 us
    ppermute x5, starting transfers between devices, from_behind(): return lax.ppermute(block, axis, route)  16.7 us
  transfers between devices with their start and end apart: 10, of which 6 were waited for; matrix products, arithmetic and copies ran while one was open for 3% of the time, Pallas kernels for 0%

commit v1 on v0

v1 whole, which is shorter than its diff:
```python
import functools

import jax
import jax.numpy as jnp
from jax import lax
from jax.experimental import pallas as pl
from jax.experimental.pallas import tpu as pltpu
from jax.sharding import PartitionSpec as P

BF = jnp.bfloat16
F32 = jnp.float32
FB = 24
CB = 6
ROWS = 80
CR = 16
XL = 4096
IDX = 2 * XL
TILES = 96


def plane_lanes(i, j):
    if i == 3:
        return (j * 256, 256)
    if j == 3:
        return (1024 + i * 256, 256)
    return (1792 + (i * 3 + j) * 128, 128)


def upper_pieces():
    pieces = [(3 * 1024, 1024)]
    pieces += [((i * 4 + 3) * 256, 256) for i in range(3)]
    pieces += [((i * 4 + j) * 256 + 128, 128) for i in range(3) for j in range(3)]
    return pieces


UPPER = sum(width for _, width in upper_pieces())


def dot(a, b, dims=((1,), (0,))):
    return lax.dot_general(a, b, (dims, ((), ())), preferred_element_type=F32)


def gate(v):
    s = 1.0 / (1.0 + jnp.exp(-v))
    return v * s, s * (1.0 + v * (1.0 - s))


def axis_sides(half):
    inner = [(0, 0, half + 1), (0, 1, half + 3)]
    return inner + ([(-1, 1, 0)] if half else [(1, 0, 5)])


def halo_blocks(p, q):
    blocks = []
    for sx, ox, cx in axis_sides(p):
        for sy, oy, cy in axis_sides(q):
            for sz, oz, cells in (
                (0, 0, [(0, 1), (1, 2)]),
                (0, 1, [(0, 3), (1, 4)]),
                (-1, 1, [(1, 0)]),
                (1, 0, [(0, 5)]),
            ):
                code = 9 * (sx + 1) + 3 * (sy + 1) + sz + 1
                if code != 13:
                    targets = [(r, (cx, cy, cz)) for r, cz in cells]
                    blocks.append((code - (code > 13), 4 * ox + 2 * oy + oz, targets))
    return blocks


HALO = len(halo_blocks(0, 0)) * CR


def octant_of(x, y, z):
    return 4 * (x // 2) + 2 * (y // 2) + z // 2, 4 * (x % 2) + 2 * (y % 2) + z % 2


def kernel(
    core_ref,
    own_ref,
    prev_ref,
    next_ref,
    far_ref,
    wd_ref,
    wc_ref,
    wt_ref,
    wu_ref,
    dec_ref,
    sum_ref,
    wide_ref,
    src_ref,
    pad_ref,
    hid_ref,
    nl_ref,
    cin_ref,
    cp_ref,
    cslope_ref,
    cout_ref,
    cs_ref,
    sp_ref,
    cst_ref,
    gd_ref,
    gc_ref,
    gu_ref,
    t_ref,
):
    zeros8 = functools.partial(jnp.zeros, dtype=F32)

    def rows(lane, width):
        at = slice(lane, lane + width)
        parts = [r[:, at].astype(F32) for r in (prev_ref, own_ref, next_ref)]
        return jnp.concatenate(parts + [zeros8((ROWS - 3 * FB, width))], axis=0)

    idx = rows(IDX, 128)
    row = lax.broadcasted_iota(jnp.int32, (ROWS, 128), 0)
    lane = lax.broadcasted_iota(jnp.int32, (ROWS, 128), 1)
    block = jnp.where(row >= FB, 1.0, 0.0) + jnp.where(row >= 2 * FB, 1.0, 0.0)
    lane_f = lane.astype(F32)

    wide_ref[...] = jnp.zeros(wide_ref.shape, BF)
    for ab in range(9):
        tap = [wd_ref[(3 * ab + e) * 64 : (3 * ab + e + 1) * 64, :] for e in range(3)]
        for at, e in ((0, 1), (64, 2), (320, 0)):
            wide_ref[ab, at : at + 64, 0:128] = tap[e]
        for at, e in ((64, 0), (128, 1), (192, 2)):
            wide_ref[ab, at : at + 64, 128:256] = tap[e]

    at = 0
    for start, width in upper_pieces():
        parts = [far_ref[:, at : at + width].astype(F32)]
        parts += [r[:, start : start + width].astype(F32) for r in (prev_ref, own_ref, next_ref)]
        src_ref[:, at : at + width] = jnp.concatenate(parts, axis=0).astype(BF)
        at += width

    def pick(code):
        wanted = idx[:, code - 1 : code] + (24.0 * block[:, 0:1] - 1.0)
        wanted = jnp.where(idx[:, code - 1 : code] > 0.0, wanted, -1.0)
        hit = jnp.where(lane_f[:, 0 : 4 * FB] == wanted, 1.0, 0.0)
        return hit.astype(BF)

    picks = {code: pick(code) for code in range(1, 8)}

    def fetch(code, i, j, last):
        start, width = plane_lanes(i, j)
        if last:
            start, width = start + width - 128, 128
        return dot(picks[code], src_ref[:, start : start + width]).astype(BF)

    for ip in range(5):
        for jp in range(5):
            i, j = (ip - 1) % 4, (jp - 1) % 4
            code = 4 * (ip == 0) + 2 * (jp == 0)
            if code:
                own = fetch(code, i, j, False)
            else:
                own = rows((i * 4 + j) * 256, 256).astype(BF)
            pad_ref[ip * 5 + jp, :, 0:256] = own
            pad_ref[ip * 5 + jp, :, 256:384] = fetch(code + 1, i, j, True)

    slope_down = []
    for pq in range(4):
        p, q = pq // 2, pq % 2
        taps = [pad_ref[(2 * p + a) * 5 + 2 * q + b] for a in range(3) for b in range(3)]
        pre = dot(jnp.concatenate(taps, axis=1), wide_ref[...].reshape(9 * 384, 256))
        value, slope = gate(pre)
        hid_ref[:, pq * 256 : (pq + 1) * 256] = value.astype(BF)
        slope_down.append(slope[FB : 2 * FB])

    code = idx[:, 7:8]
    slot = jnp.where(code > 0.0, code + (48.0 * block[:, 0:1] - 9.0), -1.0)
    column = (lane % CR * 8 + lane // CR).astype(F32)
    up_f = jnp.where(column == slot, 1.0, 0.0)
    up = up_f.astype(BF)

    def to_coarse(ref):
        return dot(up, ref[...], ((0,), (0,)))

    row16 = lax.broadcasted_iota(jnp.int32, (CR, ROWS), 0)
    lane80 = lax.broadcasted_iota(jnp.int32, (CR, ROWS), 1)
    device = jnp.where(row16 >= CB, 1, 0) + jnp.where(row16 >= 2 * CB, 1, 0)
    choose = jnp.where(lane80 == row16 + (FB - CB) * device, 1.0, 0.0).astype(BF)
    listed = dot(choose, idx.astype(BF))
    device = device[:, 0:1].astype(F32)
    place = listed + (6.0 * device - 7.0)
    place = jnp.where((listed > 0.0) & (place >= 0.0) & (place < CR), place, -1000.0)
    lane16 = lane_f[0:CR]
    for pq in range(4):
        blocks = []
        for m, octant, _ in halo_blocks(pq // 2, pq % 2):
            wanted = place[:, 8 + m : 9 + m] + float(CR * octant)
            blocks.append(jnp.where(lane16 == wanted, 1.0, 0.0))
        nl_ref[pq] = jnp.concatenate(blocks, axis=0).astype(BF)

    def fill(flat_ref, padded_ref):
        for x in range(4):
            for y in range(4):
                for z in range(4):
                    o, v = octant_of(x, y, z)
                    padded_ref[x + 1, y + 1, z + 1] = flat_ref[
                        o * CR : (o + 1) * CR, v * 128 : (v + 1) * 128
                    ]
        for pq in range(4):
            got = dot(nl_ref[pq], flat_ref[:, pq * 256 : (pq + 1) * 256]).astype(BF)
            for n, (_, _, targets) in enumerate(halo_blocks(pq // 2, pq % 2)):
                for r, (cx, cy, cz) in targets:
                    padded_ref[cx, cy, cz] = got[n * CR : (n + 1) * CR, r * 128 : (r + 1) * 128]

    def convolve(padded_ref, weight_ref, x):
        taps = [
            padded_ref[x + a, b : b + 4, e : e + 4].reshape(16 * CR, 128)
            for a in range(3)
            for b in range(3)
            for e in range(3)
        ]
        return dot(jnp.concatenate(taps, axis=1), weight_ref[...])

    def scatter_flat(ref, value, x):
        for yz in range(16):
            o, v = octant_of(x, yz // 4, yz % 4)
            ref[o * CR : (o + 1) * CR, v * 128 : (v + 1) * 128] = value[yz * CR : (yz + 1) * CR]

    cin_ref[...] = to_coarse(hid_ref).astype(BF)
    fill(cin_ref, cp_ref)
    for x in range(4):
        value, slope = gate(convolve(cp_ref, wc_ref, x))
        cslope_ref[x] = slope
        scatter_flat(cout_ref, value.astype(BF), x)

    up_in = dot(up, cout_ref[...])
    own_in, own_grad = [], []
    for v in range(8):
        p, q, r = v // 4, v // 2 % 2, v % 2
        piece = up_in[:, v * 128 : (v + 1) * 128]
        own_in.append(piece[FB : 2 * FB])
        out = dot(piece.astype(BF), wu_ref[...])
        grads = []
        for ab in range(4):
            a, b = ab // 2, ab % 2
            at = ((2 * p + a) * 4 + 2 * q + b) * 256 + r * 128
            joined = out[:, ab * 128 : (ab + 1) * 128] + rows(at, 128)
            value, slope = gate(joined)
            dec_ref[:, at : at + 128] = value[FB : 2 * FB].astype(BF)
            grads.append(rows(XL + at, 128) * slope)
        grad = jnp.concatenate(grads, axis=1)
        own_grad.append(grad[FB : 2 * FB])
        back = dot(grad.astype(BF), wu_ref[...], ((1,), (1,)))
        hid_ref[:, v * 128 : (v + 1) * 128] = back.astype(BF)
    own_in = jnp.concatenate(own_in, axis=0).astype(BF)
    own_grad = jnp.concatenate(own_grad, axis=0).astype(BF)
    found = dot(own_in, own_grad, ((0,), (0,)))
    for n in range(4):
        gu_ref[n] = found[:, n * 128 : (n + 1) * 128]

    cin_ref[...] = to_coarse(hid_ref).astype(BF)
    row_c = lax.broadcasted_iota(jnp.int32, (16 * CR, 128), 0) % CR
    mine = (row_c >= CB) & (row_c < 2 * CB)
    for x in range(4):
        pieces = []
        for yz in range(16):
            o, v = octant_of(x, yz // 4, yz % 4)
            pieces.append(cin_ref[o * CR : (o + 1) * CR, v * 128 : (v + 1) * 128])
        grad = jnp.concatenate(pieces, axis=0).astype(F32) * cslope_ref[x]
        scatter_flat(cs_ref, grad.astype(BF), x)
        kept = jnp.where(mine, grad, 0.0)
        cst_ref[:, x * 256 : (x + 1) * 256] = jnp.transpose(kept).astype(BF)
    for ab in range(9):
        a, b = ab // 3, ab % 3
        taps = [
            cp_ref[a : a + 4, b : b + 4, e : e + 4].reshape(64 * CR, 128) for e in range(3)
        ]
        found = dot(cst_ref[...], jnp.concatenate(taps, axis=1))
        for e in range(3):
            at = (3 * ab + e) * 128
            gc_ref[at : at + 128, :] = jnp.transpose(found[:, e * 128 : (e + 1) * 128])

    fill(cs_ref, sp_ref)
    for x in range(4):
        scatter_flat(cin_ref, convolve(sp_ref, wt_ref, x).astype(BF), x)

    hidden_grad = dot(up_f[FB : 2 * FB].astype(BF), cin_ref[...])
    pieces = []
    for pq in range(4):
        slope = hidden_grad[:, pq * 256 : (pq + 1) * 256] * slope_down[pq]
        pieces += [zeros8((FB, 256)), slope, zeros8((ROWS - 2 * FB, 256))]
    down = jnp.concatenate(pieces, axis=0).astype(BF)
    for ab in range(9):
        a, b = ab // 3, ab % 3
        taps = [pad_ref[(2 * p + a) * 5 + 2 * q + b] for p in range(2) for q in range(2)]
        found = dot(down, jnp.concatenate(taps, axis=0), ((0,), (0,)))
        later = found[0:128, 0:128] + found[128:256, 128:256]
        first = found[0:128, 256:384] + found[128:256, 0:128]
        gd_ref[(3 * ab) * 64 : (3 * ab + 1) * 64, :] = jnp.transpose(first)[64:128]
        gd_ref[(3 * ab + 1) * 64 : (3 * ab + 3) * 64, :] = jnp.transpose(later)

    for t in range(27):
        t_ref[t] = gd_ref[pl.ds(t, 64, stride=27), :]
    for t in range(54):
        t_ref[27 + t] = gc_ref[pl.ds(t, 64, stride=54), :]
    for t in range(8):
        t_ref[81 + t] = gu_ref[t % 4, pl.ds(t // 4, 64, stride=2), :]
    t_ref[89:TILES] = jnp.zeros((TILES - 89, 64, 128), F32)
    core = core_ref[0]
    for side in range(2):
        half = core if side == 0 else 1 - core
        for y in range(4):
            for n in range(12):
                tile = t_ref[24 * y + 12 * half + n]
                sum_ref[side, y, :, n * 128 : (n + 1) * 128] = tile.astype(BF)


def local_pass(core, own, prev, nxt, far, wd, wc, wt, wu):
    vmem = pl.BlockSpec(memory_space=pltpu.VMEM)
    return pl.pallas_call(
        kernel,
        out_shape=(
            jax.ShapeDtypeStruct((FB, XL), BF),
            jax.ShapeDtypeStruct((2, 4, 64, 1536), BF),
        ),
        in_specs=[pl.BlockSpec(memory_space=pltpu.SMEM)] + [vmem] * 8,
        out_specs=(vmem, vmem),
        scratch_shapes=[
            pltpu.VMEM((9, 384, 256), BF),
            pltpu.VMEM((4 * FB, UPPER), BF),
            pltpu.VMEM((25, ROWS, 384), BF),
            pltpu.VMEM((ROWS, 1024), BF),
            pltpu.VMEM((4, HALO, 128), BF),
            pltpu.VMEM((8 * CR, 1024), BF),
            pltpu.VMEM((6, 6, 6, CR, 128), BF),
            pltpu.VMEM((4, 16 * CR, 128), F32),
            pltpu.VMEM((8 * CR, 1024), BF),
            pltpu.VMEM((8 * CR, 1024), BF),
            pltpu.VMEM((6, 6, 6, CR, 128), BF),
            pltpu.VMEM((128, 64 * CR), BF),
            pltpu.VMEM((1728, 128), F32),
            pltpu.VMEM((3456, 128), F32),
            pltpu.VMEM((4, 128, 128), F32),
            pltpu.VMEM((TILES, 64, 128), F32),
        ],
        compiler_params=pltpu.CompilerParams(vmem_limit_bytes=48 * 2**20),
    )(core, own, prev, nxt, far, wd, wc, wt, wu)


def shift(block, distance):
    size = lax.axis_size("space")
    route = [(i, i + distance) for i in range(size) if 0 <= i + distance < size]
    return lax.ppermute(block, "space", route)


def encode(fine_nbr, parents, coarse_nbr):
    place = lax.axis_index("space")
    fine = jnp.where(fine_nbr < 0, 0, fine_nbr - FB * (place - 1) + 1)
    parent = parents - 8 * (CB * place - 1) + 1
    coarse = jnp.where(coarse_nbr < 0, 0, coarse_nbr - CB * (place - 1) + 1)
    coarse = jnp.pad(coarse, ((0, FB - CB), (0, 0)))
    filler = jnp.zeros((FB, 128 - 34), jnp.int32)
    return jnp.concatenate([fine, parent[:, None], coarse, filler], axis=1).astype(BF)


def spread_sum(sums, groups_y, groups_x, groups_z, swap):
    arrived = lax.ppermute(sums[1], "dp", swap)
    held = (sums[0].astype(F32) + arrived.astype(F32)).astype(BF)
    held = lax.all_to_all(held, "dp", 0, 0, axis_index_groups=groups_y)
    held = jnp.sum(held.astype(F32), axis=0).astype(BF)
    x_count = len(groups_x[0])
    held = held.reshape(x_count, 64 // x_count, 1536)
    held = lax.all_to_all(held, "space", 0, 0, axis_index_groups=groups_x)
    held = jnp.sum(held.astype(F32), axis=0).astype(BF)
    held = held.reshape(held.shape[0], 12, 128)
    held = lax.all_to_all(held, "space", 0, 0, axis_index_groups=groups_z)
    held = jnp.sum(held.astype(F32), axis=0)
    whole = lax.all_gather(held, "dp").reshape(TILES, 128)
    return whole


def gradients(
    fine_features,
    cotangent,
    down_weight,
    coarse_weight,
    up_weight,
    fine_neighbours,
    children,
    parent_slots,
    coarse_neighbours,
):
    features = fine_features.reshape(FB, XL)
    index = encode(fine_neighbours[0], parent_slots[0], coarse_neighbours[0])
    own = jnp.concatenate([features, cotangent.reshape(FB, XL), index], axis=1)
    upper = jnp.concatenate([features[:, s : s + w] for s, w in upper_pieces()], axis=1)
    prev = shift(own, 1)
    nxt = shift(own, -1)
    far = shift(upper, 2)
    turned = coarse_weight.reshape(27, 128, 128)[::-1].transpose(0, 2, 1).reshape(27 * 128, 128)
    core = (lax.axis_index("dp") % 2).astype(jnp.int32).reshape(1)
    decoded, sums = local_pass(
        core, own, prev, nxt, far, down_weight, coarse_weight, turned, up_weight
    )
    return decoded, sums


def body(fine_features, *rest):
    decoded, sums = gradients(fine_features, *rest)
    dp, space = lax.axis_size("dp"), lax.axis_size("space")
    depth = 4
    length = space // depth
    groups_y = [[2 * y + c for y in range(dp // 2)] for c in range(2)]
    groups_x = [[x * length + z for x in range(depth)] for z in range(length)]
    groups_z = [[x * length + z for z in range(length)] for x in range(depth)]
    swap = [(i, i ^ 1) for i in range(dp)]
    whole = spread_sum(sums, groups_y, groups_x, groups_z, swap)
    return (
        decoded.reshape(fine_features.shape),
        whole[0:27].reshape(-1),
        whole[27:81].reshape(-1),
        whole[81:89].reshape(-1),
    )


def solution(mesh):
    in_specs = (
        P("dp", "space", None, None, None),
        P("dp", "space", None, None, None),
        P(),
        P(),
        P(),
        P("dp", "space", None),
        P("dp", "space", None),
        P("dp", "space"),
        P("dp", "space", None),
    )
    out_specs = (P("dp", "space", None, None, None), P("space"), P("space"), P("space"))
    return jax.shard_map(body, mesh=mesh, in_specs=in_specs, out_specs=out_specs, check_vma=False)
```

time: 745 us -> 120 us (0.16); the launches traced: 735 us -> 119 us
  waiting for transfers between devices: 505 us -> 12.6 us
  local copies, waits for them, and re-layouts: 151 us -> 17.1 us
  blocking collectives: 0 us -> 52.4 us
  between operations: 18 us -> 0.82 us
  other arithmetic: 17.7 us -> 1.81 us
  matrix products: 14 us -> 0 us
  Pallas kernels: 0 us -> 12.1 us
    psum x1 -> x0, waiting for transfers between devices: 496 us -> none  [body(): lax.psum((flat_down, flat_coarse, flat_up), ('dp', 'space'))]
    gather x65 -> x0, local copies, waits for them, and re-layouts: 58.4 us -> none  [the longest x52 50 us: coarse_padded(): picked = faces_all[neighbours[:, column_index]]]
    all_to_all x0 -> x2, blocking collectives: none -> 35.1 us  [the longest x1 21.2 us: spread_sum(): held = lax.all_to_all(held, 'space', 0, 0, axis_index_groups=groups_x)]
    scatter x59 -> x0, local copies, waits for them, and re-layouts: 28.5 us -> none  [the longest x7 18.1 us: fine_padded(): padded = padded.at[:, place_x, place_y, place_z].set(values)]
    all_gather x0 -> x1, blocking collectives: none -> 17.3 us  [spread_sum(): whole = lax.all_gather(held, 'dp').reshape(TILES, 128)]
    dot_general x32 -> x0, matrix products: 14 us -> none  [the longest x9 4.08 us: coarse_transpose(): jnp.dot(gathered_taps, weight_block, preferred_element_type=jnp.float32)]
    concatenate x25 -> x0, other arithmetic: 14 us -> none  [the longest x18 12.8 us: pair_taps(): gathered_taps = jnp.concatenate(pieces, axis=-1)]
    ppermute x9 -> x4, starting transfers between devices: 29.3 us -> 16.6 us  [the longest x3 11.8 us: shift(): return lax.ppermute(block, 'space', route)]
  transfers between devices with their start and end apart: 10 -> 5, of which waited for: 6 -> 2; matrix products, arithmetic and copies ran while one was open for 3% -> 10% of each run, Pallas kernels for 0% -> 0%
where the time goes in v1:
time: 120 us; the launch traced here: 119 us
  blocking collectives  52.4 us (44%)
  starting transfers between devices  22.6 us (19%)
  local copies, waits for them, and re-layouts  17.1 us (14%)
  waiting for transfers between devices  12.6 us (10%)
  Pallas kernels  12.1 us (10%)
  other arithmetic  1.81 us (2%)
    all_to_all x1, blocking collectives, spread_sum(): held = lax.all_to_all(held, 'space', 0, 0, axis_index_groups=groups_x)  21.2 us
    all_gather x1, blocking collectives, spread_sum(): whole = lax.all_gather(held, 'dp').reshape(TILES, 128)  17.3 us
    all_to_all x1, blocking collectives, spread_sum(): held = lax.all_to_all(held, 'dp', 0, 0, axis_index_groups=groups_y)  13.9 us
    pallas_call x1, Pallas kernels, local_pass(): pl.pallas_call(kernel, out_shape=(jax.ShapeDtypeStruct((FB, XL), BF), jax...  12.1 us
    ppermute x3, starting transfers between devices, shift(): return lax.ppermute(block, 'space', route)  11.8 us
    all_to_all x1, waiting for transfers between devices, spread_sum(): held = lax.all_to_all(held, 'space', 0, 0, axis_index_groups=groups_z)  10.7 us
    unnamed x24, local copies, waits for them, and re-layouts  7.98 us
    all_to_all x1, starting transfers between devices, spread_sum(): held = lax.all_to_all(held, 'space', 0, 0, axis_index_groups=groups_z)  5.99 us
  transfers between devices with their start and end apart: 5, of which 2 were waited for; matrix products, arithmetic and copies ran while one was open for 10% of the time, Pallas kernels for 0%

profile of v1, /device:TPU:1, one launch (start us, length us, event | category | flops | bytes accessed | tf_op | source)
XLA Modules:
  0.0 119.4 jit_solution(1268138435934087179)
XLA Ops:
  0.6 0.7 convert_bitcast_fusion
  1.5 0.8 copy.30
  2.3 1.1 reshape.83
  3.3 1.1 reshape.84
  4.4 0.7 fusion.5
  5.2 1.3 %collective-permute-start.1 = (bf16[24,8320]{1,0:T(8,128)(2,1)S(1)}, bf16[24,8320]{1,0:T(8,128)(2,1)S(1)}, u32[]{:S(2)}, u32[]{:S(2)}) collective-permute-start(bf16[24,8320]{1,0:T(8,128)(2,1)S(1)} %concatenate.9.own_ref), channel_id=1, source_target_pairs={{1,0},{2,1},{3,2},{4,3},{5,4},{6,5},{7,6},{8,7},{9,8},{10,9},{11,1... | collective-permute-start | bytes 1198088 | tf_op jit(solution)/shard_map/ppermute | solution.py:345
  6.5 5.0 %collective-permute-start = (bf16[24,8320]{1,0:T(8,128)(2,1)S(1)}, bf16[24,8320]{1,0:T(8,128)(2,1)S(1)}, u32[]{:S(2)}, u32[]{:S(2)}) collective-permute-start(bf16[24,8320]{1,0:T(8,128)(2,1)S(1)} %concatenate.9.own_ref), channel_id=1, source_target_pairs={{0,1},{1,2},{2,3},{3,4},{4,5},{5,6},{6,7},{7,8},{8,9},{9,10},{10,1... | collective-permute-start | bytes 1198088 | tf_op jit(solution)/shard_map/ppermute | solution.py:345
  11.5 0.6 slice_dynamic-update-slice_fusion
  12.2 0.6 constant_dynamic-update-slice_fusion.11
  12.8 0.6 constant_dynamic-update-slice_fusion.10
  13.4 0.6 constant_dynamic-update-slice_fusion.9
  14.0 0.6 constant_dynamic-update-slice_fusion.8
  14.6 0.6 constant_dynamic-update-slice_fusion.7
  15.2 0.6 constant_dynamic-update-slice_fusion.6
  15.7 0.6 constant_dynamic-update-slice_fusion.5
  18.7 0.6 constant_dynamic-update-slice_fusion
  19.3 5.5 %collective-permute-start.2 = (bf16[24,2944]{1,0:T(8,128)(2,1)}, bf16[24,2944]{1,0:T(8,128)(2,1)}, u32[]{:S(2)}, u32[]{:S(2)}) collective-permute-start(bf16[24,2944]{1,0:T(8,128)(2,1)} %constant_dynamic-update-slice_fusion), channel_id=1, source_target_pairs={{0,2},{1,3},{2,4},{3,5},{4,6},{5,7},{6,8},{7,9},{8,10},{9,11},{10,... | collective-permute-start | bytes 423944 | tf_op jit(solution)/shard_map/ppermute | solution.py:345
  24.9 1.6 %copy.35 = bf16[27,128,128]{1,2,0:T(8,128)(2,1)} copy(bf16[27,128,128]{2,1,0:T(8,128)(2,1)S(1)} %bitcast.24) | data formatting | bytes 1769472 | tf_op jit(solution)/shard_map/reshape | solution.py:392
  26.5 1.2 %rev.3 = bf16[27,128,128]{1,2,0:T(8,128)(2,1)S(1)} reverse(bf16[27,128,128]{1,2,0:T(8,128)(2,1)} %copy.35), dimensions={0} | reverse | bytes 1769472 | tf_op jit(solution)/shard_map/rev | solution.py:392
  27.8 12.1 %shard_map.111 = (bf16[24,4096]{1,0:T(8,128)(2,1)S(1)}, bf16[2,4,64,1536]{3,2,1,0:T(8,128)(2,1)S(1)}) custom-call(s32[1]{0:T(128)} %bitcast.core_ref, bf16[24,8320]{1,0:T(8,128)(2,1)S(1)} %concatenate.9.own_ref, bf16[24,8320]{1,0:T(8,128)(2,1)S(1)} %collective-permute-done.prev_ref, bf16[24,8320]{1,0:T(8,128)(2,1)S(1)} %collective-permute-done.1.next_ref, ...), custom_call_target="tpu_custom_call" | custom-call | tf_op jit(solution)/shard_map/pallas_call | solution.py:312
  39.9 4.7 %collective-permute-start.3 = (bf16[4,64,1536]{2,1,0:T(8,128)(2,1)S(1)}, bf16[4,64,1536]{2,1,0:T(8,128)(2,1)S(1)}, u32[]{:S(2)}, u32[]{:S(2)}) collective-permute-start(bf16[4,64,1536]{2,1,0:T(8,128)(2,1)S(1)} %slice_bitcast_fusion), channel_id=1, source_target_pairs={{0,64},{64,0},{128,192},{192,128},{256,320},{320,256},{384,448},{4... | collective-permute-start | bytes 2359304 | tf_op jit(solution)/shard_map/ppermute | solution.py:359
  44.7 1.9 %collective-permute-done.3 = bf16[4,64,1536]{2,1,0:T(8,128)(2,1)S(1)} collective-permute-done((bf16[4,64,1536]{2,1,0:T(8,128)(2,1)S(1)}, bf16[4,64,1536]{2,1,0:T(8,128)(2,1)S(1)}, u32[]{:S(2)}, u32[]{:S(2)}) %collective-permute-start.3) | collective-permute-done | bytes 786464 | tf_op jit(solution)/shard_map/ppermute | solution.py:359
  46.8 13.9 %all_to_all.15 = bf16[4,64,1536]{2,1,0:T(8,128)(2,1)S(1)} all-to-all(bf16[4,64,1536]{2,1,0:T(8,128)(2,1)S(1)} %fusion), channel_id=1, replica_groups={{0,128,256,384},{64,192,320,448},{1,129,257,385},{65,193,321,449},{2,13..., dimensions={0} | all-to-all | bytes 1572864 | tf_op jit(solution)/shard_map/all_to_all | solution.py:361
  60.8 21.2 %all_to_all.16 = bf16[4,16,1536]{2,1,0:T(8,128)(2,1)S(1)} all-to-all(bf16[4,16,1536]{2,1,0:T(8,128)(2,1)S(1)} %bitcast.26), channel_id=1, replica_groups={{0,16,32,48},{1,17,33,49},{2,18,34,50},{3,19,35,51},{4,20,36,52},{5,21,..., dimensions={0} | all-to-all | bytes 393216 | tf_op jit(solution)/shard_map/all_to_all | solution.py:365
  82.0 0.7 reshape.89
  82.7 6.0 %all-to-all-start.2 = ((bf16[16,12,128]{2,1,0:T(8,128)(2,1)}), bf16[16,12,128]{2,1,0:T(8,128)(2,1)S(1)}, u32[]{:S(2)}, u32[]{:S(2)}) async-start(bf16[16,12,128]{2,1,0:T(8,128)(2,1)} %reshape.89), calls=%async_computation.2 | async-start | bytes 131072 | tf_op jit(solution)/shard_map/all_to_all | solution.py:368
  88.7 0.8 reshape.87
  89.5 10.7 %all-to-all-done.2 = bf16[16,12,128]{2,1,0:T(8,128)(2,1)S(1)} async-done(((bf16[16,12,128]{2,1,0:T(8,128)(2,1)}), bf16[16,12,128]{2,1,0:T(8,128)(2,1)S(1)}, u32[]{:S(2)}, u32[]{:S(2)}) %all-to-all-start.2) | async-done | bytes 49184 | tf_op jit(solution)/shard_map/all_to_all | solution.py:368
  100.3 17.3 %all-gather.1 = f32[8,12,128]{2,1,0:T(8,128)S(1)} all-gather(f32[1,12,128]{2,1,0:T(8,128)S(1)} %bitcast.27), channel_id=2, replica_groups=mesh['dp'=8,'space'=64] {'dp'}, dimensions={0}, use_global_device_ids=true | all-gather | bytes 55296 | tf_op jit(solution)/shard_map/all_gather | solution.py:370
  117.6 0.6 slice_bitcast_fusion.3
  118.2 0.6 slice_bitcast_fusion.2
  118.8 0.6 slice_bitcast_fusion.1
  (28 shorter events, 3.1 us)
Async XLA Ops:
  0.6 24.2 %copy-start = (bf16[3456,128]{1,0:T(8,128)(2,1)S(1)}, bf16[3456,128]{1,0:T(8,128)(2,1)}, u32[]{:S(2)}) copy-start(bf16[3456,128]{1,0:T(8,128)(2,1)} %wc_ref.1) | copy-start | bytes 2654212
  5.2 22.5 %collective-permute-start.1 = (bf16[24,8320]{1,0:T(8,128)(2,1)S(1)}, bf16[24,8320]{1,0:T(8,128)(2,1)S(1)}, u32[]{:S(2)}, u32[]{:S(2)}) collective-permute-start(bf16[24,8320]{1,0:T(8,128)(2,1)S(1)} %concatenate.9.own_ref), channel_id=1, source_target_pairs={{1,0},{2,1},{3,2},{4,3},{5,4},{6,5},{7,6},{8,7},{9,8},{10,9},{11,1... | collective-permute-start | bytes 1198088 | tf_op jit(solution)/shard_map/ppermute | solution.py:345
  6.5 21.2 %collective-permute-start = (bf16[24,8320]{1,0:T(8,128)(2,1)S(1)}, bf16[24,8320]{1,0:T(8,128)(2,1)S(1)}, u32[]{:S(2)}, u32[]{:S(2)}) collective-permute-start(bf16[24,8320]{1,0:T(8,128)(2,1)S(1)} %concatenate.9.own_ref), channel_id=1, source_target_pairs={{0,1},{1,2},{2,3},{3,4},{4,5},{5,6},{6,7},{7,8},{8,9},{9,10},{10,1... | collective-permute-start | bytes 1198088 | tf_op jit(solution)/shard_map/ppermute | solution.py:345
  19.3 8.4 %collective-permute-start.2 = (bf16[24,2944]{1,0:T(8,128)(2,1)}, bf16[24,2944]{1,0:T(8,128)(2,1)}, u32[]{:S(2)}, u32[]{:S(2)}) collective-permute-start(bf16[24,2944]{1,0:T(8,128)(2,1)} %constant_dynamic-update-slice_fusion), channel_id=1, source_target_pairs={{0,2},{1,3},{2,4},{3,5},{4,6},{5,7},{6,8},{7,9},{8,10},{9,11},{10,... | collective-permute-start | bytes 423944 | tf_op jit(solution)/shard_map/ppermute | solution.py:345
  24.9 2.9 %copy-start.1 = (bf16[1728,128]{1,0:T(8,128)(2,1)S(1)}, bf16[1728,128]{1,0:T(8,128)(2,1)}, u32[]{:S(2)}) copy-start(bf16[1728,128]{1,0:T(8,128)(2,1)} %wd_ref.1) | copy-start | bytes 1327108
  24.9 2.9 %copy-start.4 = (bf16[128,512]{1,0:T(8,128)(2,1)S(1)}, bf16[128,512]{1,0:T(8,128)(2,1)}, u32[]{:S(2)}) copy-start(bf16[128,512]{1,0:T(8,128)(2,1)} %wu_ref.1) | copy-start | bytes 393220
  39.9 6.9 %copy-start.2 = (bf16[24,4096]{1,0:T(8,128)(2,1)}, bf16[24,4096]{1,0:T(8,128)(2,1)S(1)}, u32[]{:S(2)}) copy-start(bf16[24,4096]{1,0:T(8,128)(2,1)S(1)} %get-tuple-element.6) | copy-start | bytes 589828
  39.9 6.6 %collective-permute-start.3 = (bf16[4,64,1536]{2,1,0:T(8,128)(2,1)S(1)}, bf16[4,64,1536]{2,1,0:T(8,128)(2,1)S(1)}, u32[]{:S(2)}, u32[]{:S(2)}) collective-permute-start(bf16[4,64,1536]{2,1,0:T(8,128)(2,1)S(1)} %slice_bitcast_fusion), channel_id=1, source_target_pairs={{0,64},{64,0},{128,192},{192,128},{256,320},{320,256},{384,448},{4... | collective-permute-start | bytes 2359304 | tf_op jit(solution)/shard_map/ppermute | solution.py:359
  60.7 28.0 %copy-start.3 = (bf16[24,4096]{1,0:T(8,128)(2,1)S(1)}, bf16[24,4096]{1,0:T(8,128)(2,1)}, u32[]{:S(2)}) copy-start(bf16[24,4096]{1,0:T(8,128)(2,1)} %copy-done.2) | copy-start | bytes 589828
  82.7 17.6 %all-to-all-start.2 = ((bf16[16,12,128]{2,1,0:T(8,128)(2,1)}), bf16[16,12,128]{2,1,0:T(8,128)(2,1)S(1)}, u32[]{:S(2)}, u32[]{:S(2)}) async-start(bf16[16,12,128]{2,1,0:T(8,128)(2,1)} %reshape.89), calls=%async_computation.2 | async-start | bytes 131072 | tf_op jit(solution)/shard_map/all_to_all | solution.py:368

commit v2 on v1

--- a/solution.py
+++ b/solution.py
@@ -34,6 +34,7 @@
 
 
 UPPER = sum(width for _, width in upper_pieces())
+SENT = 1792 + 5 * 128
 
 
 def dot(a, b, dims=((1,), (0,))):
@@ -70,12 +71,15 @@
 HALO = len(halo_blocks(0, 0)) * CR
 
 
+def swap_halves(tile):
+    return jnp.concatenate([tile[:, 64:128], tile[:, 0:64]], axis=1)
+
+
 def octant_of(x, y, z):
     return 4 * (x // 2) + 2 * (y // 2) + z // 2, 4 * (x % 2) + 2 * (y % 2) + z % 2
 
 
 def kernel(
-    core_ref,
     own_ref,
     prev_ref,
     next_ref,
@@ -101,7 +105,6 @@
     gd_ref,
     gc_ref,
     gu_ref,
-    t_ref,
 ):
     zeros8 = functools.partial(jnp.zeros, dtype=F32)
 
@@ -125,8 +128,14 @@
             wide_ref[ab, at : at + 64, 128:256] = tap[e]
 
     at = 0
-    for start, width in upper_pieces():
-        parts = [far_ref[:, at : at + width].astype(F32)]
+    for n, (start, width) in enumerate(upper_pieces()):
+        if width > 128:
+            far = far_ref[:, at : at + width].astype(F32)
+        else:
+            tile = 1792 + (n - 4) // 2 * 128
+            far = far_ref[:, tile : tile + 128].astype(F32)
+            far = far if (n - 4) % 2 else swap_halves(far)
+        parts = [far]
         parts += [r[:, start : start + width].astype(F32) for r in (prev_ref, own_ref, next_ref)]
         src_ref[:, at : at + width] = jnp.concatenate(parts, axis=0).astype(BF)
         at += width
@@ -291,23 +300,20 @@
         gd_ref[(3 * ab) * 64 : (3 * ab + 1) * 64, :] = jnp.transpose(first)[64:128]
         gd_ref[(3 * ab + 1) * 64 : (3 * ab + 3) * 64, :] = jnp.transpose(later)
 
-    for t in range(27):
-        t_ref[t] = gd_ref[pl.ds(t, 64, stride=27), :]
-    for t in range(54):
-        t_ref[27 + t] = gc_ref[pl.ds(t, 64, stride=54), :]
-    for t in range(8):
-        t_ref[81 + t] = gu_ref[t % 4, pl.ds(t // 4, 64, stride=2), :]
-    t_ref[89:TILES] = jnp.zeros((TILES - 89, 64, 128), F32)
-    core = core_ref[0]
-    for side in range(2):
-        half = core if side == 0 else 1 - core
-        for y in range(4):
-            for n in range(12):
-                tile = t_ref[24 * y + 12 * half + n]
-                sum_ref[side, y, :, n * 128 : (n + 1) * 128] = tile.astype(BF)
-
-
-def local_pass(core, own, prev, nxt, far, wd, wc, wt, wu):
+    for t in range(TILES):
+        if t < 27:
+            tile = gd_ref[pl.ds(t, 64, stride=27), :]
+        elif t < 81:
+            tile = gc_ref[pl.ds(t - 27, 64, stride=54), :]
+        elif t < 89:
+            tile = gu_ref[(t - 81) % 4, pl.ds((t - 81) // 4, 64, stride=2), :]
+        else:
+            tile = jnp.zeros((64, 128), F32)
+        n = t % 12
+        sum_ref[t // 12 % 2, t // 24, :, n * 128 : (n + 1) * 128] = tile.astype(BF)
+
+
+def local_pass(own, prev, nxt, far, wd, wc, wt, wu):
     vmem = pl.BlockSpec(memory_space=pltpu.VMEM)
     return pl.pallas_call(
         kernel,
@@ -315,7 +321,7 @@
             jax.ShapeDtypeStruct((FB, XL), BF),
             jax.ShapeDtypeStruct((2, 4, 64, 1536), BF),
         ),
-        in_specs=[pl.BlockSpec(memory_space=pltpu.SMEM)] + [vmem] * 8,
+        in_specs=[vmem] * 8,
         out_specs=(vmem, vmem),
         scratch_shapes=[
             pltpu.VMEM((9, 384, 256), BF),
@@ -333,42 +339,77 @@
             pltpu.VMEM((1728, 128), F32),
             pltpu.VMEM((3456, 128), F32),
             pltpu.VMEM((4, 128, 128), F32),
-            pltpu.VMEM((TILES, 64, 128), F32),
         ],
         compiler_params=pltpu.CompilerParams(vmem_limit_bytes=48 * 2**20),
-    )(core, own, prev, nxt, far, wd, wc, wt, wu)
+    )(own, prev, nxt, far, wd, wc, wt, wu)
+
+
+def pack(place_ref, x_ref, cot_ref, fine_ref, parent_ref, coarse_ref, own_ref, far_ref):
+    place = place_ref[0]
+    own_ref[:, 0:XL] = x_ref[...]
+    own_ref[:, XL:IDX] = cot_ref[...]
+    fine = fine_ref[...]
+    fine = jnp.where(fine < 0, 0, fine - (FB * (place - 1) - 1)).astype(F32)
+    coarse = coarse_ref[...]
+    coarse = jnp.where(coarse < 0, 0, coarse - (CB * (place - 1) - 1)).astype(F32)
+    coarse = jnp.concatenate([coarse, jnp.zeros((FB - CB, 26), F32)], axis=0)
+    parent = (parent_ref[...] - (8 * (CB * place - 1) - 1)).astype(F32)
+    diagonal = lax.broadcasted_iota(jnp.int32, (FB, FB), 0) == lax.broadcasted_iota(
+        jnp.int32, (FB, FB), 1
+    )
+    parent = jnp.sum(jnp.where(diagonal, parent, 0.0), axis=1, keepdims=True)
+    filler = jnp.zeros((FB, 128 - 34), F32)
+    own_ref[:, IDX : IDX + 128] = jnp.concatenate([fine, parent, coarse, filler], axis=1).astype(BF)
+    at = 0
+    last = []
+    for start, width in upper_pieces():
+        if width > 128:
+            far_ref[:, at : at + width] = x_ref[:, start : start + width]
+        else:
+            last.append(x_ref[:, start : start + width].astype(F32))
+        at += width
+    upper_half = lax.broadcasted_iota(jnp.int32, (FB, 128), 1) >= 64
+    for n in range(5):
+        first = swap_halves(last[2 * n])
+        second = last[2 * n + 1] if 2 * n + 1 < 9 else first
+        tile = jnp.where(upper_half, second, first)
+        far_ref[:, 1792 + n * 128 : 1920 + n * 128] = tile.astype(BF)
+
+
+def packed(place, features, cotangent, fine_nbr, parents, coarse_nbr):
+    vmem = pl.BlockSpec(memory_space=pltpu.VMEM)
+    return pl.pallas_call(
+        pack,
+        out_shape=(
+            jax.ShapeDtypeStruct((FB, IDX + 128), BF),
+            jax.ShapeDtypeStruct((FB, SENT), BF),
+        ),
+        in_specs=[pl.BlockSpec(memory_space=pltpu.SMEM)] + [vmem] * 5,
+        out_specs=(vmem, vmem),
+    )(place, features, cotangent, fine_nbr, parents, coarse_nbr)
+
+
+SPACE = ("x", "z")
 
 
 def shift(block, distance):
-    size = lax.axis_size("space")
+    size = lax.axis_size(SPACE)
     route = [(i, i + distance) for i in range(size) if 0 <= i + distance < size]
-    return lax.ppermute(block, "space", route)
-
-
-def encode(fine_nbr, parents, coarse_nbr):
-    place = lax.axis_index("space")
-    fine = jnp.where(fine_nbr < 0, 0, fine_nbr - FB * (place - 1) + 1)
-    parent = parents - 8 * (CB * place - 1) + 1
-    coarse = jnp.where(coarse_nbr < 0, 0, coarse_nbr - CB * (place - 1) + 1)
-    coarse = jnp.pad(coarse, ((0, FB - CB), (0, 0)))
-    filler = jnp.zeros((FB, 128 - 34), jnp.int32)
-    return jnp.concatenate([fine, parent[:, None], coarse, filler], axis=1).astype(BF)
-
-
-def spread_sum(sums, groups_y, groups_x, groups_z, swap):
-    arrived = lax.ppermute(sums[1], "dp", swap)
-    held = (sums[0].astype(F32) + arrived.astype(F32)).astype(BF)
-    held = lax.all_to_all(held, "dp", 0, 0, axis_index_groups=groups_y)
+    return lax.ppermute(block, SPACE, route)
+
+
+def spread_sum(sums):
+    held = lax.all_to_all(sums, "core", 0, 0)
     held = jnp.sum(held.astype(F32), axis=0).astype(BF)
-    x_count = len(groups_x[0])
-    held = held.reshape(x_count, 64 // x_count, 1536)
-    held = lax.all_to_all(held, "space", 0, 0, axis_index_groups=groups_x)
+    held = held.reshape(16, 16, 1536)
+    held = lax.all_to_all(held, ("y", "x"), 0, 0)
     held = jnp.sum(held.astype(F32), axis=0).astype(BF)
-    held = held.reshape(held.shape[0], 12, 128)
-    held = lax.all_to_all(held, "space", 0, 0, axis_index_groups=groups_z)
+    held = held.reshape(16, 12, 128)
+    held = lax.all_to_all(held, "z", 0, 0)
     held = jnp.sum(held.astype(F32), axis=0)
-    whole = lax.all_gather(held, "dp").reshape(TILES, 128)
-    return whole
+    held = jnp.broadcast_to(held[None], (8, 12, 128))
+    held = lax.all_to_all(held, ("y", "core"), 0, 0)
+    return held.reshape(TILES, 128)
 
 
 def gradients(
@@ -382,31 +423,25 @@
     parent_slots,
     coarse_neighbours,
 ):
-    features = fine_features.reshape(FB, XL)
-    index = encode(fine_neighbours[0], parent_slots[0], coarse_neighbours[0])
-    own = jnp.concatenate([features, cotangent.reshape(FB, XL), index], axis=1)
-    upper = jnp.concatenate([features[:, s : s + w] for s, w in upper_pieces()], axis=1)
+    place = lax.axis_index(SPACE).astype(jnp.int32).reshape(1)
+    own, upper = packed(
+        place,
+        fine_features.reshape(FB, XL),
+        cotangent.reshape(FB, XL),
+        fine_neighbours[0],
+        parent_slots,
+        coarse_neighbours[0],
+    )
     prev = shift(own, 1)
+    far = shift(upper, 2)
     nxt = shift(own, -1)
-    far = shift(upper, 2)
     turned = coarse_weight.reshape(27, 128, 128)[::-1].transpose(0, 2, 1).reshape(27 * 128, 128)
-    core = (lax.axis_index("dp") % 2).astype(jnp.int32).reshape(1)
-    decoded, sums = local_pass(
-        core, own, prev, nxt, far, down_weight, coarse_weight, turned, up_weight
-    )
-    return decoded, sums
+    return local_pass(own, prev, nxt, far, down_weight, coarse_weight, turned, up_weight)
 
 
 def body(fine_features, *rest):
     decoded, sums = gradients(fine_features, *rest)
-    dp, space = lax.axis_size("dp"), lax.axis_size("space")
-    depth = 4
-    length = space // depth
-    groups_y = [[2 * y + c for y in range(dp // 2)] for c in range(2)]
-    groups_x = [[x * length + z for x in range(depth)] for z in range(length)]
-    groups_z = [[x * length + z for z in range(length)] for x in range(depth)]
-    swap = [(i, i ^ 1) for i in range(dp)]
-    whole = spread_sum(sums, groups_y, groups_x, groups_z, swap)
+    whole = spread_sum(sums)
     return (
         decoded.reshape(fine_features.shape),
         whole[0:27].reshape(-1),
@@ -416,16 +451,18 @@
 
 
 def solution(mesh):
+    mesh = jax.sharding.Mesh(mesh.devices.reshape(4, 2, 4, 16), ("y", "core", "x", "z"))
+    dp = ("y", "core")
     in_specs = (
-        P("dp", "space", None, None, None),
-        P("dp", "space", None, None, None),
+        P(dp, SPACE, None, None, None),
+        P(dp, SPACE, None, None, None),
         P(),
         P(),
         P(),
-        P("dp", "space", None),
-        P("dp", "space", None),
-        P("dp", "space"),
-        P("dp", "space", None),
+        P(dp, SPACE, None),
+        P(dp, SPACE, None),
+        P(dp, SPACE),
+        P(dp, SPACE, None),
     )
-    out_specs = (P("dp", "space", None, None, None), P("space"), P("space"), P("space"))
+    out_specs = (P(dp, SPACE, None, None, None), P(SPACE), P(SPACE), P(SPACE))
     return jax.shard_map(body, mesh=mesh, in_specs=in_specs, out_specs=out_specs, check_vma=False)

time: 120 us -> 110 us (0.917)
  waiting for transfers between devices: 12.6 us -> 4.07 us
  blocking collectives: 52.4 us -> 59.5 us
  starting transfers between devices: 22.6 us -> 18.1 us
  local copies, waits for them, and re-layouts: 17.1 us -> 13 us
  Pallas kernels: 12.1 us -> 13.6 us
  other arithmetic: 1.81 us -> 0.48 us
    all_to_all x2 -> x3, blocking collectives: 35.1 us -> 59.5 us  [the longest x1 32.4 us: spread_sum(): held = lax.all_to_all(held, ('y', 'x'), 0, 0)]
    all_gather x1 -> x0, blocking collectives: 17.3 us -> none  [spread_sum(): whole = lax.all_gather(held, 'dp').reshape(TILES, 128)]
    all_to_all x1, waiting for transfers between devices: 10.7 us -> 4.06 us  [spread_sum(): held = lax.all_to_all(held, ('y', 'core'), 0, 0)]
    ppermute x4 -> x3, starting transfers between devices: 16.6 us -> 11.8 us  [shift(): return lax.ppermute(block, SPACE, route)]
    unnamed x24 -> x14, local copies, waits for them, and re-layouts: 7.98 us -> 3.41 us
    pallas_call x0 -> x1, Pallas kernels: none -> 1.93 us  [packed(): pl.pallas_call(pack, out_shape=(jax.ShapeDtypeStruct((FB, IDX + 128), BF)...]
    ppermute x4 -> x3, waiting for transfers between devices: 1.9 us -> 0.01 us  [shift(): return lax.ppermute(block, SPACE, route)]
    reshape x3 -> x4, local copies, waits for them, and re-layouts: 2.78 us -> 3.52 us  [the longest x1 1.73 us: gradients(): fine_features.reshape(FB, XL)]
  transfers between devices with their start and end apart: 5 -> 4, of which waited for: 2 -> 1; matrix products, arithmetic and copies ran while one was open for 10% -> 3% of each run, Pallas kernels for 0% -> 0%
where the time goes in v2:
time: 110 us
  blocking collectives  59.5 us (54%)
  starting transfers between devices  18.1 us (16%)
  Pallas kernels  13.6 us (12%)
  local copies, waits for them, and re-layouts  13 us (12%)
  waiting for transfers between devices  4.07 us (4%)
    all_to_all x1, blocking collectives, spread_sum(): held = lax.all_to_all(held, ('y', 'x'), 0, 0)  32.4 us
    all_to_all x1, blocking collectives, spread_sum(): held = lax.all_to_all(held, 'z', 0, 0)  17.6 us
    ppermute x3, starting transfers between devices, shift(): return lax.ppermute(block, SPACE, route)  11.8 us
    pallas_call x1, Pallas kernels, local_pass(): pl.pallas_call(kernel, out_shape=(jax.ShapeDtypeStruct((FB, XL), BF), jax...  11.7 us
    all_to_all x1, blocking collectives, spread_sum(): held = lax.all_to_all(sums, 'core', 0, 0)  9.55 us
    all_to_all x1, starting transfers between devices, spread_sum(): held = lax.all_to_all(held, ('y', 'core'), 0, 0)  6.32 us
    all_to_all x1, waiting for transfers between devices, spread_sum(): held = lax.all_to_all(held, ('y', 'core'), 0, 0)  4.06 us
    unnamed x14, local copies, waits for them, and re-layouts  3.41 us
  transfers between devices with their start and end apart: 4, of which 1 were waited for; matrix products, arithmetic and copies ran while one was open for 3% of the time, Pallas kernels for 0%

profile of v2, /device:TPU:1, one launch (start us, length us, event | category | flops | bytes accessed | tf_op | source)
XLA Modules:
  0.0 109.6 jit_solution(11819208523456115539)
XLA Ops:
  0.6 0.0 copy-start
  0.6 1.4 %copy.20 = s32[1,6,26]{2,1,0:T(8,128)} copy(s32[1,6,26]{2,0,1:T(1,128)} %param.16) | data formatting | bytes 1248
  2.0 1.4 %copy.16 = s32[1,24,7]{2,1,0:T(8,128)} copy(s32[1,24,7]{1,0,2:T(1,128)} %param.14) | data formatting | bytes 1344 | tf_op args[5]
  3.4 1.7 %reshape.46.x_ref = bf16[24,4096]{1,0:T(8,128)(2,1)} reshape(bf16[1,24,4,4,256]{4,3,2,1,0:T(4,128)(2,1)} %param.9) | data formatting | bytes 393216 | tf_op jit(solution)/shard_map/reshape | solution.py:429
  5.1 1.7 %reshape.47.cot_ref = bf16[24,4096]{1,0:T(8,128)(2,1)} reshape(bf16[1,24,4,4,256]{4,3,2,1,0:T(4,128)(2,1)} %param.10) | data formatting | bytes 393216 | tf_op jit(solution)/shard_map/reshape | solution.py:430
  6.8 1.9 %shard_map.111 = (bf16[24,8320]{1,0:T(8,128)(2,1)}, bf16[24,2432]{1,0:T(8,128)(2,1)}) custom-call(s32[1]{0:T(128)} %bitcast.place_ref, bf16[24,4096]{1,0:T(8,128)(2,1)} %reshape.46.x_ref, bf16[24,4096]{1,0:T(8,128)(2,1)} %reshape.47.cot_ref, s32[24,7]{1,0:T(8,128)} %bitcast.19, s32[1,24]{1,0:T(1,128)} %parent_ref.1, s32[6,26]{1,0:T(8,128)} %bitcast.20), custom_call_target="tpu_custom_call" | custom-call | tf_op jit(solution)/shard_map/pallas_call | solution.py:381
  8.8 1.3 %collective-permute-start.1 = (bf16[24,8320]{1,0:T(8,128)(2,1)}, bf16[24,8320]{1,0:T(8,128)(2,1)S(1)}, u32[]{:S(2)}, u32[]{:S(2)}) collective-permute-start(bf16[24,8320]{1,0:T(8,128)(2,1)} %get-tuple-element.8.own_ref), channel_id=1, source_target_pairs={{1,0},{2,1},{3,2},{4,3},{5,4},{6,5},{7,6},{8,7},{9,8},{10,9},{11,1... | collective-permute-start | bytes 1198088 | tf_op jit(solution)/shard_map/ppermute | solution.py:398
  10.0 5.0 %collective-permute-start = (bf16[24,8320]{1,0:T(8,128)(2,1)}, bf16[24,8320]{1,0:T(8,128)(2,1)S(1)}, u32[]{:S(2)}, u32[]{:S(2)}) collective-permute-start(bf16[24,8320]{1,0:T(8,128)(2,1)} %get-tuple-element.8.own_ref), channel_id=1, source_target_pairs={{0,1},{1,2},{2,3},{3,4},{4,5},{5,6},{6,7},{7,8},{8,9},{9,10},{10,1... | collective-permute-start | bytes 1198088 | tf_op jit(solution)/shard_map/ppermute | solution.py:398
  15.1 5.5 %collective-permute-start.2 = (bf16[24,2432]{1,0:T(8,128)(2,1)}, bf16[24,2432]{1,0:T(8,128)(2,1)}, u32[]{:S(2)}, u32[]{:S(2)}) collective-permute-start(bf16[24,2432]{1,0:T(8,128)(2,1)} %get-tuple-element.9), channel_id=1, source_target_pairs={{0,2},{1,3},{2,4},{3,5},{4,6},{5,7},{6,8},{7,9},{8,10},{9,11},{10,... | collective-permute-start | bytes 350216 | tf_op jit(solution)/shard_map/ppermute | solution.py:398
  20.6 0.0 copy-done
  20.6 1.6 %copy.17 = bf16[27,128,128]{1,2,0:T(8,128)(2,1)} copy(bf16[27,128,128]{2,1,0:T(8,128)(2,1)S(1)} %bitcast.16) | data formatting | bytes 1769472 | tf_op jit(solution)/shard_map/reshape | solution.py:438
  22.2 1.2 %rev.3 = bf16[27,128,128]{1,2,0:T(8,128)(2,1)S(1)} reverse(bf16[27,128,128]{1,2,0:T(8,128)(2,1)} %copy.17), dimensions={0} | reverse | bytes 1769472 | tf_op jit(solution)/shard_map/rev | solution.py:438
  23.5 0.0 collective-permute-done.2.far_ref
  23.5 0.0 collective-permute-done.1.next_ref
  23.5 0.0 collective-permute-done.prev_ref
  23.5 11.7 %shard_map.112 = (bf16[24,4096]{1,0:T(8,128)(2,1)S(1)}, bf16[2,4,64,1536]{3,2,1,0:T(8,128)(2,1)S(1)}) custom-call(bf16[24,8320]{1,0:T(8,128)(2,1)S(1)} %copy-done.2, bf16[24,8320]{1,0:T(8,128)(2,1)S(1)} %collective-permute-done.prev_ref, bf16[24,8320]{1,0:T(8,128)(2,1)S(1)} %collective-permute-done.1.next_ref, ...), custom_call_target="tpu_custom_call" | custom-call | tf_op jit(solution)/shard_map/pallas_call | solution.py:318
  35.2 0.0 copy-start.3
  35.2 0.7 copy-done.3
  35.9 9.5 %all_to_all.20 = bf16[2,4,64,1536]{3,2,1,0:T(8,128)(2,1)S(1)} all-to-all(bf16[2,4,64,1536]{3,2,1,0:T(8,128)(2,1)S(1)} %get-tuple-element.11), channel_id=1, replica_groups=mesh['y'=4,'core'=2,'x'=4,'z'=16] {'core'}, dimensions={0} | all-to-all | bytes 3145728 | tf_op jit(solution)/shard_map/all_to_all | solution.py:402
  45.5 0.3 reduce_sum.33
  45.8 0.0 copy-start.4
  45.8 32.4 %all_to_all.21 = bf16[16,16,1536]{2,1,0:T(8,128)(2,1)S(1)} all-to-all(bf16[16,16,1536]{2,1,0:T(8,128)(2,1)S(1)} %bitcast.18), channel_id=1, replica_groups=mesh['y'=4,'core'=2,'x'=4,'z'=16] {'y','x'}, dimensions={0} | all-to-all | bytes 1572864 | tf_op jit(solution)/shard_map/all_to_all | solution.py:405
  78.2 0.1 reduce_sum.34
  78.3 0.1 reshape.52
  78.4 17.6 %all_to_all.22 = bf16[16,12,128]{2,1,0:T(8,128)(2,1)S(1)} all-to-all(bf16[16,12,128]{2,1,0:T(8,128)(2,1)S(1)} %reshape.52), channel_id=1, replica_groups=mesh['y'=4,'core'=2,'x'=4,'z'=16] {'z'}, dimensions={0} | all-to-all | bytes 98304 | tf_op jit(solution)/shard_map/all_to_all | solution.py:408
  96.0 0.6 broadcast_in_dim.2
  96.6 6.3 %all-to-all-start.3 = ((f32[8,12,128]{2,1,0:T(8,128)}), f32[8,12,128]{2,1,0:T(8,128)S(1)}, u32[]{:S(2)}, u32[]{:S(2)}) async-start(f32[8,12,128]{2,1,0:T(8,128)} %broadcast_in_dim.2), calls=%async_computation.3 | async-start | bytes 131072 | tf_op jit(solution)/shard_map/all_to_all | solution.py:411
  102.9 0.8 reshape.50
  103.7 4.1 %all-to-all-done.3 = f32[8,12,128]{2,1,0:T(8,128)S(1)} async-done(((f32[8,12,128]{2,1,0:T(8,128)}), f32[8,12,128]{2,1,0:T(8,128)S(1)}, u32[]{:S(2)}, u32[]{:S(2)}) %all-to-all-start.3) | async-done | bytes 49184 | tf_op jit(solution)/shard_map/all_to_all | solution.py:411
  107.8 0.6 slice_bitcast_fusion.2
  108.4 0.6 slice_bitcast_fusion.1
  109.0 0.6 slice_bitcast_fusion
  (9 shorter events, 0.0 us)
Async XLA Ops:
  0.6 20.0 %copy-start = (bf16[3456,128]{1,0:T(8,128)(2,1)S(1)}, bf16[3456,128]{1,0:T(8,128)(2,1)}, u32[]{:S(2)}) copy-start(bf16[3456,128]{1,0:T(8,128)(2,1)} %wc_ref.1) | copy-start | bytes 2654212
  8.8 14.7 %collective-permute-start.1 = (bf16[24,8320]{1,0:T(8,128)(2,1)}, bf16[24,8320]{1,0:T(8,128)(2,1)S(1)}, u32[]{:S(2)}, u32[]{:S(2)}) collective-permute-start(bf16[24,8320]{1,0:T(8,128)(2,1)} %get-tuple-element.8.own_ref), channel_id=1, source_target_pairs={{1,0},{2,1},{3,2},{4,3},{5,4},{6,5},{7,6},{8,7},{9,8},{10,9},{11,1... | collective-permute-start | bytes 1198088 | tf_op jit(solution)/shard_map/ppermute | solution.py:398
  10.0 13.4 %collective-permute-start = (bf16[24,8320]{1,0:T(8,128)(2,1)}, bf16[24,8320]{1,0:T(8,128)(2,1)S(1)}, u32[]{:S(2)}, u32[]{:S(2)}) collective-permute-start(bf16[24,8320]{1,0:T(8,128)(2,1)} %get-tuple-element.8.own_ref), channel_id=1, source_target_pairs={{0,1},{1,2},{2,3},{3,4},{4,5},{5,6},{6,7},{7,8},{8,9},{9,10},{10,1... | collective-permute-start | bytes 1198088 | tf_op jit(solution)/shard_map/ppermute | solution.py:398
  15.1 8.4 %collective-permute-start.2 = (bf16[24,2432]{1,0:T(8,128)(2,1)}, bf16[24,2432]{1,0:T(8,128)(2,1)}, u32[]{:S(2)}, u32[]{:S(2)}) collective-permute-start(bf16[24,2432]{1,0:T(8,128)(2,1)} %get-tuple-element.9), channel_id=1, source_target_pairs={{0,2},{1,3},{2,4},{3,5},{4,6},{5,7},{6,8},{7,9},{8,10},{9,11},{10,... | collective-permute-start | bytes 350216 | tf_op jit(solution)/shard_map/ppermute | solution.py:398
  20.6 2.9 %copy-start.1 = (bf16[1728,128]{1,0:T(8,128)(2,1)S(1)}, bf16[1728,128]{1,0:T(8,128)(2,1)}, u32[]{:S(2)}) copy-start(bf16[1728,128]{1,0:T(8,128)(2,1)} %wd_ref.1) | copy-start | bytes 1327108
  20.6 2.9 %copy-start.2 = (bf16[24,8320]{1,0:T(8,128)(2,1)S(1)}, bf16[24,8320]{1,0:T(8,128)(2,1)}, u32[]{:S(2)}) copy-start(bf16[24,8320]{1,0:T(8,128)(2,1)} %get-tuple-element.8.own_ref) | copy-start | bytes 1198084
  20.6 2.9 %copy-start.5 = (bf16[128,512]{1,0:T(8,128)(2,1)S(1)}, bf16[128,512]{1,0:T(8,128)(2,1)}, u32[]{:S(2)}) copy-start(bf16[128,512]{1,0:T(8,128)(2,1)} %wu_ref.1) | copy-start | bytes 393220
  35.2 0.7 copy-start.3
  45.8 57.1 %copy-start.4 = (bf16[24,4096]{1,0:T(8,128)(2,1)S(1)}, bf16[24,4096]{1,0:T(8,128)(2,1)}, u32[]{:S(2)}) copy-start(bf16[24,4096]{1,0:T(8,128)(2,1)} %copy-done.3) | copy-start | bytes 589828
  96.6 11.2 %all-to-all-start.3 = ((f32[8,12,128]{2,1,0:T(8,128)}), f32[8,12,128]{2,1,0:T(8,128)S(1)}, u32[]{:S(2)}, u32[]{:S(2)}) async-start(f32[8,12,128]{2,1,0:T(8,128)} %broadcast_in_dim.2), calls=%async_computation.3 | async-start | bytes 131072 | tf_op jit(solution)/shard_map/all_to_all | solution.py:411

commit v3 on v2

--- a/solution.py
+++ b/solution.py
@@ -81,8 +81,8 @@
 
 def kernel(
     own_ref,
+    next_ref,
     prev_ref,
-    next_ref,
     far_ref,
     wd_ref,
     wc_ref,
@@ -341,32 +341,33 @@
             pltpu.VMEM((4, 128, 128), F32),
         ],
         compiler_params=pltpu.CompilerParams(vmem_limit_bytes=48 * 2**20),
-    )(own, prev, nxt, far, wd, wc, wt, wu)
+    )(own, nxt, prev, far, wd, wc, wt, wu)
 
 
 def pack(place_ref, x_ref, cot_ref, fine_ref, parent_ref, coarse_ref, own_ref, far_ref):
     place = place_ref[0]
-    own_ref[:, 0:XL] = x_ref[...]
-    own_ref[:, XL:IDX] = cot_ref[...]
-    fine = fine_ref[...]
+    own_ref[:, 0:XL] = x_ref[...].reshape(FB, XL)
+    own_ref[:, XL:IDX] = cot_ref[...].reshape(FB, XL)
+    fine = jnp.concatenate([fine_ref[m] for m in range(7)], axis=0)
     fine = jnp.where(fine < 0, 0, fine - (FB * (place - 1) - 1)).astype(F32)
-    coarse = coarse_ref[...]
+    coarse = jnp.concatenate([coarse_ref[c] for c in range(CB)], axis=0)
     coarse = jnp.where(coarse < 0, 0, coarse - (CB * (place - 1) - 1)).astype(F32)
     coarse = jnp.concatenate([coarse, jnp.zeros((FB - CB, 26), F32)], axis=0)
     parent = (parent_ref[...] - (8 * (CB * place - 1) - 1)).astype(F32)
-    diagonal = lax.broadcasted_iota(jnp.int32, (FB, FB), 0) == lax.broadcasted_iota(
+    lists = jnp.concatenate([fine, parent], axis=0).astype(BF)
+    unit = lax.broadcasted_iota(jnp.int32, (FB, FB), 0) == lax.broadcasted_iota(
         jnp.int32, (FB, FB), 1
     )
-    parent = jnp.sum(jnp.where(diagonal, parent, 0.0), axis=1, keepdims=True)
+    lists = dot(jnp.where(unit, 1.0, 0.0).astype(BF), lists, ((1,), (1,)))
     filler = jnp.zeros((FB, 128 - 34), F32)
-    own_ref[:, IDX : IDX + 128] = jnp.concatenate([fine, parent, coarse, filler], axis=1).astype(BF)
+    own_ref[:, IDX : IDX + 128] = jnp.concatenate([lists, coarse, filler], axis=1).astype(BF)
     at = 0
     last = []
     for start, width in upper_pieces():
         if width > 128:
-            far_ref[:, at : at + width] = x_ref[:, start : start + width]
+            far_ref[:, at : at + width] = own_ref[:, start : start + width]
         else:
-            last.append(x_ref[:, start : start + width].astype(F32))
+            last.append(own_ref[:, start : start + width].astype(F32))
         at += width
     upper_half = lax.broadcasted_iota(jnp.int32, (FB, 128), 1) >= 64
     for n in range(5):
@@ -386,6 +387,7 @@
         ),
         in_specs=[pl.BlockSpec(memory_space=pltpu.SMEM)] + [vmem] * 5,
         out_specs=(vmem, vmem),
+        compiler_params=pltpu.CompilerParams(vmem_limit_bytes=8 * 2**20),
     )(place, features, cotangent, fine_nbr, parents, coarse_nbr)
 
 
@@ -396,6 +398,19 @@
     size = lax.axis_size(SPACE)
     route = [(i, i + distance) for i in range(size) if 0 <= i + distance < size]
     return lax.ppermute(block, SPACE, route)
+
+
+def sum_copies(in_ref, out_ref):
+    total = jnp.sum(in_ref[...].astype(F32), axis=0)
+    for n in range(out_ref.shape[0]):
+        out_ref[n] = total
+
+
+def split(in_ref, down_ref, coarse_ref, up_ref):
+    whole = jnp.concatenate([in_ref[n] for n in range(8)], axis=0)
+    down_ref[...] = whole[0:27]
+    coarse_ref[...] = whole[27:81]
+    up_ref[...] = whole[81:89]
 
 
 def spread_sum(sums):
@@ -406,10 +421,18 @@
     held = jnp.sum(held.astype(F32), axis=0).astype(BF)
     held = held.reshape(16, 12, 128)
     held = lax.all_to_all(held, "z", 0, 0)
-    held = jnp.sum(held.astype(F32), axis=0)
-    held = jnp.broadcast_to(held[None], (8, 12, 128))
+    held = pl.pallas_call(
+        sum_copies,
+        out_shape=jax.ShapeDtypeStruct((8, 12, 128), F32),
+        compiler_params=pltpu.CompilerParams(vmem_limit_bytes=2 * 2**20),
+    )(held)
     held = lax.all_to_all(held, ("y", "core"), 0, 0)
-    return held.reshape(TILES, 128)
+    shares = pl.pallas_call(
+        split,
+        out_shape=tuple(jax.ShapeDtypeStruct((n, 128), F32) for n in (27, 54, 8)),
+        compiler_params=pltpu.CompilerParams(vmem_limit_bytes=2 * 2**20),
+    )(held)
+    return tuple(share.reshape(-1) for share in shares)
 
 
 def gradients(
@@ -426,11 +449,11 @@
     place = lax.axis_index(SPACE).astype(jnp.int32).reshape(1)
     own, upper = packed(
         place,
-        fine_features.reshape(FB, XL),
-        cotangent.reshape(FB, XL),
-        fine_neighbours[0],
+        fine_features[0],
+        cotangent[0],
+        fine_neighbours.transpose(2, 0, 1),
         parent_slots,
-        coarse_neighbours[0],
+        coarse_neighbours[0].reshape(CB, 1, 26),
     )
     prev = shift(own, 1)
     far = shift(upper, 2)
@@ -441,13 +464,7 @@
 
 def body(fine_features, *rest):
     decoded, sums = gradients(fine_features, *rest)
-    whole = spread_sum(sums)
-    return (
-        decoded.reshape(fine_features.shape),
-        whole[0:27].reshape(-1),
-        whole[27:81].reshape(-1),
-        whole[81:89].reshape(-1),
-    )
+    return (decoded.reshape(fine_features.shape), *spread_sum(sums))
 
 
 def solution(mesh):

time: 110 us -> 103 us (0.936)
  local copies, waits for them, and re-layouts: 13 us -> 8.96 us
  blocking collectives: 59.5 us -> 56.7 us
    reshape x7 -> x1, local copies, waits for them, and re-layouts: 6.09 us -> 0.81 us  [body(): return (decoded.reshape(fine_features.shape), *spread_sum(sums))]
    all_to_all x1, blocking collectives: 32.4 us -> 29.6 us  [spread_sum(): held = lax.all_to_all(held, ('y', 'x'), 0, 0)]
    all_to_all x1, blocking collectives: 9.55 us -> 7.27 us  [spread_sum(): held = lax.all_to_all(sums, 'core', 0, 0)]
    all_to_all x1, blocking collectives: 17.6 us -> 19.8 us  [spread_sum(): held = lax.all_to_all(held, 'z', 0, 0)]
    pallas_call x0 -> x2, Pallas kernels: none -> 1.27 us  [the longest x1 0.65 us: spread_sum(): pl.pallas_call(sum_copies, out_shape=jax.ShapeDtypeStruct((8, 12, 128), F...]
    unnamed x14 -> x20, local copies, waits for them, and re-layouts: 3.41 us -> 4.56 us
  transfers between devices with their start and end apart: 4 -> 4, of which waited for: 1 -> 1; matrix products, arithmetic and copies ran while one was open for 3% -> 4% of each run, Pallas kernels for 0% -> 0%
where the time goes in v3:
time: 103 us
  blocking collectives  56.7 us (55%)
  starting transfers between devices  18.1 us (18%)
  Pallas kernels  13.9 us (13%)
  local copies, waits for them, and re-layouts  8.96 us (9%)
  waiting for transfers between devices  4.07 us (4%)
    all_to_all x1, blocking collectives, spread_sum(): held = lax.all_to_all(held, ('y', 'x'), 0, 0)  29.6 us
    all_to_all x1, blocking collectives, spread_sum(): held = lax.all_to_all(held, 'z', 0, 0)  19.8 us
    ppermute x3, starting transfers between devices, shift(): return lax.ppermute(block, SPACE, route)  11.8 us
    pallas_call x1, Pallas kernels, local_pass(): pl.pallas_call(kernel, out_shape=(jax.ShapeDtypeStruct((FB, XL), BF), jax...  11.7 us
    all_to_all x1, blocking collectives, spread_sum(): held = lax.all_to_all(sums, 'core', 0, 0)  7.27 us
    all_to_all x1, starting transfers between devices, spread_sum(): held = lax.all_to_all(held, ('y', 'core'), 0, 0)  6.32 us
    unnamed x20, local copies, waits for them, and re-layouts  4.56 us
    all_to_all x1, waiting for transfers between devices, spread_sum(): held = lax.all_to_all(held, ('y', 'core'), 0, 0)  4.06 us
  transfers between devices with their start and end apart: 4, of which 1 were waited for; matrix products, arithmetic and copies ran while one was open for 4% of the time, Pallas kernels for 0%

profile of v3, /device:TPU:1, one launch (start us, length us, event | category | flops | bytes accessed | tf_op | source)
XLA Modules:
  0.0 102.9 jit_solution(15243383271042430712)
XLA Ops:
  0.6 0.0 copy-start.2
  0.6 0.9 copy-done.2
  1.6 0.9 copy-done.3
  2.5 0.7 copy-done.7
  3.2 0.7 copy-done.8
  3.9 0.7 copy-done.9
  4.5 0.9 shard_map.111
  5.4 4.4 %collective-permute-start.1 = (bf16[24,8320]{1,0:T(8,128)(2,1)S(1)}, bf16[24,8320]{1,0:T(8,128)(2,1)S(1)}, u32[]{:S(2)}, u32[]{:S(2)}) collective-permute-start(bf16[24,8320]{1,0:T(8,128)(2,1)S(1)} %get-tuple-element.11.own_ref), channel_id=1, source_target_pairs={{0,1},{1,2},{2,3},{3,4},{4,5},{5,6},{6,7},{7,8},{8,9},{9,10},{10,1... | collective-permute-start | bytes 1198088 | tf_op jit(solution)/shard_map/ppermute | solution.py:400
  9.8 1.3 %collective-permute-start = (bf16[24,8320]{1,0:T(8,128)(2,1)S(1)}, bf16[24,8320]{1,0:T(8,128)(2,1)S(1)}, u32[]{:S(2)}, u32[]{:S(2)}) collective-permute-start(bf16[24,8320]{1,0:T(8,128)(2,1)S(1)} %get-tuple-element.11.own_ref), channel_id=1, source_target_pairs={{1,0},{2,1},{3,2},{4,3},{5,4},{6,5},{7,6},{8,7},{9,8},{10,9},{11,1... | collective-permute-start | bytes 1198088 | tf_op jit(solution)/shard_map/ppermute | solution.py:400
  11.1 6.1 %collective-permute-start.2 = (bf16[24,2432]{1,0:T(8,128)(2,1)}, bf16[24,2432]{1,0:T(8,128)(2,1)}, u32[]{:S(2)}, u32[]{:S(2)}) collective-permute-start(bf16[24,2432]{1,0:T(8,128)(2,1)} %get-tuple-element.12), channel_id=1, source_target_pairs={{0,2},{1,3},{2,4},{3,5},{4,6},{5,7},{6,8},{7,9},{8,10},{9,11},{10,... | collective-permute-start | bytes 350216 | tf_op jit(solution)/shard_map/ppermute | solution.py:400
  17.2 2.3 %copy.14 = bf16[27,128,128]{1,2,0:T(8,128)(2,1)} copy(bf16[27,128,128]{2,1,0:T(8,128)(2,1)} %bitcast.13) | data formatting | bytes 1769472 | tf_op jit(solution)/shard_map/reshape | solution.py:461
  19.5 1.2 %rev.3 = bf16[27,128,128]{1,2,0:T(8,128)(2,1)S(1)} reverse(bf16[27,128,128]{1,2,0:T(8,128)(2,1)} %copy.14), dimensions={0} | reverse | bytes 1769472 | tf_op jit(solution)/shard_map/rev | solution.py:461
  20.8 0.0 collective-permute-done.2.far_ref
  20.8 0.0 collective-permute-done.1.prev_ref
  20.8 0.0 collective-permute-done.next_ref
  20.8 0.0 copy-done
  20.8 0.0 copy-done.1
  20.8 11.7 %shard_map.112 = (bf16[24,4096]{1,0:T(8,128)(2,1)S(1)}, bf16[2,4,64,1536]{3,2,1,0:T(8,128)(2,1)S(1)}) custom-call(bf16[24,8320]{1,0:T(8,128)(2,1)S(1)} %get-tuple-element.11.own_ref, bf16[24,8320]{1,0:T(8,128)(2,1)S(1)} %collective-permute-done.next_ref, bf16[24,8320]{1,0:T(8,128)(2,1)S(1)} %collective-permute-done.1.prev_ref, ...), custom_call_target="tpu_custom_call" | custom-call | tf_op jit(solution)/shard_map/pallas_call | solution.py:318
  32.6 0.0 copy-start.4
  32.6 0.7 copy-done.4
  33.2 7.3 %all_to_all.20 = bf16[2,4,64,1536]{3,2,1,0:T(8,128)(2,1)S(1)} all-to-all(bf16[2,4,64,1536]{3,2,1,0:T(8,128)(2,1)S(1)} %get-tuple-element.14), channel_id=1, replica_groups=mesh['y'=4,'core'=2,'x'=4,'z'=16] {'core'}, dimensions={0} | all-to-all | bytes 3145728 | tf_op jit(solution)/shard_map/all_to_all | solution.py:417
  40.5 0.3 reduce_sum.24
  40.9 0.0 copy-start.5
  40.9 29.6 %all_to_all.21 = bf16[16,16,1536]{2,1,0:T(8,128)(2,1)S(1)} all-to-all(bf16[16,16,1536]{2,1,0:T(8,128)(2,1)S(1)} %bitcast.19), channel_id=1, replica_groups=mesh['y'=4,'core'=2,'x'=4,'z'=16] {'y','x'}, dimensions={0} | all-to-all | bytes 1572864 | tf_op jit(solution)/shard_map/all_to_all | solution.py:420
  70.5 0.1 reduce_sum.25
  70.6 0.1 reshape.40
  70.7 19.8 %all_to_all.22.in_ref = bf16[16,12,128]{2,1,0:T(8,128)(2,1)S(1)} all-to-all(bf16[16,12,128]{2,1,0:T(8,128)(2,1)S(1)} %reshape.40), channel_id=1, replica_groups=mesh['y'=4,'core'=2,'x'=4,'z'=16] {'z'}, dimensions={0} | all-to-all | bytes 98304 | tf_op jit(solution)/shard_map/all_to_all | solution.py:423
  90.5 0.7 shard_map.113
  91.1 6.3 %all-to-all-start.3 = ((f32[8,12,128]{2,1,0:T(8,128)}), f32[8,12,128]{2,1,0:T(8,128)S(1)}, u32[]{:S(2)}, u32[]{:S(2)}) async-start(f32[8,12,128]{2,1,0:T(8,128)} %shard_map.113), calls=%async_computation.3 | async-start | bytes 131072 | tf_op jit(solution)/shard_map/all_to_all | solution.py:429
  97.4 0.8 reshape.38
  98.2 4.1 %all-to-all-done.3.in_ref = f32[8,12,128]{2,1,0:T(8,128)S(1)} async-done(((f32[8,12,128]{2,1,0:T(8,128)}), f32[8,12,128]{2,1,0:T(8,128)S(1)}, u32[]{:S(2)}, u32[]{:S(2)}) %all-to-all-start.3) | async-done | bytes 49184 | tf_op jit(solution)/shard_map/all_to_all | solution.py:429
  102.3 0.6 shard_map.114
  (9 shorter events, 0.0 us)
Async XLA Ops:
  0.6 0.9 copy-start.2
  1.6 0.9 copy-start.3
  2.5 0.7 copy-start.7
  3.2 0.7 copy-start.8
  3.9 0.7 copy-start.9
  5.4 15.4 %collective-permute-start.1 = (bf16[24,8320]{1,0:T(8,128)(2,1)S(1)}, bf16[24,8320]{1,0:T(8,128)(2,1)S(1)}, u32[]{:S(2)}, u32[]{:S(2)}) collective-permute-start(bf16[24,8320]{1,0:T(8,128)(2,1)S(1)} %get-tuple-element.11.own_ref), channel_id=1, source_target_pairs={{0,1},{1,2},{2,3},{3,4},{4,5},{5,6},{6,7},{7,8},{8,9},{9,10},{10,1... | collective-permute-start | bytes 1198088 | tf_op jit(solution)/shard_map/ppermute | solution.py:400
  9.8 11.0 %collective-permute-start = (bf16[24,8320]{1,0:T(8,128)(2,1)S(1)}, bf16[24,8320]{1,0:T(8,128)(2,1)S(1)}, u32[]{:S(2)}, u32[]{:S(2)}) collective-permute-start(bf16[24,8320]{1,0:T(8,128)(2,1)S(1)} %get-tuple-element.11.own_ref), channel_id=1, source_target_pairs={{1,0},{2,1},{3,2},{4,3},{5,4},{6,5},{7,6},{8,7},{9,8},{10,9},{11,1... | collective-permute-start | bytes 1198088 | tf_op jit(solution)/shard_map/ppermute | solution.py:400
  11.1 9.7 %collective-permute-start.2 = (bf16[24,2432]{1,0:T(8,128)(2,1)}, bf16[24,2432]{1,0:T(8,128)(2,1)}, u32[]{:S(2)}, u32[]{:S(2)}) collective-permute-start(bf16[24,2432]{1,0:T(8,128)(2,1)} %get-tuple-element.12), channel_id=1, source_target_pairs={{0,2},{1,3},{2,4},{3,5},{4,6},{5,7},{6,8},{7,9},{8,10},{9,11},{10,... | collective-permute-start | bytes 350216 | tf_op jit(solution)/shard_map/ppermute | solution.py:400
  17.2 3.6 %copy-start = (bf16[3456,128]{1,0:T(8,128)(2,1)S(1)}, bf16[3456,128]{1,0:T(8,128)(2,1)}, u32[]{:S(2)}) copy-start(bf16[3456,128]{1,0:T(8,128)(2,1)} %wc_ref.1) | copy-start | bytes 2654212
  17.2 3.6 %copy-start.1 = (bf16[1728,128]{1,0:T(8,128)(2,1)S(1)}, bf16[1728,128]{1,0:T(8,128)(2,1)}, u32[]{:S(2)}) copy-start(bf16[1728,128]{1,0:T(8,128)(2,1)} %wd_ref.1) | copy-start | bytes 1327108
  17.2 3.6 %copy-start.6 = (bf16[128,512]{1,0:T(8,128)(2,1)S(1)}, bf16[128,512]{1,0:T(8,128)(2,1)}, u32[]{:S(2)}) copy-start(bf16[128,512]{1,0:T(8,128)(2,1)} %wu_ref.1) | copy-start | bytes 393220
  32.6 0.7 copy-start.4
  40.9 56.6 %copy-start.5 = (bf16[24,4096]{1,0:T(8,128)(2,1)S(1)}, bf16[24,4096]{1,0:T(8,128)(2,1)}, u32[]{:S(2)}) copy-start(bf16[24,4096]{1,0:T(8,128)(2,1)} %copy-done.4) | copy-start | bytes 589828
  91.1 11.2 %all-to-all-start.3 = ((f32[8,12,128]{2,1,0:T(8,128)}), f32[8,12,128]{2,1,0:T(8,128)S(1)}, u32[]{:S(2)}, u32[]{:S(2)}) async-start(f32[8,12,128]{2,1,0:T(8,128)} %shard_map.113), calls=%async_computation.3 | async-start | bytes 131072 | tf_op jit(solution)/shard_map/all_to_all | solution.py:429

commit v4 on v3

--- a/solution.py
+++ b/solution.py
@@ -79,6 +79,43 @@
     return 4 * (x // 2) + 2 * (y // 2) + z // 2, 4 * (x % 2) + 2 * (y % 2) + z % 2
 
 
+def widen(wd_ref, wc_ref, down_ref, coarse_ref, turned_ref):
+    down_ref[...] = jnp.zeros(down_ref.shape, BF)
+    for ab in range(9):
+        tap = [wd_ref[(3 * ab + e) * 64 : (3 * ab + e + 1) * 64, :] for e in range(3)]
+        at = ab * 384
+        for row, e in ((0, 1), (64, 2), (320, 0)):
+            down_ref[at + row : at + row + 64, 0:128] = tap[e]
+        for row, e in ((64, 0), (128, 1), (192, 2)):
+            down_ref[at + row : at + row + 64, 128:256] = tap[e]
+    zero = jnp.zeros((128, 128), BF)
+    for ab in range(9):
+        for e in range(3):
+            tap = 3 * ab + e
+            plain = wc_ref[tap * 128 : (tap + 1) * 128, :]
+            other = (26 - tap) * 128
+            turned = jnp.transpose(wc_ref[other : other + 128, :].astype(F32)).astype(BF)
+            for ref, block in ((coarse_ref, plain), (turned_ref, turned)):
+                for r in range(2):
+                    row = ab * 512 + (e + r) * 128
+                    ref[row : row + 128, r * 128 : (r + 1) * 128] = block
+        for ref in (coarse_ref, turned_ref):
+            ref[ab * 512 + 384 : ab * 512 + 512, 0:128] = zero
+            ref[ab * 512 : ab * 512 + 128, 128:256] = zero
+
+
+def widened(down_weight, coarse_weight):
+    vmem = pl.BlockSpec(memory_space=pltpu.VMEM)
+    shapes = ((9 * 384, 256), (9 * 512, 256), (9 * 512, 256))
+    return pl.pallas_call(
+        widen,
+        out_shape=tuple(jax.ShapeDtypeStruct(shape, BF) for shape in shapes),
+        in_specs=[vmem] * 2,
+        out_specs=(vmem,) * 3,
+        compiler_params=pltpu.CompilerParams(vmem_limit_bytes=12 * 2**20),
+    )(down_weight, coarse_weight)
+
+
 def kernel(
     own_ref,
     next_ref,
@@ -90,9 +127,9 @@
     wu_ref,
     dec_ref,
     sum_ref,
-    wide_ref,
     src_ref,
     pad_ref,
+    mine_ref,
     hid_ref,
     nl_ref,
     cin_ref,
@@ -119,14 +156,6 @@
     block = jnp.where(row >= FB, 1.0, 0.0) + jnp.where(row >= 2 * FB, 1.0, 0.0)
     lane_f = lane.astype(F32)
 
-    wide_ref[...] = jnp.zeros(wide_ref.shape, BF)
-    for ab in range(9):
-        tap = [wd_ref[(3 * ab + e) * 64 : (3 * ab + e + 1) * 64, :] for e in range(3)]
-        for at, e in ((0, 1), (64, 2), (320, 0)):
-            wide_ref[ab, at : at + 64, 0:128] = tap[e]
-        for at, e in ((64, 0), (128, 1), (192, 2)):
-            wide_ref[ab, at : at + 64, 128:256] = tap[e]
-
     at = 0
     for n, (start, width) in enumerate(upper_pieces()):
         if width > 128:
@@ -152,7 +181,10 @@
         start, width = plane_lanes(i, j)
         if last:
             start, width = start + width - 128, 128
-        return dot(picks[code], src_ref[:, start : start + width]).astype(BF)
+        return dot(picks[code], src_ref[:, start : start + width])
+
+    def only_own(array):
+        return jnp.concatenate([array[FB : 2 * FB], zeros8((8, array.shape[1]))], axis=0)
 
     for ip in range(5):
         for jp in range(5):
@@ -161,16 +193,22 @@
             if code:
                 own = fetch(code, i, j, False)
             else:
-                own = rows((i * 4 + j) * 256, 256).astype(BF)
-            pad_ref[ip * 5 + jp, :, 0:256] = own
-            pad_ref[ip * 5 + jp, :, 256:384] = fetch(code + 1, i, j, True)
-
+                own = rows((i * 4 + j) * 256, 256)
+            behind = fetch(code + 1, i, j, True)
+            pad_ref[ip * 5 + jp, :, 0:256] = own.astype(BF)
+            pad_ref[ip * 5 + jp, :, 256:384] = behind.astype(BF)
+            mine_ref[ip * 5 + jp, :, 0:256] = only_own(own).astype(BF)
+            mine_ref[ip * 5 + jp, :, 256:384] = only_own(behind).astype(BF)
+
+    outs = []
+    for p in range(2):
+        for q in range(2):
+            taps = [pad_ref[(2 * p + a) * 5 + 2 * q + b] for a in range(3) for b in range(3)]
+            outs.append(dot(jnp.concatenate(taps, axis=1), wd_ref[...]))
+    pre = jnp.concatenate(outs, axis=0)
     slope_down = []
     for pq in range(4):
-        p, q = pq // 2, pq % 2
-        taps = [pad_ref[(2 * p + a) * 5 + 2 * q + b] for a in range(3) for b in range(3)]
-        pre = dot(jnp.concatenate(taps, axis=1), wide_ref[...].reshape(9 * 384, 256))
-        value, slope = gate(pre)
+        value, slope = gate(pre[pq * ROWS : (pq + 1) * ROWS])
         hid_ref[:, pq * 256 : (pq + 1) * 256] = value.astype(BF)
         slope_down.append(slope[FB : 2 * FB])
 
@@ -204,55 +242,67 @@
             for y in range(4):
                 for z in range(4):
                     o, v = octant_of(x, y, z)
-                    padded_ref[x + 1, y + 1, z + 1] = flat_ref[
+                    padded_ref[x + 1, y + 1, (z + 1) // 2, (z + 1) % 2] = flat_ref[
                         o * CR : (o + 1) * CR, v * 128 : (v + 1) * 128
                     ]
         for pq in range(4):
             got = dot(nl_ref[pq], flat_ref[:, pq * 256 : (pq + 1) * 256]).astype(BF)
             for n, (_, _, targets) in enumerate(halo_blocks(pq // 2, pq % 2)):
                 for r, (cx, cy, cz) in targets:
-                    padded_ref[cx, cy, cz] = got[n * CR : (n + 1) * CR, r * 128 : (r + 1) * 128]
-
-    def convolve(padded_ref, weight_ref, x):
-        taps = [
-            padded_ref[x + a, b : b + 4, e : e + 4].reshape(16 * CR, 128)
-            for a in range(3)
-            for b in range(3)
-            for e in range(3)
-        ]
-        return dot(jnp.concatenate(taps, axis=1), weight_ref[...])
-
-    def scatter_flat(ref, value, x):
-        for yz in range(16):
-            o, v = octant_of(x, yz // 4, yz % 4)
-            ref[o * CR : (o + 1) * CR, v * 128 : (v + 1) * 128] = value[yz * CR : (yz + 1) * CR]
+                    padded_ref[cx, cy, cz // 2, cz % 2] = got[
+                        n * CR : (n + 1) * CR, r * 128 : (r + 1) * 128
+                    ]
+
+    def convolve(padded_ref, weight_ref):
+        outs = []
+        for x in range(0, 4, 1):
+            taps = [
+                padded_ref[x + a : x + a + 1, b : b + 4, zz // 2 : zz // 2 + 2, zz % 2].reshape(1 * 8 * CR, 128)
+                for a in range(3)
+                for b in range(3)
+                for zz in range(4)
+            ]
+            outs.append(dot(jnp.concatenate(taps, axis=1), weight_ref[...]))
+        return jnp.concatenate(outs, axis=0)
+
+    voxels = [
+        (row * CR, r * 128, octant_of(row // 8, row // 2 % 4, row % 2 * 2 + r))
+        for row in range(32)
+        for r in range(2)
+    ]
+
+    def scatter_flat(ref, value):
+        for row, lane, (o, v) in voxels:
+            piece = value[row : row + CR, lane : lane + 128]
+            ref[o * CR : (o + 1) * CR, v * 128 : (v + 1) * 128] = piece
 
     cin_ref[...] = to_coarse(hid_ref).astype(BF)
     fill(cin_ref, cp_ref)
-    for x in range(4):
-        value, slope = gate(convolve(cp_ref, wc_ref, x))
-        cslope_ref[x] = slope
-        scatter_flat(cout_ref, value.astype(BF), x)
+    value, slope = gate(convolve(cp_ref, wc_ref))
+    cslope_ref[...] = slope
+    scatter_flat(cout_ref, value.astype(BF))
 
     up_in = dot(up, cout_ref[...])
-    own_in, own_grad = [], []
+    pieces = [up_in[:, v * 128 : (v + 1) * 128] for v in range(8)]
+    own_in = [piece[FB : 2 * FB] for piece in pieces]
+    out = dot(jnp.concatenate(pieces, axis=0).astype(BF), wu_ref[...])
+    all_grad, own_grad = [], []
     for v in range(8):
         p, q, r = v // 4, v // 2 % 2, v % 2
-        piece = up_in[:, v * 128 : (v + 1) * 128]
-        own_in.append(piece[FB : 2 * FB])
-        out = dot(piece.astype(BF), wu_ref[...])
         grads = []
         for ab in range(4):
             a, b = ab // 2, ab % 2
             at = ((2 * p + a) * 4 + 2 * q + b) * 256 + r * 128
-            joined = out[:, ab * 128 : (ab + 1) * 128] + rows(at, 128)
+            joined = out[v * ROWS : (v + 1) * ROWS, ab * 128 : (ab + 1) * 128] + rows(at, 128)
             value, slope = gate(joined)
             dec_ref[:, at : at + 128] = value[FB : 2 * FB].astype(BF)
             grads.append(rows(XL + at, 128) * slope)
         grad = jnp.concatenate(grads, axis=1)
         own_grad.append(grad[FB : 2 * FB])
-        back = dot(grad.astype(BF), wu_ref[...], ((1,), (1,)))
-        hid_ref[:, v * 128 : (v + 1) * 128] = back.astype(BF)
+        all_grad.append(grad.astype(BF))
+    back = dot(jnp.concatenate(all_grad, axis=0), wu_ref[...], ((1,), (1,))).astype(BF)
+    for v in range(8):
+        hid_ref[:, v * 128 : (v + 1) * 128] = back[v * ROWS : (v + 1) * ROWS]
     own_in = jnp.concatenate(own_in, axis=0).astype(BF)
     own_grad = jnp.concatenate(own_grad, axis=0).astype(BF)
     found = dot(own_in, own_grad, ((0,), (0,)))
@@ -260,43 +310,50 @@
         gu_ref[n] = found[:, n * 128 : (n + 1) * 128]
 
     cin_ref[...] = to_coarse(hid_ref).astype(BF)
-    row_c = lax.broadcasted_iota(jnp.int32, (16 * CR, 128), 0) % CR
+    row_c = lax.broadcasted_iota(jnp.int32, (8 * CR, 128), 0) % CR
     mine = (row_c >= CB) & (row_c < 2 * CB)
+    for row, lane, (o, v) in voxels:
+        grad = cin_ref[o * CR : (o + 1) * CR, v * 128 : (v + 1) * 128].astype(F32)
+        grad = grad * cslope_ref[row : row + CR, lane : lane + 128]
+        cslope_ref[row : row + CR, lane : lane + 128] = grad
+        cs_ref[o * CR : (o + 1) * CR, v * 128 : (v + 1) * 128] = grad.astype(BF)
     for x in range(4):
-        pieces = []
-        for yz in range(16):
-            o, v = octant_of(x, yz // 4, yz % 4)
-            pieces.append(cin_ref[o * CR : (o + 1) * CR, v * 128 : (v + 1) * 128])
-        grad = jnp.concatenate(pieces, axis=0).astype(F32) * cslope_ref[x]
-        scatter_flat(cs_ref, grad.astype(BF), x)
-        kept = jnp.where(mine, grad, 0.0)
-        cst_ref[:, x * 256 : (x + 1) * 256] = jnp.transpose(kept).astype(BF)
+        for r in range(2):
+            kept = cslope_ref[x * 128 : (x + 1) * 128, r * 128 : (r + 1) * 128]
+            kept = jnp.transpose(jnp.where(mine, kept, 0.0)).astype(BF)
+            cst_ref[:, r * 512 + x * 128 : r * 512 + (x + 1) * 128] = kept
     for ab in range(9):
         a, b = ab // 3, ab % 3
-        taps = [
-            cp_ref[a : a + 4, b : b + 4, e : e + 4].reshape(64 * CR, 128) for e in range(3)
-        ]
+        taps = []
+        for e in range(3):
+            parts = [
+                cp_ref[a : a + 4, b : b + 4, (e + r) // 2 : (e + r) // 2 + 2, (e + r) % 2]
+                for r in range(2)
+            ]
+            parts = [part.reshape(32 * CR, 128) for part in parts]
+            taps.append(jnp.concatenate(parts, axis=0))
         found = dot(cst_ref[...], jnp.concatenate(taps, axis=1))
         for e in range(3):
             at = (3 * ab + e) * 128
             gc_ref[at : at + 128, :] = jnp.transpose(found[:, e * 128 : (e + 1) * 128])
 
     fill(cs_ref, sp_ref)
-    for x in range(4):
-        scatter_flat(cin_ref, convolve(sp_ref, wt_ref, x).astype(BF), x)
+    scatter_flat(cin_ref, convolve(sp_ref, wt_ref).astype(BF))
 
     hidden_grad = dot(up_f[FB : 2 * FB].astype(BF), cin_ref[...])
     pieces = []
     for pq in range(4):
         slope = hidden_grad[:, pq * 256 : (pq + 1) * 256] * slope_down[pq]
-        pieces += [zeros8((FB, 256)), slope, zeros8((ROWS - 2 * FB, 256))]
-    down = jnp.concatenate(pieces, axis=0).astype(BF)
+        pieces += [slope, zeros8((8, 256))]
+    down = jnp.transpose(jnp.concatenate(pieces, axis=0)).astype(BF)
     for ab in range(9):
         a, b = ab // 3, ab % 3
-        taps = [pad_ref[(2 * p + a) * 5 + 2 * q + b] for p in range(2) for q in range(2)]
-        found = dot(down, jnp.concatenate(taps, axis=0), ((0,), (0,)))
-        later = found[0:128, 0:128] + found[128:256, 128:256]
-        first = found[0:128, 256:384] + found[128:256, 0:128]
+        taps = [mine_ref[(2 * p + a) * 5 + 2 * q + b] for p in range(2) for q in range(2)]
+        taps = jnp.concatenate(taps, axis=0)
+        low = dot(down[0:128], jnp.concatenate([taps[:, 0:128], taps[:, 256:384]], axis=1))
+        high = dot(down[128:256], taps[:, 0:256])
+        later = low[:, 0:128] + high[:, 128:256]
+        first = low[:, 128:256] + high[:, 0:128]
         gd_ref[(3 * ab) * 64 : (3 * ab + 1) * 64, :] = jnp.transpose(first)[64:128]
         gd_ref[(3 * ab + 1) * 64 : (3 * ab + 3) * 64, :] = jnp.transpose(later)
 
@@ -324,27 +381,37 @@
         in_specs=[vmem] * 8,
         out_specs=(vmem, vmem),
         scratch_shapes=[
-            pltpu.VMEM((9, 384, 256), BF),
             pltpu.VMEM((4 * FB, UPPER), BF),
             pltpu.VMEM((25, ROWS, 384), BF),
+            pltpu.VMEM((25, FB + 8, 384), BF),
             pltpu.VMEM((ROWS, 1024), BF),
             pltpu.VMEM((4, HALO, 128), BF),
             pltpu.VMEM((8 * CR, 1024), BF),
-            pltpu.VMEM((6, 6, 6, CR, 128), BF),
-            pltpu.VMEM((4, 16 * CR, 128), F32),
+            pltpu.VMEM((6, 6, 3, 2, CR, 128), BF),
+            pltpu.VMEM((32 * CR, 256), F32),
             pltpu.VMEM((8 * CR, 1024), BF),
             pltpu.VMEM((8 * CR, 1024), BF),
-            pltpu.VMEM((6, 6, 6, CR, 128), BF),
+            pltpu.VMEM((6, 6, 3, 2, CR, 128), BF),
             pltpu.VMEM((128, 64 * CR), BF),
             pltpu.VMEM((1728, 128), F32),
             pltpu.VMEM((3456, 128), F32),
             pltpu.VMEM((4, 128, 128), F32),
         ],
-        compiler_params=pltpu.CompilerParams(vmem_limit_bytes=48 * 2**20),
+        compiler_params=pltpu.CompilerParams(vmem_limit_bytes=32 * 2**20),
     )(own, nxt, prev, far, wd, wc, wt, wu)
 
 
-def pack(place_ref, x_ref, cot_ref, fine_ref, parent_ref, coarse_ref, own_ref, far_ref):
+def pack(place_ref, *refs):
+    given, own_ref, far_ref, held, sems = refs[:5], refs[5], refs[6], refs[7:12], refs[12]
+    copies = [
+        pltpu.make_async_copy(source, target, sems.at[n])
+        for n, (source, target) in enumerate(zip(given, held))
+    ]
+    for copy in copies:
+        copy.start()
+    for copy in copies:
+        copy.wait()
+    x_ref, cot_ref, fine_ref, parent_ref, coarse_ref = held
     place = place_ref[0]
     own_ref[:, 0:XL] = x_ref[...].reshape(FB, XL)
     own_ref[:, XL:IDX] = cot_ref[...].reshape(FB, XL)
@@ -385,9 +452,14 @@
             jax.ShapeDtypeStruct((FB, IDX + 128), BF),
             jax.ShapeDtypeStruct((FB, SENT), BF),
         ),
-        in_specs=[pl.BlockSpec(memory_space=pltpu.SMEM)] + [vmem] * 5,
+        in_specs=[pl.BlockSpec(memory_space=pltpu.SMEM)]
+        + [pl.BlockSpec(memory_space=pltpu.HBM)] * 5,
         out_specs=(vmem, vmem),
-        compiler_params=pltpu.CompilerParams(vmem_limit_bytes=8 * 2**20),
+        scratch_shapes=[
+            pltpu.VMEM(array.shape, array.dtype)
+            for array in (features, cotangent, fine_nbr, parents, coarse_nbr)
+        ]
+        + [pltpu.SemaphoreType.DMA((5,))],
     )(place, features, cotangent, fine_nbr, parents, coarse_nbr)
 
 
@@ -458,8 +530,8 @@
     prev = shift(own, 1)
     far = shift(upper, 2)
     nxt = shift(own, -1)
-    turned = coarse_weight.reshape(27, 128, 128)[::-1].transpose(0, 2, 1).reshape(27 * 128, 128)
-    return local_pass(own, prev, nxt, far, down_weight, coarse_weight, turned, up_weight)
+    wide = widened(down_weight, coarse_weight)
+    return local_pass(own, prev, nxt, far, *wide, up_weight)
 
 
 def body(fine_features, *rest):

time: 103 us -> 98.4 us (0.955)
  local copies, waits for them, and re-layouts: 8.96 us -> 4.03 us
    pallas_call x1, Pallas kernels: 11.7 us -> 9.11 us  [local_pass(): pl.pallas_call(kernel, out_shape=(jax.ShapeDtypeStruct((FB, XL), BF), jax...]
    reshape x1 -> x0, local copies, waits for them, and re-layouts: 2.32 us -> none  [gradients(): coarse_weight.reshape(27, 128, 128)[::-1].transpose(0, 2, 1)]
    unnamed x20 -> x8, local copies, waits for them, and re-layouts: 4.56 us -> 3.17 us
    rev x1 -> x0, local copies, waits for them, and re-layouts: 1.22 us -> none  [gradients(): coarse_weight.reshape(27, 128, 128)[::-1].transpose(0, 2, 1)]
    pallas_call x1, Pallas kernels: 0.85 us -> 2.03 us  [packed(): pl.pallas_call(pack, out_shape=(jax.ShapeDtypeStruct((FB, IDX + 128), BF)...]
    all_to_all x1, blocking collectives: 7.27 us -> 8.38 us  [spread_sum(): held = lax.all_to_all(sums, 'core', 0, 0)]
  transfers between devices with their start and end apart: 4 -> 4, of which waited for: 1 -> 2; matrix products, arithmetic and copies ran while one was open for 4% -> 1% of each run, Pallas kernels for 0% -> 1%
where the time goes in v4:
time: 98.4 us; the launch traced here: 97.9 us
  blocking collectives  57.5 us (58%)
  starting transfers between devices  17.5 us (18%)
  Pallas kernels  13.3 us (14%)
  waiting for transfers between devices  4.33 us (4%)
  local copies, waits for them, and re-layouts  4.03 us (4%)
    all_to_all x1, blocking collectives, spread_sum(): held = lax.all_to_all(held, ('y', 'x'), 0, 0)  29.3 us
    all_to_all x1, blocking collectives, spread_sum(): held = lax.all_to_all(held, 'z', 0, 0)  19.8 us
    ppermute x3, starting transfers between devices, shift(): return lax.ppermute(block, SPACE, route)  11.2 us
    pallas_call x1, Pallas kernels, local_pass(): pl.pallas_call(kernel, out_shape=(jax.ShapeDtypeStruct((FB, XL), BF), jax...  9.11 us
    all_to_all x1, blocking collectives, spread_sum(): held = lax.all_to_all(sums, 'core', 0, 0)  8.38 us
    all_to_all x1, starting transfers between devices, spread_sum(): held = lax.all_to_all(held, ('y', 'core'), 0, 0)  6.32 us
    all_to_all x1, waiting for transfers between devices, spread_sum(): held = lax.all_to_all(held, ('y', 'core'), 0, 0)  4.06 us
    unnamed x8, local copies, waits for them, and re-layouts  3.17 us
  transfers between devices with their start and end apart: 4, of which 2 were waited for; matrix products, arithmetic and copies ran while one was open for 1% of the time, Pallas kernels for 1%

profile of v4, /device:TPU:1, one launch (start us, length us, event | category | flops | bytes accessed | tf_op | source)
XLA Modules:
  0.0 97.9 jit_solution(1909412497388873171)
XLA Ops:
  0.6 0.0 copy-start.3
  0.6 2.0 %shard_map.111 = (bf16[24,8320]{1,0:T(8,128)(2,1)}, bf16[24,2432]{1,0:T(8,128)(2,1)}) custom-call(s32[1]{0:T(128)} %bitcast.place_ref, bf16[24,4,4,256]{3,2,1,0:T(4,128)(2,1)} %bitcast.10, bf16[24,4,4,256]{3,2,1,0:T(4,128)(2,1)} %bitcast.11, s32[7,1,24]{2,1,0:T(1,128)} %bitcast.12, s32[1,24]{1,0:T(1,128)} %refs_3_.1, s32[6,1,26]{2,1,0:T(1,128)} %bitcast.13), custom_call_target="tpu_custom_call" | custom-call | tf_op jit(solution)/shard_map/pallas_call | solution.py:449
  2.7 4.4 %collective-permute-start.1 = (bf16[24,8320]{1,0:T(8,128)(2,1)}, bf16[24,8320]{1,0:T(8,128)(2,1)S(1)}, u32[]{:S(2)}, u32[]{:S(2)}) collective-permute-start(bf16[24,8320]{1,0:T(8,128)(2,1)} %get-tuple-element.14.own_ref), channel_id=1, source_target_pairs={{0,1},{1,2},{2,3},{3,4},{4,5},{5,6},{6,7},{7,8},{8,9},{9,10},{10,1... | collective-permute-start | bytes 1198088 | tf_op jit(solution)/shard_map/ppermute | solution.py:472
  7.1 1.3 %collective-permute-start = (bf16[24,8320]{1,0:T(8,128)(2,1)}, bf16[24,8320]{1,0:T(8,128)(2,1)S(1)}, u32[]{:S(2)}, u32[]{:S(2)}) collective-permute-start(bf16[24,8320]{1,0:T(8,128)(2,1)} %get-tuple-element.14.own_ref), channel_id=1, source_target_pairs={{1,0},{2,1},{3,2},{4,3},{5,4},{6,5},{7,6},{8,7},{9,8},{10,9},{11,1... | collective-permute-start | bytes 1198088 | tf_op jit(solution)/shard_map/ppermute | solution.py:472
  8.4 5.5 %collective-permute-start.2 = (bf16[24,2432]{1,0:T(8,128)(2,1)}, bf16[24,2432]{1,0:T(8,128)(2,1)S(1)}, u32[]{:S(2)}, u32[]{:S(2)}) collective-permute-start(bf16[24,2432]{1,0:T(8,128)(2,1)} %get-tuple-element.15), channel_id=1, source_target_pairs={{0,2},{1,3},{2,4},{3,5},{4,6},{5,7},{6,8},{7,9},{8,10},{9,11},{10,... | collective-permute-start | bytes 350216 | tf_op jit(solution)/shard_map/ppermute | solution.py:472
  13.9 0.0 copy-start
  13.9 1.2 %copy-done = bf16[3456,128]{1,0:T(8,128)(2,1)S(1)} copy-done((bf16[3456,128]{1,0:T(8,128)(2,1)S(1)}, bf16[3456,128]{1,0:T(8,128)(2,1)}, u32[]{:S(2)}) %copy-start) | copy-done | bytes 884760
  15.1 0.0 copy-start.1
  15.1 1.0 %copy-done.1 = bf16[1728,128]{1,0:T(8,128)(2,1)S(1)} copy-done((bf16[1728,128]{1,0:T(8,128)(2,1)S(1)}, bf16[1728,128]{1,0:T(8,128)(2,1)}, u32[]{:S(2)}) %copy-start.1) | copy-done | bytes 442392
  16.1 0.9 shard_map.112
  17.0 0.3 collective-permute-done.2.far_ref
  17.3 0.0 collective-permute-done.1.prev_ref
  17.3 0.0 collective-permute-done.next_ref
  17.3 0.0 copy-done.3
  17.3 0.0 copy-start.2
  17.3 1.0 %copy-done.2 = bf16[24,8320]{1,0:T(8,128)(2,1)S(1)} copy-done((bf16[24,8320]{1,0:T(8,128)(2,1)S(1)}, bf16[24,8320]{1,0:T(8,128)(2,1)}, u32[]{:S(2)}) %copy-start.2) | copy-done | bytes 399384
  18.3 9.1 %shard_map.113 = (bf16[24,4096]{1,0:T(8,128)(2,1)S(1)}, bf16[2,4,64,1536]{3,2,1,0:T(8,128)(2,1)S(1)}) custom-call(bf16[24,8320]{1,0:T(8,128)(2,1)S(1)} %copy-done.2, bf16[24,8320]{1,0:T(8,128)(2,1)S(1)} %collective-permute-done.next_ref, bf16[24,8320]{1,0:T(8,128)(2,1)S(1)} %collective-permute-done.1.prev_ref, ...), custom_call_target="tpu_custom_call" | custom-call | tf_op jit(solution)/shard_map/pallas_call | solution.py:375
  27.4 8.4 %all_to_all.20 = bf16[2,4,64,1536]{3,2,1,0:T(8,128)(2,1)S(1)} all-to-all(bf16[2,4,64,1536]{3,2,1,0:T(8,128)(2,1)S(1)} %get-tuple-element.20), channel_id=1, replica_groups=mesh['y'=4,'core'=2,'x'=4,'z'=16] {'core'}, dimensions={0} | all-to-all | bytes 3145728 | tf_op jit(solution)/shard_map/all_to_all | solution.py:489
  35.8 0.3 reduce_sum.24
  36.1 29.3 %all_to_all.21 = bf16[16,16,1536]{2,1,0:T(8,128)(2,1)S(1)} all-to-all(bf16[16,16,1536]{2,1,0:T(8,128)(2,1)S(1)} %bitcast.9), channel_id=1, replica_groups=mesh['y'=4,'core'=2,'x'=4,'z'=16] {'y','x'}, dimensions={0} | all-to-all | bytes 1572864 | tf_op jit(solution)/shard_map/all_to_all | solution.py:492
  65.5 0.1 reduce_sum.25
  65.6 0.1 reshape.32
  65.6 19.8 %all_to_all.22.in_ref = bf16[16,12,128]{2,1,0:T(8,128)(2,1)S(1)} all-to-all(bf16[16,12,128]{2,1,0:T(8,128)(2,1)S(1)} %reshape.32), channel_id=1, replica_groups=mesh['y'=4,'core'=2,'x'=4,'z'=16] {'z'}, dimensions={0} | all-to-all | bytes 98304 | tf_op jit(solution)/shard_map/all_to_all | solution.py:495
  85.4 0.6 shard_map.114
  86.1 6.3 %all-to-all-start.3 = ((f32[8,12,128]{2,1,0:T(8,128)}), f32[8,12,128]{2,1,0:T(8,128)S(1)}, u32[]{:S(2)}, u32[]{:S(2)}) async-start(f32[8,12,128]{2,1,0:T(8,128)} %shard_map.114), calls=%async_computation.3 | async-start | bytes 131072 | tf_op jit(solution)/shard_map/all_to_all | solution.py:501
  92.4 0.8 reshape.30
  93.2 4.1 %all-to-all-done.3.in_ref = f32[8,12,128]{2,1,0:T(8,128)S(1)} async-done(((f32[8,12,128]{2,1,0:T(8,128)}), f32[8,12,128]{2,1,0:T(8,128)S(1)}, u32[]{:S(2)}, u32[]{:S(2)}) %all-to-all-start.3) | async-done | bytes 49184 | tf_op jit(solution)/shard_map/all_to_all | solution.py:501
  97.3 0.6 shard_map.115
Async XLA Ops:
  0.6 16.6 %copy-start.3 = (bf16[128,512]{1,0:T(8,128)(2,1)S(1)}, bf16[128,512]{1,0:T(8,128)(2,1)}, u32[]{:S(2)}) copy-start(bf16[128,512]{1,0:T(8,128)(2,1)} %wu_ref.1) | copy-start | bytes 393220
  2.7 14.6 %collective-permute-start.1 = (bf16[24,8320]{1,0:T(8,128)(2,1)}, bf16[24,8320]{1,0:T(8,128)(2,1)S(1)}, u32[]{:S(2)}, u32[]{:S(2)}) collective-permute-start(bf16[24,8320]{1,0:T(8,128)(2,1)} %get-tuple-element.14.own_ref), channel_id=1, source_target_pairs={{0,1},{1,2},{2,3},{3,4},{4,5},{5,6},{6,7},{7,8},{8,9},{9,10},{10,1... | collective-permute-start | bytes 1198088 | tf_op jit(solution)/shard_map/ppermute | solution.py:472
  7.1 10.2 %collective-permute-start = (bf16[24,8320]{1,0:T(8,128)(2,1)}, bf16[24,8320]{1,0:T(8,128)(2,1)S(1)}, u32[]{:S(2)}, u32[]{:S(2)}) collective-permute-start(bf16[24,8320]{1,0:T(8,128)(2,1)} %get-tuple-element.14.own_ref), channel_id=1, source_target_pairs={{1,0},{2,1},{3,2},{4,3},{5,4},{6,5},{7,6},{8,7},{9,8},{10,9},{11,1... | collective-permute-start | bytes 1198088 | tf_op jit(solution)/shard_map/ppermute | solution.py:472
  8.4 8.9 %collective-permute-start.2 = (bf16[24,2432]{1,0:T(8,128)(2,1)}, bf16[24,2432]{1,0:T(8,128)(2,1)S(1)}, u32[]{:S(2)}, u32[]{:S(2)}) collective-permute-start(bf16[24,2432]{1,0:T(8,128)(2,1)} %get-tuple-element.15), channel_id=1, source_target_pairs={{0,2},{1,3},{2,4},{3,5},{4,6},{5,7},{6,8},{7,9},{8,10},{9,11},{10,... | collective-permute-start | bytes 350216 | tf_op jit(solution)/shard_map/ppermute | solution.py:472
  13.9 1.2 %copy-start = (bf16[3456,128]{1,0:T(8,128)(2,1)S(1)}, bf16[3456,128]{1,0:T(8,128)(2,1)}, u32[]{:S(2)}) copy-start(bf16[3456,128]{1,0:T(8,128)(2,1)} %wc_ref.1) | copy-start | bytes 2654212
  15.1 1.0 %copy-start.1 = (bf16[1728,128]{1,0:T(8,128)(2,1)S(1)}, bf16[1728,128]{1,0:T(8,128)(2,1)}, u32[]{:S(2)}) copy-start(bf16[1728,128]{1,0:T(8,128)(2,1)} %wd_ref.1) | copy-start | bytes 1327108
  17.3 1.0 %copy-start.2 = (bf16[24,8320]{1,0:T(8,128)(2,1)S(1)}, bf16[24,8320]{1,0:T(8,128)(2,1)}, u32[]{:S(2)}) copy-start(bf16[24,8320]{1,0:T(8,128)(2,1)} %get-tuple-element.14.own_ref) | copy-start | bytes 1198084
  86.1 11.2 %all-to-all-start.3 = ((f32[8,12,128]{2,1,0:T(8,128)}), f32[8,12,128]{2,1,0:T(8,128)S(1)}, u32[]{:S(2)}, u32[]{:S(2)}) async-start(f32[8,12,128]{2,1,0:T(8,128)} %shard_map.114), calls=%async_computation.3 | async-start | bytes 131072 | tf_op jit(solution)/shard_map/all_to_all | solution.py:501

commit v5 on v4

--- a/solution.py
+++ b/solution.py
@@ -14,7 +14,9 @@
 ROWS = 80
 CR = 16
 XL = 4096
-IDX = 2 * XL
+EARLY = 7 * 256
+IDX = XL + EARLY
+VMEM_A, VMEM_B = 20 * 2**20, 24 * 2**20
 TILES = 96
 
 
@@ -79,7 +81,9 @@
     return 4 * (x // 2) + 2 * (y // 2) + z // 2, 4 * (x % 2) + 2 * (y % 2) + z % 2
 
 
-def widen(wd_ref, wc_ref, down_ref, coarse_ref, turned_ref):
+def widen(wd_ref, wc_ref, x_ref, cot_ref, down_ref, coarse_ref, turned_ref, own_ref, cots_ref):
+    own_ref[...] = x_ref[...]
+    cots_ref[...] = cot_ref[...]
     down_ref[...] = jnp.zeros(down_ref.shape, BF)
     for ab in range(9):
         tap = [wd_ref[(3 * ab + e) * 64 : (3 * ab + e + 1) * 64, :] for e in range(3)]
@@ -104,51 +108,91 @@
             ref[ab * 512 : ab * 512 + 128, 128:256] = zero
 
 
-def widened(down_weight, coarse_weight):
+def widened(down_weight, coarse_weight, own, cot):
     vmem = pl.BlockSpec(memory_space=pltpu.VMEM)
-    shapes = ((9 * 384, 256), (9 * 512, 256), (9 * 512, 256))
+    shapes = ((9 * 384, 256), (9 * 512, 256), (9 * 512, 256), own.shape, cot.shape)
     return pl.pallas_call(
         widen,
         out_shape=tuple(jax.ShapeDtypeStruct(shape, BF) for shape in shapes),
-        in_specs=[vmem] * 2,
-        out_specs=(vmem,) * 3,
+        in_specs=[vmem] * 4,
+        out_specs=(vmem,) * 5,
         compiler_params=pltpu.CompilerParams(vmem_limit_bytes=12 * 2**20),
-    )(down_weight, coarse_weight)
-
-
-def kernel(
+    )(down_weight, coarse_weight, own, cot)
+
+
+def rows_of(refs, lane, width):
+    parts = [ref[:, lane : lane + width].astype(F32) for ref in refs]
+    return jnp.concatenate(parts + [jnp.zeros((ROWS - 3 * FB, width), F32)], axis=0)
+
+
+def to_coarse(up, ref):
+    return dot(up, ref[...], ((0,), (0,)))
+
+
+def fill(nl_ref, flat_ref, padded_ref):
+    for x in range(4):
+        for y in range(4):
+            for z in range(4):
+                o, v = octant_of(x, y, z)
+                padded_ref[x + 1, y + 1, (z + 1) // 2, (z + 1) % 2] = flat_ref[
+                    o * CR : (o + 1) * CR, v * 128 : (v + 1) * 128
+                ]
+    for pq in range(4):
+        got = dot(nl_ref[pq], flat_ref[:, pq * 256 : (pq + 1) * 256]).astype(BF)
+        for n, (_, _, targets) in enumerate(halo_blocks(pq // 2, pq % 2)):
+            for r, (cx, cy, cz) in targets:
+                padded_ref[cx, cy, cz // 2, cz % 2] = got[
+                    n * CR : (n + 1) * CR, r * 128 : (r + 1) * 128
+                ]
+
+
+def convolve(padded_ref, weight_ref):
+    outs = []
+    for x in range(0, 4, 1):
+        taps = [
+            padded_ref[x + a : x + a + 1, b : b + 4, zz // 2 : zz // 2 + 2, zz % 2].reshape(1 * 8 * CR, 128)
+            for a in range(3)
+            for b in range(3)
+            for zz in range(4)
+        ]
+        outs.append(dot(jnp.concatenate(taps, axis=1), weight_ref[...]))
+    return jnp.concatenate(outs, axis=0)
+
+
+VOXELS = [
+    (row * CR, r * 128, octant_of(row // 8, row // 2 % 4, row % 2 * 2 + r))
+    for row in range(32)
+    for r in range(2)
+]
+
+
+def scatter_flat(ref, value):
+    for row, lane, (o, v) in VOXELS:
+        piece = value[row : row + CR, lane : lane + 128]
+        ref[o * CR : (o + 1) * CR, v * 128 : (v + 1) * 128] = piece
+
+
+def forward(
     own_ref,
+    prev_ref,
     next_ref,
-    prev_ref,
     far_ref,
     wd_ref,
     wc_ref,
-    wt_ref,
-    wu_ref,
-    dec_ref,
-    sum_ref,
-    src_ref,
-    pad_ref,
     mine_ref,
-    hid_ref,
+    up_ref,
     nl_ref,
-    cin_ref,
     cp_ref,
     cslope_ref,
     cout_ref,
-    cs_ref,
-    sp_ref,
-    cst_ref,
-    gd_ref,
-    gc_ref,
-    gu_ref,
+    dslope_ref,
+    src_ref,
+    pad_ref,
+    hid_ref,
+    cin_ref,
 ):
     zeros8 = functools.partial(jnp.zeros, dtype=F32)
-
-    def rows(lane, width):
-        at = slice(lane, lane + width)
-        parts = [r[:, at].astype(F32) for r in (prev_ref, own_ref, next_ref)]
-        return jnp.concatenate(parts + [zeros8((ROWS - 3 * FB, width))], axis=0)
+    rows = functools.partial(rows_of, (prev_ref, own_ref, next_ref))
 
     idx = rows(IDX, 128)
     row = lax.broadcasted_iota(jnp.int32, (ROWS, 128), 0)
@@ -206,20 +250,17 @@
             taps = [pad_ref[(2 * p + a) * 5 + 2 * q + b] for a in range(3) for b in range(3)]
             outs.append(dot(jnp.concatenate(taps, axis=1), wd_ref[...]))
     pre = jnp.concatenate(outs, axis=0)
-    slope_down = []
     for pq in range(4):
         value, slope = gate(pre[pq * ROWS : (pq + 1) * ROWS])
         hid_ref[:, pq * 256 : (pq + 1) * 256] = value.astype(BF)
-        slope_down.append(slope[FB : 2 * FB])
+        dslope_ref[pq] = slope[FB : 2 * FB]
 
     code = idx[:, 7:8]
     slot = jnp.where(code > 0.0, code + (48.0 * block[:, 0:1] - 9.0), -1.0)
     column = (lane % CR * 8 + lane // CR).astype(F32)
     up_f = jnp.where(column == slot, 1.0, 0.0)
+    up_ref[...] = up_f
     up = up_f.astype(BF)
-
-    def to_coarse(ref):
-        return dot(up, ref[...], ((0,), (0,)))
 
     row16 = lax.broadcasted_iota(jnp.int32, (CR, ROWS), 0)
     lane80 = lax.broadcasted_iota(jnp.int32, (CR, ROWS), 1)
@@ -237,50 +278,52 @@
             blocks.append(jnp.where(lane16 == wanted, 1.0, 0.0))
         nl_ref[pq] = jnp.concatenate(blocks, axis=0).astype(BF)
 
-    def fill(flat_ref, padded_ref):
-        for x in range(4):
-            for y in range(4):
-                for z in range(4):
-                    o, v = octant_of(x, y, z)
-                    padded_ref[x + 1, y + 1, (z + 1) // 2, (z + 1) % 2] = flat_ref[
-                        o * CR : (o + 1) * CR, v * 128 : (v + 1) * 128
-                    ]
-        for pq in range(4):
-            got = dot(nl_ref[pq], flat_ref[:, pq * 256 : (pq + 1) * 256]).astype(BF)
-            for n, (_, _, targets) in enumerate(halo_blocks(pq // 2, pq % 2)):
-                for r, (cx, cy, cz) in targets:
-                    padded_ref[cx, cy, cz // 2, cz % 2] = got[
-                        n * CR : (n + 1) * CR, r * 128 : (r + 1) * 128
-                    ]
-
-    def convolve(padded_ref, weight_ref):
-        outs = []
-        for x in range(0, 4, 1):
-            taps = [
-                padded_ref[x + a : x + a + 1, b : b + 4, zz // 2 : zz // 2 + 2, zz % 2].reshape(1 * 8 * CR, 128)
-                for a in range(3)
-                for b in range(3)
-                for zz in range(4)
-            ]
-            outs.append(dot(jnp.concatenate(taps, axis=1), weight_ref[...]))
-        return jnp.concatenate(outs, axis=0)
-
-    voxels = [
-        (row * CR, r * 128, octant_of(row // 8, row // 2 % 4, row % 2 * 2 + r))
-        for row in range(32)
-        for r in range(2)
-    ]
-
-    def scatter_flat(ref, value):
-        for row, lane, (o, v) in voxels:
-            piece = value[row : row + CR, lane : lane + 128]
-            ref[o * CR : (o + 1) * CR, v * 128 : (v + 1) * 128] = piece
-
-    cin_ref[...] = to_coarse(hid_ref).astype(BF)
-    fill(cin_ref, cp_ref)
+    cin_ref[...] = to_coarse(up, hid_ref).astype(BF)
+    fill(nl_ref, cin_ref, cp_ref)
     value, slope = gate(convolve(cp_ref, wc_ref))
     cslope_ref[...] = slope
     scatter_flat(cout_ref, value.astype(BF))
+
+
+def backward(
+    own_ref,
+    prev_ref,
+    next_ref,
+    cot_own_ref,
+    cot_prev_ref,
+    cot_next_ref,
+    wt_ref,
+    wu_ref,
+    mine_ref,
+    up_ref,
+    nl_ref,
+    cp_ref,
+    cslope_ref,
+    cout_ref,
+    dslope_ref,
+    dec_ref,
+    sum_ref,
+    hid_ref,
+    cin_ref,
+    cs_ref,
+    sp_ref,
+    cst_ref,
+    grad_ref,
+    gd_ref,
+    gc_ref,
+    gu_ref,
+):
+    zeros8 = functools.partial(jnp.zeros, dtype=F32)
+    rows = functools.partial(rows_of, (prev_ref, own_ref, next_ref))
+
+
+    def cot_rows(lane, width):
+        if lane < EARLY:
+            return rows(XL + lane, width)
+        return rows_of((cot_prev_ref, cot_own_ref, cot_next_ref), lane - EARLY, width)
+
+    up_f = up_ref[...]
+    up = up_f.astype(BF)
 
     up_in = dot(up, cout_ref[...])
     pieces = [up_in[:, v * 128 : (v + 1) * 128] for v in range(8)]
@@ -296,7 +339,7 @@
             joined = out[v * ROWS : (v + 1) * ROWS, ab * 128 : (ab + 1) * 128] + rows(at, 128)
             value, slope = gate(joined)
             dec_ref[:, at : at + 128] = value[FB : 2 * FB].astype(BF)
-            grads.append(rows(XL + at, 128) * slope)
+            grads.append(cot_rows(at, 128) * slope)
         grad = jnp.concatenate(grads, axis=1)
         own_grad.append(grad[FB : 2 * FB])
         all_grad.append(grad.astype(BF))
@@ -309,17 +352,17 @@
     for n in range(4):
         gu_ref[n] = found[:, n * 128 : (n + 1) * 128]
 
-    cin_ref[...] = to_coarse(hid_ref).astype(BF)
+    cin_ref[...] = to_coarse(up, hid_ref).astype(BF)
     row_c = lax.broadcasted_iota(jnp.int32, (8 * CR, 128), 0) % CR
     mine = (row_c >= CB) & (row_c < 2 * CB)
-    for row, lane, (o, v) in voxels:
+    for row, lane, (o, v) in VOXELS:
         grad = cin_ref[o * CR : (o + 1) * CR, v * 128 : (v + 1) * 128].astype(F32)
         grad = grad * cslope_ref[row : row + CR, lane : lane + 128]
-        cslope_ref[row : row + CR, lane : lane + 128] = grad
+        grad_ref[row : row + CR, lane : lane + 128] = grad
         cs_ref[o * CR : (o + 1) * CR, v * 128 : (v + 1) * 128] = grad.astype(BF)
     for x in range(4):
         for r in range(2):
-            kept = cslope_ref[x * 128 : (x + 1) * 128, r * 128 : (r + 1) * 128]
+            kept = grad_ref[x * 128 : (x + 1) * 128, r * 128 : (r + 1) * 128]
             kept = jnp.transpose(jnp.where(mine, kept, 0.0)).astype(BF)
             cst_ref[:, r * 512 + x * 128 : r * 512 + (x + 1) * 128] = kept
     for ab in range(9):
@@ -337,13 +380,13 @@
             at = (3 * ab + e) * 128
             gc_ref[at : at + 128, :] = jnp.transpose(found[:, e * 128 : (e + 1) * 128])
 
-    fill(cs_ref, sp_ref)
+    fill(nl_ref, cs_ref, sp_ref)
     scatter_flat(cin_ref, convolve(sp_ref, wt_ref).astype(BF))
 
     hidden_grad = dot(up_f[FB : 2 * FB].astype(BF), cin_ref[...])
     pieces = []
     for pq in range(4):
-        slope = hidden_grad[:, pq * 256 : (pq + 1) * 256] * slope_down[pq]
+        slope = hidden_grad[:, pq * 256 : (pq + 1) * 256] * dslope_ref[pq]
         pieces += [slope, zeros8((8, 256))]
     down = jnp.transpose(jnp.concatenate(pieces, axis=0)).astype(BF)
     for ab in range(9):
@@ -370,39 +413,60 @@
         sum_ref[t // 12 % 2, t // 24, :, n * 128 : (n + 1) * 128] = tile.astype(BF)
 
 
-def local_pass(own, prev, nxt, far, wd, wc, wt, wu):
+def forward_pass(own, prev, nxt, far, wd, wc):
+    vmem = pl.BlockSpec(memory_space=pltpu.VMEM)
+    made = (
+        ((25, FB + 8, 384), BF),
+        ((ROWS, 128), F32),
+        ((4, HALO, 128), BF),
+        ((6, 6, 3, 2, CR, 128), BF),
+        ((32 * CR, 256), F32),
+        ((8 * CR, 1024), BF),
+        ((4, FB, 256), F32),
+    )
+    return pl.pallas_call(
+        forward,
+        out_shape=tuple(jax.ShapeDtypeStruct(*one) for one in made),
+        in_specs=[vmem] * 6,
+        out_specs=(vmem,) * len(made),
+        scratch_shapes=[
+            pltpu.VMEM((4 * FB, UPPER), BF),
+            pltpu.VMEM((25, ROWS, 384), BF),
+            pltpu.VMEM((ROWS, 1024), BF),
+            pltpu.VMEM((8 * CR, 1024), BF),
+        ],
+        compiler_params=pltpu.CompilerParams(vmem_limit_bytes=VMEM_A),
+    )(own, prev, nxt, far, wd, wc)
+
+
+def backward_pass(*given):
     vmem = pl.BlockSpec(memory_space=pltpu.VMEM)
     return pl.pallas_call(
-        kernel,
+        backward,
         out_shape=(
             jax.ShapeDtypeStruct((FB, XL), BF),
             jax.ShapeDtypeStruct((2, 4, 64, 1536), BF),
         ),
-        in_specs=[vmem] * 8,
+        in_specs=[vmem] * len(given),
         out_specs=(vmem, vmem),
         scratch_shapes=[
-            pltpu.VMEM((4 * FB, UPPER), BF),
-            pltpu.VMEM((25, ROWS, 384), BF),
-            pltpu.VMEM((25, FB + 8, 384), BF),
             pltpu.VMEM((ROWS, 1024), BF),
-            pltpu.VMEM((4, HALO, 128), BF),
-            pltpu.VMEM((8 * CR, 1024), BF),
-            pltpu.VMEM((6, 6, 3, 2, CR, 128), BF),
-            pltpu.VMEM((32 * CR, 256), F32),
             pltpu.VMEM((8 * CR, 1024), BF),
             pltpu.VMEM((8 * CR, 1024), BF),
             pltpu.VMEM((6, 6, 3, 2, CR, 128), BF),
             pltpu.VMEM((128, 64 * CR), BF),
+            pltpu.VMEM((32 * CR, 256), F32),
             pltpu.VMEM((1728, 128), F32),
             pltpu.VMEM((3456, 128), F32),
             pltpu.VMEM((4, 128, 128), F32),
         ],
-        compiler_params=pltpu.CompilerParams(vmem_limit_bytes=32 * 2**20),
-    )(own, nxt, prev, far, wd, wc, wt, wu)
+        compiler_params=pltpu.CompilerParams(vmem_limit_bytes=VMEM_B),
+    )(*given)
 
 
 def pack(place_ref, *refs):
-    given, own_ref, far_ref, held, sems = refs[:5], refs[5], refs[6], refs[7:12], refs[12]
+    given, held, sems = refs[:5], refs[8:13], refs[13]
+    own_ref, cots_ref, far_ref = refs[5:8]
     copies = [
         pltpu.make_async_copy(source, target, sems.at[n])
         for n, (source, target) in enumerate(zip(given, held))
@@ -414,7 +478,9 @@
     x_ref, cot_ref, fine_ref, parent_ref, coarse_ref = held
     place = place_ref[0]
     own_ref[:, 0:XL] = x_ref[...].reshape(FB, XL)
-    own_ref[:, XL:IDX] = cot_ref[...].reshape(FB, XL)
+    cot = cot_ref[...].reshape(FB, XL)
+    own_ref[:, XL:IDX] = cot[:, 0:EARLY]
+    cots_ref[...] = cot[:, EARLY:XL]
     fine = jnp.concatenate([fine_ref[m] for m in range(7)], axis=0)
     fine = jnp.where(fine < 0, 0, fine - (FB * (place - 1) - 1)).astype(F32)
     coarse = jnp.concatenate([coarse_ref[c] for c in range(CB)], axis=0)
@@ -450,11 +516,12 @@
         pack,
         out_shape=(
             jax.ShapeDtypeStruct((FB, IDX + 128), BF),
+            jax.ShapeDtypeStruct((FB, XL - EARLY), BF),
             jax.ShapeDtypeStruct((FB, SENT), BF),
         ),
         in_specs=[pl.BlockSpec(memory_space=pltpu.SMEM)]
         + [pl.BlockSpec(memory_space=pltpu.HBM)] * 5,
-        out_specs=(vmem, vmem),
+        out_specs=(vmem,) * 3,
         scratch_shapes=[
             pltpu.VMEM(array.shape, array.dtype)
             for array in (features, cotangent, fine_nbr, parents, coarse_nbr)
@@ -519,7 +586,7 @@
     coarse_neighbours,
 ):
     place = lax.axis_index(SPACE).astype(jnp.int32).reshape(1)
-    own, upper = packed(
+    own, cot, upper = packed(
         place,
         fine_features[0],
         cotangent[0],
@@ -530,8 +597,11 @@
     prev = shift(own, 1)
     far = shift(upper, 2)
     nxt = shift(own, -1)
-    wide = widened(down_weight, coarse_weight)
-    return local_pass(own, prev, nxt, far, *wide, up_weight)
+    cot_prev = shift(cot, 1)
+    cot_next = shift(cot, -1)
+    wide_down, wide, turned, own, cot = widened(down_weight, coarse_weight, own, cot)
+    kept = forward_pass(own, prev, nxt, far, wide_down, wide)
+    return backward_pass(own, prev, nxt, cot, cot_prev, cot_next, turned, up_weight, *kept)
 
 
 def body(fine_features, *rest):

time: 98.4 us -> 99.6 us (1.012)
  starting transfers between devices: 17.5 us -> 23.6 us
  blocking collectives: 57.5 us -> 51.8 us
    ppermute x3 -> x5, starting transfers between devices: 11.2 us -> 17.2 us  [shift(): return lax.ppermute(block, SPACE, route)]
    all_to_all x1, blocking collectives: 29.3 us -> 26.3 us  [spread_sum(): held = lax.all_to_all(held, ('y', 'x'), 0, 0)]
    all_to_all x1, blocking collectives: 8.38 us -> 6.14 us  [spread_sum(): held = lax.all_to_all(sums, 'core', 0, 0)]
    unnamed x8 -> x10, local copies, waits for them, and re-layouts: 3.17 us -> 4.04 us
    pallas_call x1 -> x2, Pallas kernels: 9.11 us -> 9.23 us  [the longest x1 5.47 us: backward_pass(): pl.pallas_call(backward, out_shape=(jax.ShapeDtypeStruct((FB, XL), BF), j...]
  transfers between devices with their start and end apart: 4 -> 6, of which waited for: 2 -> 1; matrix products, arithmetic and copies ran while one was open for 1% -> 1% of each run, Pallas kernels for 1% -> 5%
where the time goes in v5:
time: 99.6 us; the launch traced here: 99 us
  blocking collectives  51.8 us (52%)
  starting transfers between devices  23.6 us (24%)
  Pallas kernels  13.4 us (13%)
  local copies, waits for them, and re-layouts  4.9 us (5%)
  waiting for transfers between devices  4.07 us (4%)
    all_to_all x1, blocking collectives, spread_sum(): held = lax.all_to_all(held, ('y', 'x'), 0, 0)  26.3 us
    all_to_all x1, blocking collectives, spread_sum(): held = lax.all_to_all(held, 'z', 0, 0)  19.4 us
    ppermute x5, starting transfers between devices, shift(): return lax.ppermute(block, SPACE, route)  17.2 us
    all_to_all x1, starting transfers between devices, spread_sum(): held = lax.all_to_all(held, ('y', 'core'), 0, 0)  6.32 us
    all_to_all x1, blocking collectives, spread_sum(): held = lax.all_to_all(sums, 'core', 0, 0)  6.14 us
    pallas_call x1, Pallas kernels, backward_pass(): pl.pallas_call(backward, out_shape=(jax.ShapeDtypeStruct((FB, XL), BF), j...  5.47 us
    all_to_all x1, waiting for transfers between devices, spread_sum(): held = lax.all_to_all(held, ('y', 'core'), 0, 0)  4.06 us
    unnamed x10, local copies, waits for them, and re-layouts  4.04 us
  transfers between devices with their start and end apart: 6, of which 1 were waited for; matrix products, arithmetic and copies ran while one was open for 1% of the time, Pallas kernels for 5%

profile of v5, /device:TPU:1, one launch (start us, length us, event | category | flops | bytes accessed | tf_op | source)
XLA Modules:
  0.0 99.0 jit_solution(3070316297539494661)
XLA Ops:
  0.6 2.0 %shard_map.111 = (bf16[24,6016]{1,0:T(8,128)(2,1)}, bf16[24,2304]{1,0:T(8,128)(2,1)}, bf16[24,2432]{1,0:T(8,128)(2,1)}) custom-call(s32[1]{0:T(128)} %bitcast.place_ref, bf16[24,4,4,256]{3,2,1,0:T(4,128)(2,1)} %bitcast.10, bf16[24,4,4,256]{3,2,1,0:T(4,128)(2,1)} %bitcast.11, s32[7,1,24]{2,1,0:T(1,128)} %bitcast.12, s32[1,24]{1,0:T(1,128)} %refs_3_.1, ...), custom_call_target="tpu_custom_call" | custom-call | tf_op jit(solution)/shard_map/pallas_call | solution.py:515
  2.6 4.4 %collective-permute-start = (bf16[24,6016]{1,0:T(8,128)(2,1)}, bf16[24,6016]{1,0:T(8,128)(2,1)S(1)}, u32[]{:S(2)}, u32[]{:S(2)}) collective-permute-start(bf16[24,6016]{1,0:T(8,128)(2,1)} %get-tuple-element.24.x_ref), channel_id=1, source_target_pairs={{0,1},{1,2},{2,3},{3,4},{4,5},{5,6},{6,7},{7,8},{8,9},{9,10},{10,1... | collective-permute-start | bytes 866312 | tf_op jit(solution)/shard_map/ppermute | solution.py:539
  7.0 1.3 %collective-permute-start.1 = (bf16[24,6016]{1,0:T(8,128)(2,1)}, bf16[24,6016]{1,0:T(8,128)(2,1)S(1)}, u32[]{:S(2)}, u32[]{:S(2)}) collective-permute-start(bf16[24,6016]{1,0:T(8,128)(2,1)} %get-tuple-element.24.x_ref), channel_id=1, source_target_pairs={{1,0},{2,1},{3,2},{4,3},{5,4},{6,5},{7,6},{8,7},{9,8},{10,9},{11,1... | collective-permute-start | bytes 866312 | tf_op jit(solution)/shard_map/ppermute | solution.py:539
  8.3 5.5 %collective-permute-start.4 = (bf16[24,2432]{1,0:T(8,128)(2,1)}, bf16[24,2432]{1,0:T(8,128)(2,1)S(1)}, u32[]{:S(2)}, u32[]{:S(2)}) collective-permute-start(bf16[24,2432]{1,0:T(8,128)(2,1)} %get-tuple-element.29), channel_id=1, source_target_pairs={{0,2},{1,3},{2,4},{3,5},{4,6},{5,7},{6,8},{7,9},{8,10},{9,11},{10,... | collective-permute-start | bytes 350216 | tf_op jit(solution)/shard_map/ppermute | solution.py:539
  13.8 4.8 %collective-permute-start.2 = (bf16[24,2304]{1,0:T(8,128)(2,1)}, bf16[24,2304]{1,0:T(8,128)(2,1)S(1)}, u32[]{:S(2)}, u32[]{:S(2)}) collective-permute-start(bf16[24,2304]{1,0:T(8,128)(2,1)} %get-tuple-element.25.cot_ref), channel_id=1, source_target_pairs={{0,1},{1,2},{2,3},{3,4},{4,5},{5,6},{6,7},{7,8},{8,9},{9,10},{10,1... | collective-permute-start | bytes 331784 | tf_op jit(solution)/shard_map/ppermute | solution.py:539
  18.6 1.3 %collective-permute-start.3 = (bf16[24,2304]{1,0:T(8,128)(2,1)}, bf16[24,2304]{1,0:T(8,128)(2,1)S(1)}, u32[]{:S(2)}, u32[]{:S(2)}) collective-permute-start(bf16[24,2304]{1,0:T(8,128)(2,1)} %get-tuple-element.25.cot_ref), channel_id=1, source_target_pairs={{1,0},{2,1},{3,2},{4,3},{5,4},{6,5},{7,6},{8,7},{9,8},{10,9},{11,1... | collective-permute-start | bytes 331784 | tf_op jit(solution)/shard_map/ppermute | solution.py:539
  19.9 0.0 copy-start
  19.9 1.2 %copy-done = bf16[3456,128]{1,0:T(8,128)(2,1)S(1)} copy-done((bf16[3456,128]{1,0:T(8,128)(2,1)S(1)}, bf16[3456,128]{1,0:T(8,128)(2,1)}, u32[]{:S(2)}) %copy-start) | copy-done | bytes 884760
  21.1 1.0 %copy-done.1 = bf16[1728,128]{1,0:T(8,128)(2,1)S(1)} copy-done((bf16[1728,128]{1,0:T(8,128)(2,1)S(1)}, bf16[1728,128]{1,0:T(8,128)(2,1)}, u32[]{:S(2)}) %copy-start.1) | copy-done | bytes 442392
  22.1 1.0 copy-done.2
  23.1 0.9 copy-done.4
  24.0 0.9 shard_map.112
  24.9 0.0 collective-permute-done.4.far_ref
  24.9 0.0 collective-permute-done.prev_ref
  24.9 0.0 collective-permute-done.1.next_ref
  24.9 0.0 copy-start.3
  24.9 3.8 %shard_map.113 = (bf16[25,32,384]{2,1,0:T(8,128)(2,1)S(1)}, f32[80,128]{1,0:T(8,128)S(1)}, bf16[4,448,128]{2,1,0:T(8,128)(2,1)S(1)}, bf16[6,6,3,2,16,128]{5,4,3,...) custom-call(bf16[24,6016]{1,0:T(8,128)(2,1)S(1)} %get-tuple-element.26.own, ...), custom_call_target="tpu_custom_call" | custom-call | tf_op jit(solution)/shard_map/pallas_call | solution.py:427
  28.7 0.0 collective-permute-done.2.cot_prev_ref
  28.7 0.0 collective-permute-done.3.cot_next_ref
  28.7 0.0 copy-done.3
  28.7 5.5 %shard_map.114 = (bf16[24,4096]{1,0:T(8,128)(2,1)S(1)}, bf16[2,4,64,1536]{3,2,1,0:T(8,128)(2,1)S(1)}) custom-call(bf16[24,6016]{1,0:T(8,128)(2,1)S(1)} %get-tuple-element.26.own_ref, bf16[24,6016]{1,0:T(8,128)(2,1)S(1)} %collective-permute-done.prev_ref, bf16[24,6016]{1,0:T(8,128)(2,1)S(1)} %collective-permute-done.1.next_ref, ...), custom_call_target="tpu_custom_call" | custom-call | tf_op jit(solution)/shard_map/pallas_call | solution.py:444
  34.2 6.1 %all_to_all.20 = bf16[2,4,64,1536]{3,2,1,0:T(8,128)(2,1)S(1)} all-to-all(bf16[2,4,64,1536]{3,2,1,0:T(8,128)(2,1)S(1)} %get-tuple-element.40), channel_id=1, replica_groups=mesh['y'=4,'core'=2,'x'=4,'z'=16] {'core'}, dimensions={0} | all-to-all | bytes 3145728 | tf_op jit(solution)/shard_map/all_to_all | solution.py:556
  40.4 0.3 reduce_sum.24
  40.7 26.3 %all_to_all.21 = bf16[16,16,1536]{2,1,0:T(8,128)(2,1)S(1)} all-to-all(bf16[16,16,1536]{2,1,0:T(8,128)(2,1)S(1)} %bitcast.9), channel_id=1, replica_groups=mesh['y'=4,'core'=2,'x'=4,'z'=16] {'y','x'}, dimensions={0} | all-to-all | bytes 1572864 | tf_op jit(solution)/shard_map/all_to_all | solution.py:559
  67.0 0.1 reduce_sum.25
  67.1 0.1 reshape.32
  67.2 19.4 %all_to_all.22.in_ref = bf16[16,12,128]{2,1,0:T(8,128)(2,1)S(1)} all-to-all(bf16[16,12,128]{2,1,0:T(8,128)(2,1)S(1)} %reshape.32), channel_id=1, replica_groups=mesh['y'=4,'core'=2,'x'=4,'z'=16] {'z'}, dimensions={0} | all-to-all | bytes 98304 | tf_op jit(solution)/shard_map/all_to_all | solution.py:562
  86.6 0.6 shard_map.115
  87.2 6.3 %all-to-all-start.3 = ((f32[8,12,128]{2,1,0:T(8,128)}), f32[8,12,128]{2,1,0:T(8,128)S(1)}, u32[]{:S(2)}, u32[]{:S(2)}) async-start(f32[8,12,128]{2,1,0:T(8,128)} %shard_map.115), calls=%async_computation.3 | async-start | bytes 131072 | tf_op jit(solution)/shard_map/all_to_all | solution.py:568
  93.5 0.8 reshape.30
  94.3 4.1 %all-to-all-done.3.in_ref = f32[8,12,128]{2,1,0:T(8,128)S(1)} async-done(((f32[8,12,128]{2,1,0:T(8,128)}), f32[8,12,128]{2,1,0:T(8,128)S(1)}, u32[]{:S(2)}, u32[]{:S(2)}) %all-to-all-start.3) | async-done | bytes 49184 | tf_op jit(solution)/shard_map/all_to_all | solution.py:568
  98.4 0.6 shard_map.116
  (3 shorter events, 0.0 us)
Async XLA Ops:
  2.6 22.3 %collective-permute-start = (bf16[24,6016]{1,0:T(8,128)(2,1)}, bf16[24,6016]{1,0:T(8,128)(2,1)S(1)}, u32[]{:S(2)}, u32[]{:S(2)}) collective-permute-start(bf16[24,6016]{1,0:T(8,128)(2,1)} %get-tuple-element.24.x_ref), channel_id=1, source_target_pairs={{0,1},{1,2},{2,3},{3,4},{4,5},{5,6},{6,7},{7,8},{8,9},{9,10},{10,1... | collective-permute-start | bytes 866312 | tf_op jit(solution)/shard_map/ppermute | solution.py:539
  7.0 17.9 %collective-permute-start.1 = (bf16[24,6016]{1,0:T(8,128)(2,1)}, bf16[24,6016]{1,0:T(8,128)(2,1)S(1)}, u32[]{:S(2)}, u32[]{:S(2)}) collective-permute-start(bf16[24,6016]{1,0:T(8,128)(2,1)} %get-tuple-element.24.x_ref), channel_id=1, source_target_pairs={{1,0},{2,1},{3,2},{4,3},{5,4},{6,5},{7,6},{8,7},{9,8},{10,9},{11,1... | collective-permute-start | bytes 866312 | tf_op jit(solution)/shard_map/ppermute | solution.py:539
  8.3 16.6 %collective-permute-start.4 = (bf16[24,2432]{1,0:T(8,128)(2,1)}, bf16[24,2432]{1,0:T(8,128)(2,1)S(1)}, u32[]{:S(2)}, u32[]{:S(2)}) collective-permute-start(bf16[24,2432]{1,0:T(8,128)(2,1)} %get-tuple-element.29), channel_id=1, source_target_pairs={{0,2},{1,3},{2,4},{3,5},{4,6},{5,7},{6,8},{7,9},{8,10},{9,11},{10,... | collective-permute-start | bytes 350216 | tf_op jit(solution)/shard_map/ppermute | solution.py:539
  13.8 14.9 %collective-permute-start.2 = (bf16[24,2304]{1,0:T(8,128)(2,1)}, bf16[24,2304]{1,0:T(8,128)(2,1)S(1)}, u32[]{:S(2)}, u32[]{:S(2)}) collective-permute-start(bf16[24,2304]{1,0:T(8,128)(2,1)} %get-tuple-element.25.cot_ref), channel_id=1, source_target_pairs={{0,1},{1,2},{2,3},{3,4},{4,5},{5,6},{6,7},{7,8},{8,9},{9,10},{10,1... | collective-permute-start | bytes 331784 | tf_op jit(solution)/shard_map/ppermute | solution.py:539
  18.6 10.1 %collective-permute-start.3 = (bf16[24,2304]{1,0:T(8,128)(2,1)}, bf16[24,2304]{1,0:T(8,128)(2,1)S(1)}, u32[]{:S(2)}, u32[]{:S(2)}) collective-permute-start(bf16[24,2304]{1,0:T(8,128)(2,1)} %get-tuple-element.25.cot_ref), channel_id=1, source_target_pairs={{1,0},{2,1},{3,2},{4,3},{5,4},{6,5},{7,6},{8,7},{9,8},{10,9},{11,1... | collective-permute-start | bytes 331784 | tf_op jit(solution)/shard_map/ppermute | solution.py:539
  19.9 1.2 %copy-start = (bf16[3456,128]{1,0:T(8,128)(2,1)S(1)}, bf16[3456,128]{1,0:T(8,128)(2,1)}, u32[]{:S(2)}) copy-start(bf16[3456,128]{1,0:T(8,128)(2,1)} %wc_ref.1) | copy-start | bytes 2654212
  21.1 1.0 %copy-start.1 = (bf16[1728,128]{1,0:T(8,128)(2,1)S(1)}, bf16[1728,128]{1,0:T(8,128)(2,1)}, u32[]{:S(2)}) copy-start(bf16[1728,128]{1,0:T(8,128)(2,1)} %wd_ref.1) | copy-start | bytes 1327108
  22.1 1.0 copy-start.2
  23.1 0.9 copy-start.4
  24.9 3.8 %copy-start.3 = (bf16[128,512]{1,0:T(8,128)(2,1)S(1)}, bf16[128,512]{1,0:T(8,128)(2,1)}, u32[]{:S(2)}) copy-start(bf16[128,512]{1,0:T(8,128)(2,1)} %wu_ref.1) | copy-start | bytes 393220
  87.2 11.2 %all-to-all-start.3 = ((f32[8,12,128]{2,1,0:T(8,128)}), f32[8,12,128]{2,1,0:T(8,128)S(1)}, u32[]{:S(2)}, u32[]{:S(2)}) async-start(f32[8,12,128]{2,1,0:T(8,128)} %shard_map.115), calls=%async_computation.3 | async-start | bytes 131072 | tf_op jit(solution)/shard_map/all_to_all | solution.py:568

commit v6 on v5

--- a/solution.py
+++ b/solution.py
@@ -81,10 +81,17 @@
     return 4 * (x // 2) + 2 * (y // 2) + z // 2, 4 * (x % 2) + 2 * (y % 2) + z % 2
 
 
-def widen(wd_ref, wc_ref, x_ref, cot_ref, down_ref, coarse_ref, turned_ref, own_ref, cots_ref):
-    own_ref[...] = x_ref[...]
-    cots_ref[...] = cot_ref[...]
+def in_hbm(*arrays):
+    return [pltpu.with_memory_space_constraint(array, pltpu.HBM) for array in arrays]
+
+
+def widen(wd_hbm, wc_hbm, down_ref, coarse_ref, turned_ref, wd_ref, wc_ref, sems):
+    first = pltpu.make_async_copy(wd_hbm, wd_ref, sems.at[0])
+    second = pltpu.make_async_copy(wc_hbm, wc_ref, sems.at[1])
+    first.start()
+    second.start()
     down_ref[...] = jnp.zeros(down_ref.shape, BF)
+    first.wait()
     for ab in range(9):
         tap = [wd_ref[(3 * ab + e) * 64 : (3 * ab + e + 1) * 64, :] for e in range(3)]
         at = ab * 384
@@ -92,6 +99,7 @@
             down_ref[at + row : at + row + 64, 0:128] = tap[e]
         for row, e in ((64, 0), (128, 1), (192, 2)):
             down_ref[at + row : at + row + 64, 128:256] = tap[e]
+    second.wait()
     zero = jnp.zeros((128, 128), BF)
     for ab in range(9):
         for e in range(3):
@@ -108,16 +116,21 @@
             ref[ab * 512 : ab * 512 + 128, 128:256] = zero
 
 
-def widened(down_weight, coarse_weight, own, cot):
+def widened(down_weight, coarse_weight):
     vmem = pl.BlockSpec(memory_space=pltpu.VMEM)
-    shapes = ((9 * 384, 256), (9 * 512, 256), (9 * 512, 256), own.shape, cot.shape)
+    shapes = ((9 * 384, 256), (9 * 512, 256), (9 * 512, 256))
     return pl.pallas_call(
         widen,
         out_shape=tuple(jax.ShapeDtypeStruct(shape, BF) for shape in shapes),
-        in_specs=[vmem] * 4,
-        out_specs=(vmem,) * 5,
+        in_specs=[pl.BlockSpec(memory_space=pltpu.HBM)] * 2,
+        out_specs=(vmem,) * 3,
+        scratch_shapes=[
+            pltpu.VMEM(down_weight.shape, BF),
+            pltpu.VMEM(coarse_weight.shape, BF),
+            pltpu.SemaphoreType.DMA((2,)),
+        ],
         compiler_params=pltpu.CompilerParams(vmem_limit_bytes=12 * 2**20),
-    )(down_weight, coarse_weight, own, cot)
+    )(*in_hbm(down_weight, coarse_weight))
 
 
 def rows_of(refs, lane, width):
@@ -527,7 +540,8 @@
             for array in (features, cotangent, fine_nbr, parents, coarse_nbr)
         ]
         + [pltpu.SemaphoreType.DMA((5,))],
-    )(place, features, cotangent, fine_nbr, parents, coarse_nbr)
+        compiler_params=pltpu.CompilerParams(vmem_limit_bytes=8 * 2**20),
+    )(place, *in_hbm(features, cotangent, fine_nbr, parents, coarse_nbr))
 
 
 SPACE = ("x", "z")
@@ -599,7 +613,7 @@
     nxt = shift(own, -1)
     cot_prev = shift(cot, 1)
     cot_next = shift(cot, -1)
-    wide_down, wide, turned, own, cot = widened(down_weight, coarse_weight, own, cot)
+    wide_down, wide, turned = widened(down_weight, coarse_weight)
     kept = forward_pass(own, prev, nxt, far, wide_down, wide)
     return backward_pass(own, prev, nxt, cot, cot_prev, cot_next, turned, up_weight, *kept)
 

time: 99.6 us -> 95.8 us (0.962)
  local copies, waits for them, and re-layouts: 4.9 us -> 0.87 us
    unnamed x10 -> x2, local copies, waits for them, and re-layouts: 4.04 us -> 0.01 us
    pallas_call x1, Pallas kernels: 0.93 us -> 1.99 us  [widened(): pl.pallas_call(widen, out_shape=tuple((jax.ShapeDtypeStruct(shape, BF) fo...]
  transfers between devices with their start and end apart: 6 -> 6, of which waited for: 1 -> 1; matrix products, arithmetic and copies ran while one was open for 1% -> 1% of each run, Pallas kernels for 5% -> 6%
where the time goes in v6:
time: 95.8 us; the launch traced here: 95.3 us
  blocking collectives  51.8 us (54%)
  starting transfers between devices  23.6 us (25%)
  Pallas kernels  13.8 us (14%)
  waiting for transfers between devices  4.07 us (4%)
    all_to_all x1, blocking collectives, spread_sum(): held = lax.all_to_all(held, ('y', 'x'), 0, 0)  26.5 us
    all_to_all x1, blocking collectives, spread_sum(): held = lax.all_to_all(held, 'z', 0, 0)  18.5 us
    ppermute x5, starting transfers between devices, shift(): return lax.ppermute(block, SPACE, route)  17.2 us
    all_to_all x1, blocking collectives, spread_sum(): held = lax.all_to_all(sums, 'core', 0, 0)  6.83 us
    all_to_all x1, starting transfers between devices, spread_sum(): held = lax.all_to_all(held, ('y', 'core'), 0, 0)  6.32 us
    pallas_call x1, Pallas kernels, backward_pass(): pl.pallas_call(backward, out_shape=(jax.ShapeDtypeStruct((FB, XL), BF), j...  5.45 us
    all_to_all x1, waiting for transfers between devices, spread_sum(): held = lax.all_to_all(held, ('y', 'core'), 0, 0)  4.06 us
    pallas_call x1, Pallas kernels, forward_pass(): pl.pallas_call(forward, out_shape=tuple((jax.ShapeDtypeStruct(*one) for o...  3.78 us
  transfers between devices with their start and end apart: 6, of which 1 were waited for; matrix products, arithmetic and copies ran while one was open for 1% of the time, Pallas kernels for 6%

profile of v6, /device:TPU:1, one launch (start us, length us, event | category | flops | bytes accessed | tf_op | source)
XLA Modules:
  0.0 95.3 jit_solution(18397146141519521853)
XLA Ops:
  0.6 1.3 %shard_map.111 = (bf16[24,6016]{1,0:T(8,128)(2,1)S(1)}, bf16[24,2304]{1,0:T(8,128)(2,1)S(1)}, bf16[24,2432]{1,0:T(8,128)(2,1)S(1)}) custom-call(s32[1]{0:T(128)} %bitcast.place_ref, bf16[24,4,4,256]{3,2,1,0:T(4,128)(2,1)} %bitcast.10, bf16[24,4,4,256]{3,2,1,0:T(4,128)(2,1)} %bitcast.11, s32[7,1,24]{2,1,0:T(1,128)} %bitcast.12, s32[1,24]{1,0:T(1,128)} %refs_3_.1, ...), custom_call_target="tpu_custom_call" | custom-call | tf_op jit(solution)/shard_map/pallas_call | solution.py:528
  1.9 4.4 %collective-permute-start = (bf16[24,6016]{1,0:T(8,128)(2,1)S(1)}, bf16[24,6016]{1,0:T(8,128)(2,1)S(1)}, u32[]{:S(2)}, u32[]{:S(2)}) collective-permute-start(bf16[24,6016]{1,0:T(8,128)(2,1)S(1)} %get-tuple-element.22.own_ref), channel_id=1, source_target_pairs={{0,1},{1,2},{2,3},{3,4},{4,5},{5,6},{6,7},{7,8},{8,9},{9,10},{10,1... | collective-permute-start | bytes 866312 | tf_op jit(solution)/shard_map/ppermute | solution.py:553
  6.3 1.3 %collective-permute-start.1 = (bf16[24,6016]{1,0:T(8,128)(2,1)S(1)}, bf16[24,6016]{1,0:T(8,128)(2,1)S(1)}, u32[]{:S(2)}, u32[]{:S(2)}) collective-permute-start(bf16[24,6016]{1,0:T(8,128)(2,1)S(1)} %get-tuple-element.22.own_ref), channel_id=1, source_target_pairs={{1,0},{2,1},{3,2},{4,3},{5,4},{6,5},{7,6},{8,7},{9,8},{10,9},{11,1... | collective-permute-start | bytes 866312 | tf_op jit(solution)/shard_map/ppermute | solution.py:553
  7.6 5.5 %collective-permute-start.4 = (bf16[24,2432]{1,0:T(8,128)(2,1)S(1)}, bf16[24,2432]{1,0:T(8,128)(2,1)S(1)}, u32[]{:S(2)}, u32[]{:S(2)}) collective-permute-start(bf16[24,2432]{1,0:T(8,128)(2,1)S(1)} %get-tuple-element.25), channel_id=1, source_target_pairs={{0,2},{1,3},{2,4},{3,5},{4,6},{5,7},{6,8},{7,9},{8,10},{9,11},{10,... | collective-permute-start | bytes 350216 | tf_op jit(solution)/shard_map/ppermute | solution.py:553
  13.2 4.8 %collective-permute-start.2 = (bf16[24,2304]{1,0:T(8,128)(2,1)S(1)}, bf16[24,2304]{1,0:T(8,128)(2,1)S(1)}, u32[]{:S(2)}, u32[]{:S(2)}) collective-permute-start(bf16[24,2304]{1,0:T(8,128)(2,1)S(1)} %get-tuple-element.23.cot_own_ref), channel_id=1, source_target_pairs={{0,1},{1,2},{2,3},{3,4},{4,5},{5,6},{6,7},{7,8},{8,9},{9,10},{10,1... | collective-permute-start | bytes 331784 | tf_op jit(solution)/shard_map/ppermute | solution.py:553
  17.9 1.3 %collective-permute-start.3 = (bf16[24,2304]{1,0:T(8,128)(2,1)S(1)}, bf16[24,2304]{1,0:T(8,128)(2,1)S(1)}, u32[]{:S(2)}, u32[]{:S(2)}) collective-permute-start(bf16[24,2304]{1,0:T(8,128)(2,1)S(1)} %get-tuple-element.23.cot_own_ref), channel_id=1, source_target_pairs={{1,0},{2,1},{3,2},{4,3},{5,4},{6,5},{7,6},{8,7},{9,8},{10,9},{11,1... | collective-permute-start | bytes 331784 | tf_op jit(solution)/shard_map/ppermute | solution.py:553
  19.2 2.0 %shard_map.112 = (bf16[3456,256]{1,0:T(8,128)(2,1)S(1)}, bf16[4608,256]{1,0:T(8,128)(2,1)S(1)}, bf16[4608,256]{1,0:T(8,128)(2,1)S(1)}) custom-call(bf16[1728,128]{1,0:T(8,128)(2,1)} %wd_hbm.1, bf16[3456,128]{1,0:T(8,128)(2,1)} %wc_hbm.1), custom_call_target="tpu_custom_call" | custom-call | tf_op jit(solution)/shard_map/pallas_call | solution.py:122
  21.2 0.0 collective-permute-done.4.far_ref
  21.2 0.0 collective-permute-done.prev_ref
  21.2 0.0 collective-permute-done.1.next_ref
  21.2 0.0 copy-start
  21.3 3.8 %shard_map.113 = (bf16[25,32,384]{2,1,0:T(8,128)(2,1)S(1)}, f32[80,128]{1,0:T(8,128)S(1)}, bf16[4,448,128]{2,1,0:T(8,128)(2,1)S(1)}, bf16[6,6,3,2,16,128]{5,4,3,...) custom-call(bf16[24,6016]{1,0:T(8,128)(2,1)S(1)} %get-tuple-element.22.own, ...), custom_call_target="tpu_custom_call" | custom-call | tf_op jit(solution)/shard_map/pallas_call | solution.py:440
  25.0 0.0 collective-permute-done.2.cot_prev_ref
  25.0 0.0 collective-permute-done.3.cot_next_ref
  25.1 0.0 copy-done
  25.1 5.5 %shard_map.114 = (bf16[24,4096]{1,0:T(8,128)(2,1)S(1)}, bf16[2,4,64,1536]{3,2,1,0:T(8,128)(2,1)S(1)}) custom-call(bf16[24,6016]{1,0:T(8,128)(2,1)S(1)} %get-tuple-element.22.own_ref, bf16[24,6016]{1,0:T(8,128)(2,1)S(1)} %collective-permute-done.prev_ref, bf16[24,6016]{1,0:T(8,128)(2,1)S(1)} %collective-permute-done.1.next_ref, ...), custom_call_target="tpu_custom_call" | custom-call | tf_op jit(solution)/shard_map/pallas_call | solution.py:457
  30.5 6.8 %all_to_all.20 = bf16[2,4,64,1536]{3,2,1,0:T(8,128)(2,1)S(1)} all-to-all(bf16[2,4,64,1536]{3,2,1,0:T(8,128)(2,1)S(1)} %get-tuple-element.36), channel_id=1, replica_groups=mesh['y'=4,'core'=2,'x'=4,'z'=16] {'core'}, dimensions={0} | all-to-all | bytes 3145728 | tf_op jit(solution)/shard_map/all_to_all | solution.py:570
  37.4 0.3 reduce_sum.24
  37.7 26.5 %all_to_all.21 = bf16[16,16,1536]{2,1,0:T(8,128)(2,1)S(1)} all-to-all(bf16[16,16,1536]{2,1,0:T(8,128)(2,1)S(1)} %bitcast.9), channel_id=1, replica_groups=mesh['y'=4,'core'=2,'x'=4,'z'=16] {'y','x'}, dimensions={0} | all-to-all | bytes 1572864 | tf_op jit(solution)/shard_map/all_to_all | solution.py:573
  64.2 0.1 reduce_sum.25
  64.3 0.1 reshape.32
  64.3 18.5 %all_to_all.22.in_ref = bf16[16,12,128]{2,1,0:T(8,128)(2,1)S(1)} all-to-all(bf16[16,12,128]{2,1,0:T(8,128)(2,1)S(1)} %reshape.32), channel_id=1, replica_groups=mesh['y'=4,'core'=2,'x'=4,'z'=16] {'z'}, dimensions={0} | all-to-all | bytes 98304 | tf_op jit(solution)/shard_map/all_to_all | solution.py:576
  82.9 0.6 shard_map.115
  83.5 6.3 %all-to-all-start.3 = ((f32[8,12,128]{2,1,0:T(8,128)}), f32[8,12,128]{2,1,0:T(8,128)S(1)}, u32[]{:S(2)}, u32[]{:S(2)}) async-start(f32[8,12,128]{2,1,0:T(8,128)} %shard_map.115), calls=%async_computation.3 | async-start | bytes 131072 | tf_op jit(solution)/shard_map/all_to_all | solution.py:582
  89.8 0.8 reshape.30
  90.6 4.1 %all-to-all-done.3.in_ref = f32[8,12,128]{2,1,0:T(8,128)S(1)} async-done(((f32[8,12,128]{2,1,0:T(8,128)}), f32[8,12,128]{2,1,0:T(8,128)S(1)}, u32[]{:S(2)}, u32[]{:S(2)}) %all-to-all-start.3) | async-done | bytes 49184 | tf_op jit(solution)/shard_map/all_to_all | solution.py:582
  94.7 0.6 shard_map.116
Async XLA Ops:
  1.9 19.3 %collective-permute-start = (bf16[24,6016]{1,0:T(8,128)(2,1)S(1)}, bf16[24,6016]{1,0:T(8,128)(2,1)S(1)}, u32[]{:S(2)}, u32[]{:S(2)}) collective-permute-start(bf16[24,6016]{1,0:T(8,128)(2,1)S(1)} %get-tuple-element.22.own_ref), channel_id=1, source_target_pairs={{0,1},{1,2},{2,3},{3,4},{4,5},{5,6},{6,7},{7,8},{8,9},{9,10},{10,1... | collective-permute-start | bytes 866312 | tf_op jit(solution)/shard_map/ppermute | solution.py:553
  6.3 14.9 %collective-permute-start.1 = (bf16[24,6016]{1,0:T(8,128)(2,1)S(1)}, bf16[24,6016]{1,0:T(8,128)(2,1)S(1)}, u32[]{:S(2)}, u32[]{:S(2)}) collective-permute-start(bf16[24,6016]{1,0:T(8,128)(2,1)S(1)} %get-tuple-element.22.own_ref), channel_id=1, source_target_pairs={{1,0},{2,1},{3,2},{4,3},{5,4},{6,5},{7,6},{8,7},{9,8},{10,9},{11,1... | collective-permute-start | bytes 866312 | tf_op jit(solution)/shard_map/ppermute | solution.py:553
  7.6 13.6 %collective-permute-start.4 = (bf16[24,2432]{1,0:T(8,128)(2,1)S(1)}, bf16[24,2432]{1,0:T(8,128)(2,1)S(1)}, u32[]{:S(2)}, u32[]{:S(2)}) collective-permute-start(bf16[24,2432]{1,0:T(8,128)(2,1)S(1)} %get-tuple-element.25), channel_id=1, source_target_pairs={{0,2},{1,3},{2,4},{3,5},{4,6},{5,7},{6,8},{7,9},{8,10},{9,11},{10,... | collective-permute-start | bytes 350216 | tf_op jit(solution)/shard_map/ppermute | solution.py:553
  13.2 11.9 %collective-permute-start.2 = (bf16[24,2304]{1,0:T(8,128)(2,1)S(1)}, bf16[24,2304]{1,0:T(8,128)(2,1)S(1)}, u32[]{:S(2)}, u32[]{:S(2)}) collective-permute-start(bf16[24,2304]{1,0:T(8,128)(2,1)S(1)} %get-tuple-element.23.cot_own_ref), channel_id=1, source_target_pairs={{0,1},{1,2},{2,3},{3,4},{4,5},{5,6},{6,7},{7,8},{8,9},{9,10},{10,1... | collective-permute-start | bytes 331784 | tf_op jit(solution)/shard_map/ppermute | solution.py:553
  17.9 7.1 %collective-permute-start.3 = (bf16[24,2304]{1,0:T(8,128)(2,1)S(1)}, bf16[24,2304]{1,0:T(8,128)(2,1)S(1)}, u32[]{:S(2)}, u32[]{:S(2)}) collective-permute-start(bf16[24,2304]{1,0:T(8,128)(2,1)S(1)} %get-tuple-element.23.cot_own_ref), channel_id=1, source_target_pairs={{1,0},{2,1},{3,2},{4,3},{5,4},{6,5},{7,6},{8,7},{9,8},{10,9},{11,1... | collective-permute-start | bytes 331784 | tf_op jit(solution)/shard_map/ppermute | solution.py:553
  21.2 3.8 %copy-start = (bf16[128,512]{1,0:T(8,128)(2,1)S(1)}, bf16[128,512]{1,0:T(8,128)(2,1)}, u32[]{:S(2)}) copy-start(bf16[128,512]{1,0:T(8,128)(2,1)} %wu_ref.1) | copy-start | bytes 393220
  83.5 11.2 %all-to-all-start.3 = ((f32[8,12,128]{2,1,0:T(8,128)}), f32[8,12,128]{2,1,0:T(8,128)S(1)}, u32[]{:S(2)}, u32[]{:S(2)}) async-start(f32[8,12,128]{2,1,0:T(8,128)} %shard_map.115), calls=%async_computation.3 | async-start | bytes 131072 | tf_op jit(solution)/shard_map/all_to_all | solution.py:582

commit v7 on v6

--- a/solution.py
+++ b/solution.py
@@ -14,8 +14,10 @@
 ROWS = 80
 CR = 16
 XL = 4096
-EARLY = 7 * 256
-IDX = XL + EARLY
+IDX = XL
+COT = XL + 128
+FULL = COT + XL
+EARLY = COT + 7 * 256
 VMEM_A, VMEM_B = 20 * 2**20, 24 * 2**20
 TILES = 96
 
@@ -302,9 +304,7 @@
     own_ref,
     prev_ref,
     next_ref,
-    cot_own_ref,
-    cot_prev_ref,
-    cot_next_ref,
+    late_ref,
     wt_ref,
     wu_ref,
     mine_ref,
@@ -331,9 +331,12 @@
 
 
     def cot_rows(lane, width):
+        lane += COT
         if lane < EARLY:
-            return rows(XL + lane, width)
-        return rows_of((cot_prev_ref, cot_own_ref, cot_next_ref), lane - EARLY, width)
+            return rows(lane, width)
+        parts = [late_ref[:, lane - EARLY : lane - EARLY + width].astype(F32)]
+        parts += [ref[:, lane : lane + width].astype(F32) for ref in (own_ref, next_ref)]
+        return jnp.concatenate(parts + [zeros8((ROWS - 3 * FB, width))], axis=0)
 
     up_f = up_ref[...]
     up = up_f.astype(BF)
@@ -478,8 +481,8 @@
 
 
 def pack(place_ref, *refs):
-    given, held, sems = refs[:5], refs[8:13], refs[13]
-    own_ref, cots_ref, far_ref = refs[5:8]
+    given, held, sems = refs[:5], refs[9:14], refs[14]
+    own_ref, early_ref, late_ref, far_ref = refs[5:9]
     copies = [
         pltpu.make_async_copy(source, target, sems.at[n])
         for n, (source, target) in enumerate(zip(given, held))
@@ -492,8 +495,8 @@
     place = place_ref[0]
     own_ref[:, 0:XL] = x_ref[...].reshape(FB, XL)
     cot = cot_ref[...].reshape(FB, XL)
-    own_ref[:, XL:IDX] = cot[:, 0:EARLY]
-    cots_ref[...] = cot[:, EARLY:XL]
+    own_ref[:, COT:FULL] = cot
+    late_ref[...] = cot[:, EARLY - COT : XL]
     fine = jnp.concatenate([fine_ref[m] for m in range(7)], axis=0)
     fine = jnp.where(fine < 0, 0, fine - (FB * (place - 1) - 1)).astype(F32)
     coarse = jnp.concatenate([coarse_ref[c] for c in range(CB)], axis=0)
@@ -506,7 +509,8 @@
     )
     lists = dot(jnp.where(unit, 1.0, 0.0).astype(BF), lists, ((1,), (1,)))
     filler = jnp.zeros((FB, 128 - 34), F32)
-    own_ref[:, IDX : IDX + 128] = jnp.concatenate([lists, coarse, filler], axis=1).astype(BF)
+    own_ref[:, IDX:COT] = jnp.concatenate([lists, coarse, filler], axis=1).astype(BF)
+    early_ref[...] = own_ref[:, 0:EARLY]
     at = 0
     last = []
     for start, width in upper_pieces():
@@ -528,13 +532,14 @@
     return pl.pallas_call(
         pack,
         out_shape=(
-            jax.ShapeDtypeStruct((FB, IDX + 128), BF),
-            jax.ShapeDtypeStruct((FB, XL - EARLY), BF),
+            jax.ShapeDtypeStruct((FB, FULL), BF),
+            jax.ShapeDtypeStruct((FB, EARLY), BF),
+            jax.ShapeDtypeStruct((FB, FULL - EARLY), BF),
             jax.ShapeDtypeStruct((FB, SENT), BF),
         ),
         in_specs=[pl.BlockSpec(memory_space=pltpu.SMEM)]
         + [pl.BlockSpec(memory_space=pltpu.HBM)] * 5,
-        out_specs=(vmem,) * 3,
+        out_specs=(vmem,) * 4,
         scratch_shapes=[
             pltpu.VMEM(array.shape, array.dtype)
             for array in (features, cotangent, fine_nbr, parents, coarse_nbr)
@@ -600,7 +605,7 @@
     coarse_neighbours,
 ):
     place = lax.axis_index(SPACE).astype(jnp.int32).reshape(1)
-    own, cot, upper = packed(
+    own, early, late, upper = packed(
         place,
         fine_features[0],
         cotangent[0],
@@ -608,14 +613,13 @@
         parent_slots,
         coarse_neighbours[0].reshape(CB, 1, 26),
     )
-    prev = shift(own, 1)
+    prev = shift(early, 1)
     far = shift(upper, 2)
     nxt = shift(own, -1)
-    cot_prev = shift(cot, 1)
-    cot_next = shift(cot, -1)
+    late = shift(late, 1)
     wide_down, wide, turned = widened(down_weight, coarse_weight)
     kept = forward_pass(own, prev, nxt, far, wide_down, wide)
-    return backward_pass(own, prev, nxt, cot, cot_prev, cot_next, turned, up_weight, *kept)
+    return backward_pass(own, prev, nxt, late, turned, up_weight, *kept)
 
 
 def body(fine_features, *rest):

time: 95.8 us -> 97.3 us (1.016)
  blocking collectives: 51.8 us -> 54.7 us
  starting transfers between devices: 23.6 us -> 22.3 us
    all_to_all x1, blocking collectives: 26.5 us -> 30.4 us  [spread_sum(): held = lax.all_to_all(held, ('y', 'x'), 0, 0)]
    ppermute x5 -> x4, starting transfers between devices: 17.2 us -> 16 us  [shift(): return lax.ppermute(block, SPACE, route)]
  transfers between devices with their start and end apart: 6 -> 5, of which waited for: 1 -> 1; matrix products, arithmetic and copies ran while one was open for 1% -> 1% of each run, Pallas kernels for 6% -> 6%
where the time goes in v7:
time: 97.3 us; the launch traced here: 96.9 us
  blocking collectives  54.7 us (56%)
  starting transfers between devices  22.3 us (23%)
  Pallas kernels  13.7 us (14%)
  waiting for transfers between devices  4.07 us (4%)
    all_to_all x1, blocking collectives, spread_sum(): held = lax.all_to_all(held, ('y', 'x'), 0, 0)  30.4 us
    all_to_all x1, blocking collectives, spread_sum(): held = lax.all_to_all(held, 'z', 0, 0)  18.1 us
    ppermute x4, starting transfers between devices, shift(): return lax.ppermute(block, SPACE, route)  16 us
    all_to_all x1, starting transfers between devices, spread_sum(): held = lax.all_to_all(held, ('y', 'core'), 0, 0)  6.32 us
    all_to_all x1, blocking collectives, spread_sum(): held = lax.all_to_all(sums, 'core', 0, 0)  6.23 us
    pallas_call x1, Pallas kernels, backward_pass(): pl.pallas_call(backward, out_shape=(jax.ShapeDtypeStruct((FB, XL), BF), j...  5.38 us
    all_to_all x1, waiting for transfers between devices, spread_sum(): held = lax.all_to_all(held, ('y', 'core'), 0, 0)  4.06 us
    pallas_call x1, Pallas kernels, forward_pass(): pl.pallas_call(forward, out_shape=tuple((jax.ShapeDtypeStruct(*one) for o...  3.83 us
  transfers between devices with their start and end apart: 5, of which 1 were waited for; matrix products, arithmetic and copies ran while one was open for 1% of the time, Pallas kernels for 6%

profile of v7, /device:TPU:1, one launch (start us, length us, event | category | flops | bytes accessed | tf_op | source)
XLA Modules:
  0.0 96.9 jit_solution(3716478079004578329)
XLA Ops:
  0.6 1.3 %shard_map.111 = (bf16[24,8320]{1,0:T(8,128)(2,1)S(1)}, bf16[24,6016]{1,0:T(8,128)(2,1)S(1)}, bf16[24,2304]{1,0:T(8,128)(2,1)S(1)}, bf16[24,2432]{1,0:T(8,128)(2,1)S(1)}) custom-call(s32[1]{0:T(128)} %bitcast.place_ref, bf16[24,4,4,256]{3,2,1,0:T(4,128)(2,1)} %bitcast.10, bf16[24,4,4,256]{3,2,1,0:T(4,128)(2,1)} %bitcast.11, s32[7,1,24]{2,1,0:T(1,128)} %bitcast.12, ...), custom_call_target="tpu_custom_call" | custom-call | tf_op jit(solution)/shard_map/pallas_call | solution.py:532
  1.9 1.3 %collective-permute-start.1 = (bf16[24,8320]{1,0:T(8,128)(2,1)S(1)}, bf16[24,8320]{1,0:T(8,128)(2,1)S(1)}, u32[]{:S(2)}, u32[]{:S(2)}) collective-permute-start(bf16[24,8320]{1,0:T(8,128)(2,1)S(1)} %get-tuple-element.23.own_ref), channel_id=1, source_target_pairs={{1,0},{2,1},{3,2},{4,3},{5,4},{6,5},{7,6},{8,7},{9,8},{10,9},{11,1... | collective-permute-start | bytes 1198088 | tf_op jit(solution)/shard_map/ppermute | solution.py:558
  3.2 5.0 %collective-permute-start = (bf16[24,6016]{1,0:T(8,128)(2,1)S(1)}, bf16[24,6016]{1,0:T(8,128)(2,1)S(1)}, u32[]{:S(2)}, u32[]{:S(2)}) collective-permute-start(bf16[24,6016]{1,0:T(8,128)(2,1)S(1)} %get-tuple-element.24), channel_id=1, source_target_pairs={{0,1},{1,2},{2,3},{3,4},{4,5},{5,6},{6,7},{7,8},{8,9},{9,10},{10,1... | collective-permute-start | bytes 866312 | tf_op jit(solution)/shard_map/ppermute | solution.py:558
  8.2 4.9 %collective-permute-start.3 = (bf16[24,2432]{1,0:T(8,128)(2,1)S(1)}, bf16[24,2432]{1,0:T(8,128)(2,1)S(1)}, u32[]{:S(2)}, u32[]{:S(2)}) collective-permute-start(bf16[24,2432]{1,0:T(8,128)(2,1)S(1)} %get-tuple-element.27), channel_id=1, source_target_pairs={{0,2},{1,3},{2,4},{3,5},{4,6},{5,7},{6,8},{7,9},{8,10},{9,11},{10,... | collective-permute-start | bytes 350216 | tf_op jit(solution)/shard_map/ppermute | solution.py:558
  13.1 4.8 %collective-permute-start.2 = (bf16[24,2304]{1,0:T(8,128)(2,1)S(1)}, bf16[24,2304]{1,0:T(8,128)(2,1)S(1)}, u32[]{:S(2)}, u32[]{:S(2)}) collective-permute-start(bf16[24,2304]{1,0:T(8,128)(2,1)S(1)} %get-tuple-element.25), channel_id=1, source_target_pairs={{0,1},{1,2},{2,3},{3,4},{4,5},{5,6},{6,7},{7,8},{8,9},{9,10},{10,1... | collective-permute-start | bytes 331784 | tf_op jit(solution)/shard_map/ppermute | solution.py:558
  17.9 2.0 %shard_map.112 = (bf16[3456,256]{1,0:T(8,128)(2,1)S(1)}, bf16[4608,256]{1,0:T(8,128)(2,1)S(1)}, bf16[4608,256]{1,0:T(8,128)(2,1)S(1)}) custom-call(bf16[1728,128]{1,0:T(8,128)(2,1)} %wd_hbm.1, bf16[3456,128]{1,0:T(8,128)(2,1)} %wc_hbm.1), custom_call_target="tpu_custom_call" | custom-call | tf_op jit(solution)/shard_map/pallas_call | solution.py:124
  19.9 0.0 collective-permute-done.3.far_ref
  19.9 0.0 collective-permute-done.prev_ref
  19.9 0.0 collective-permute-done.1.next_ref
  19.9 0.0 copy-start
  19.9 3.8 %shard_map.113 = (bf16[25,32,384]{2,1,0:T(8,128)(2,1)S(1)}, f32[80,128]{1,0:T(8,128)S(1)}, bf16[4,448,128]{2,1,0:T(8,128)(2,1)S(1)}, bf16[6,6,3,2,16,128]{5,4,3,...) custom-call(bf16[24,8320]{1,0:T(8,128)(2,1)S(1)} %get-tuple-element.23.own, ...), custom_call_target="tpu_custom_call" | custom-call | tf_op jit(solution)/shard_map/pallas_call | solution.py:443
  23.8 0.0 collective-permute-done.2.late_ref
  23.8 0.0 copy-done
  23.8 5.4 %shard_map.114 = (bf16[24,4096]{1,0:T(8,128)(2,1)S(1)}, bf16[2,4,64,1536]{3,2,1,0:T(8,128)(2,1)S(1)}) custom-call(bf16[24,8320]{1,0:T(8,128)(2,1)S(1)} %get-tuple-element.23.own_ref, bf16[24,6016]{1,0:T(8,128)(2,1)S(1)} %collective-permute-done.prev_ref, bf16[24,8320]{1,0:T(8,128)(2,1)S(1)} %collective-permute-done.1.next_ref, ...), custom_call_target="tpu_custom_call" | custom-call | tf_op jit(solution)/shard_map/pallas_call | solution.py:460
  29.2 6.2 %all_to_all.20 = bf16[2,4,64,1536]{3,2,1,0:T(8,128)(2,1)S(1)} all-to-all(bf16[2,4,64,1536]{3,2,1,0:T(8,128)(2,1)S(1)} %get-tuple-element.38), channel_id=1, replica_groups=mesh['y'=4,'core'=2,'x'=4,'z'=16] {'core'}, dimensions={0} | all-to-all | bytes 3145728 | tf_op jit(solution)/shard_map/all_to_all | solution.py:575
  35.4 0.3 reduce_sum.24
  35.8 30.4 %all_to_all.21 = bf16[16,16,1536]{2,1,0:T(8,128)(2,1)S(1)} all-to-all(bf16[16,16,1536]{2,1,0:T(8,128)(2,1)S(1)} %bitcast.9), channel_id=1, replica_groups=mesh['y'=4,'core'=2,'x'=4,'z'=16] {'y','x'}, dimensions={0} | all-to-all | bytes 1572864 | tf_op jit(solution)/shard_map/all_to_all | solution.py:578
  66.2 0.1 reduce_sum.25
  66.3 0.1 reshape.32
  66.4 18.1 %all_to_all.22.in_ref = bf16[16,12,128]{2,1,0:T(8,128)(2,1)S(1)} all-to-all(bf16[16,12,128]{2,1,0:T(8,128)(2,1)S(1)} %reshape.32), channel_id=1, replica_groups=mesh['y'=4,'core'=2,'x'=4,'z'=16] {'z'}, dimensions={0} | all-to-all | bytes 98304 | tf_op jit(solution)/shard_map/all_to_all | solution.py:581
  84.4 0.7 shard_map.115
  85.1 6.3 %all-to-all-start.3 = ((f32[8,12,128]{2,1,0:T(8,128)}), f32[8,12,128]{2,1,0:T(8,128)S(1)}, u32[]{:S(2)}, u32[]{:S(2)}) async-start(f32[8,12,128]{2,1,0:T(8,128)} %shard_map.115), calls=%async_computation.3 | async-start | bytes 131072 | tf_op jit(solution)/shard_map/all_to_all | solution.py:587
  91.4 0.8 reshape.30
  92.2 4.1 %all-to-all-done.3.in_ref = f32[8,12,128]{2,1,0:T(8,128)S(1)} async-done(((f32[8,12,128]{2,1,0:T(8,128)}), f32[8,12,128]{2,1,0:T(8,128)S(1)}, u32[]{:S(2)}, u32[]{:S(2)}) %all-to-all-start.3) | async-done | bytes 49184 | tf_op jit(solution)/shard_map/all_to_all | solution.py:587
  96.3 0.6 shard_map.116
Async XLA Ops:
  1.9 18.0 %collective-permute-start.1 = (bf16[24,8320]{1,0:T(8,128)(2,1)S(1)}, bf16[24,8320]{1,0:T(8,128)(2,1)S(1)}, u32[]{:S(2)}, u32[]{:S(2)}) collective-permute-start(bf16[24,8320]{1,0:T(8,128)(2,1)S(1)} %get-tuple-element.23.own_ref), channel_id=1, source_target_pairs={{1,0},{2,1},{3,2},{4,3},{5,4},{6,5},{7,6},{8,7},{9,8},{10,9},{11,1... | collective-permute-start | bytes 1198088 | tf_op jit(solution)/shard_map/ppermute | solution.py:558
  3.2 16.7 %collective-permute-start = (bf16[24,6016]{1,0:T(8,128)(2,1)S(1)}, bf16[24,6016]{1,0:T(8,128)(2,1)S(1)}, u32[]{:S(2)}, u32[]{:S(2)}) collective-permute-start(bf16[24,6016]{1,0:T(8,128)(2,1)S(1)} %get-tuple-element.24), channel_id=1, source_target_pairs={{0,1},{1,2},{2,3},{3,4},{4,5},{5,6},{6,7},{7,8},{8,9},{9,10},{10,1... | collective-permute-start | bytes 866312 | tf_op jit(solution)/shard_map/ppermute | solution.py:558
  8.2 11.7 %collective-permute-start.3 = (bf16[24,2432]{1,0:T(8,128)(2,1)S(1)}, bf16[24,2432]{1,0:T(8,128)(2,1)S(1)}, u32[]{:S(2)}, u32[]{:S(2)}) collective-permute-start(bf16[24,2432]{1,0:T(8,128)(2,1)S(1)} %get-tuple-element.27), channel_id=1, source_target_pairs={{0,2},{1,3},{2,4},{3,5},{4,6},{5,7},{6,8},{7,9},{8,10},{9,11},{10,... | collective-permute-start | bytes 350216 | tf_op jit(solution)/shard_map/ppermute | solution.py:558
  13.1 10.6 %collective-permute-start.2 = (bf16[24,2304]{1,0:T(8,128)(2,1)S(1)}, bf16[24,2304]{1,0:T(8,128)(2,1)S(1)}, u32[]{:S(2)}, u32[]{:S(2)}) collective-permute-start(bf16[24,2304]{1,0:T(8,128)(2,1)S(1)} %get-tuple-element.25), channel_id=1, source_target_pairs={{0,1},{1,2},{2,3},{3,4},{4,5},{5,6},{6,7},{7,8},{8,9},{9,10},{10,1... | collective-permute-start | bytes 331784 | tf_op jit(solution)/shard_map/ppermute | solution.py:558
  19.9 3.9 %copy-start = (bf16[128,512]{1,0:T(8,128)(2,1)S(1)}, bf16[128,512]{1,0:T(8,128)(2,1)}, u32[]{:S(2)}) copy-start(bf16[128,512]{1,0:T(8,128)(2,1)} %wu_ref.1) | copy-start | bytes 393220
  85.1 11.2 %all-to-all-start.3 = ((f32[8,12,128]{2,1,0:T(8,128)}), f32[8,12,128]{2,1,0:T(8,128)S(1)}, u32[]{:S(2)}, u32[]{:S(2)}) async-start(f32[8,12,128]{2,1,0:T(8,128)} %shard_map.115), calls=%async_computation.3 | async-start | bytes 131072 | tf_op jit(solution)/shard_map/all_to_all | solution.py:587

commit v8 on v5

--- a/solution.py
+++ b/solution.py
@@ -81,9 +81,11 @@
     return 4 * (x // 2) + 2 * (y // 2) + z // 2, 4 * (x % 2) + 2 * (y % 2) + z % 2
 
 
-def widen(wd_ref, wc_ref, x_ref, cot_ref, down_ref, coarse_ref, turned_ref, own_ref, cots_ref):
-    own_ref[...] = x_ref[...]
-    cots_ref[...] = cot_ref[...]
+def in_hbm(*arrays):
+    return [pltpu.with_memory_space_constraint(array, pltpu.HBM) for array in arrays]
+
+
+def widen(wd_ref, wc_ref, down_ref, coarse_ref, turned_ref):
     down_ref[...] = jnp.zeros(down_ref.shape, BF)
     for ab in range(9):
         tap = [wd_ref[(3 * ab + e) * 64 : (3 * ab + e + 1) * 64, :] for e in range(3)]
@@ -108,18 +110,6 @@
             ref[ab * 512 : ab * 512 + 128, 128:256] = zero
 
 
-def widened(down_weight, coarse_weight, own, cot):
-    vmem = pl.BlockSpec(memory_space=pltpu.VMEM)
-    shapes = ((9 * 384, 256), (9 * 512, 256), (9 * 512, 256), own.shape, cot.shape)
-    return pl.pallas_call(
-        widen,
-        out_shape=tuple(jax.ShapeDtypeStruct(shape, BF) for shape in shapes),
-        in_specs=[vmem] * 4,
-        out_specs=(vmem,) * 5,
-        compiler_params=pltpu.CompilerParams(vmem_limit_bytes=12 * 2**20),
-    )(down_weight, coarse_weight, own, cot)
-
-
 def rows_of(refs, lane, width):
     parts = [ref[:, lane : lane + width].astype(F32) for ref in refs]
     return jnp.concatenate(parts + [jnp.zeros((ROWS - 3 * FB, width), F32)], axis=0)
@@ -177,8 +167,9 @@
     prev_ref,
     next_ref,
     far_ref,
-    wd_ref,
-    wc_ref,
+    wd_hbm,
+    wc_hbm,
+    wt_ref,
     mine_ref,
     up_ref,
     nl_ref,
@@ -190,7 +181,18 @@
     pad_ref,
     hid_ref,
     cin_ref,
+    raw_down_ref,
+    raw_coarse_ref,
+    wd_ref,
+    wc_ref,
+    sems,
 ):
+    copies = [
+        pltpu.make_async_copy(wd_hbm, raw_down_ref, sems.at[0]),
+        pltpu.make_async_copy(wc_hbm, raw_coarse_ref, sems.at[1]),
+    ]
+    for copy in copies:
+        copy.start()
     zeros8 = functools.partial(jnp.zeros, dtype=F32)
     rows = functools.partial(rows_of, (prev_ref, own_ref, next_ref))
 
@@ -243,6 +245,10 @@
             pad_ref[ip * 5 + jp, :, 256:384] = behind.astype(BF)
             mine_ref[ip * 5 + jp, :, 0:256] = only_own(own).astype(BF)
             mine_ref[ip * 5 + jp, :, 256:384] = only_own(behind).astype(BF)
+
+    for copy in copies:
+        copy.wait()
+    widen(raw_down_ref, raw_coarse_ref, wd_ref, wc_ref, wt_ref)
 
     outs = []
     for p in range(2):
@@ -416,6 +422,7 @@
 def forward_pass(own, prev, nxt, far, wd, wc):
     vmem = pl.BlockSpec(memory_space=pltpu.VMEM)
     made = (
+        ((9 * 512, 256), BF),
         ((25, FB + 8, 384), BF),
         ((ROWS, 128), F32),
         ((4, HALO, 128), BF),
@@ -427,16 +434,21 @@
     return pl.pallas_call(
         forward,
         out_shape=tuple(jax.ShapeDtypeStruct(*one) for one in made),
-        in_specs=[vmem] * 6,
+        in_specs=[vmem] * 4 + [pl.BlockSpec(memory_space=pltpu.HBM)] * 2,
         out_specs=(vmem,) * len(made),
         scratch_shapes=[
             pltpu.VMEM((4 * FB, UPPER), BF),
             pltpu.VMEM((25, ROWS, 384), BF),
             pltpu.VMEM((ROWS, 1024), BF),
             pltpu.VMEM((8 * CR, 1024), BF),
+            pltpu.VMEM(wd.shape, BF),
+            pltpu.VMEM(wc.shape, BF),
+            pltpu.VMEM((9 * 384, 256), BF),
+            pltpu.VMEM((9 * 512, 256), BF),
+            pltpu.SemaphoreType.DMA((2,)),
         ],
         compiler_params=pltpu.CompilerParams(vmem_limit_bytes=VMEM_A),
-    )(own, prev, nxt, far, wd, wc)
+    )(own, prev, nxt, far, *in_hbm(wd, wc))
 
 
 def backward_pass(*given):
@@ -527,7 +539,8 @@
             for array in (features, cotangent, fine_nbr, parents, coarse_nbr)
         ]
         + [pltpu.SemaphoreType.DMA((5,))],
-    )(place, features, cotangent, fine_nbr, parents, coarse_nbr)
+        compiler_params=pltpu.CompilerParams(vmem_limit_bytes=8 * 2**20),
+    )(place, *in_hbm(features, cotangent, fine_nbr, parents, coarse_nbr))
 
 
 SPACE = ("x", "z")
@@ -599,8 +612,7 @@
     nxt = shift(own, -1)
     cot_prev = shift(cot, 1)
     cot_next = shift(cot, -1)
-    wide_down, wide, turned, own, cot = widened(down_weight, coarse_weight, own, cot)
-    kept = forward_pass(own, prev, nxt, far, wide_down, wide)
+    turned, *kept = forward_pass(own, prev, nxt, far, down_weight, coarse_weight)
     return backward_pass(own, prev, nxt, cot, cot_prev, cot_next, turned, up_weight, *kept)
 
 

time: 99.6 us -> 98.4 us (0.988)
  local copies, waits for them, and re-layouts: 4.9 us -> 0.86 us
  blocking collectives: 51.8 us -> 54.3 us
    unnamed x10 -> x2, local copies, waits for them, and re-layouts: 4.04 us -> 0.01 us
    all_to_all x1, blocking collectives: 26.3 us -> 29.6 us  [spread_sum(): held = lax.all_to_all(held, ('y', 'x'), 0, 0)]
    pallas_call x1, Pallas kernels: 3.77 us -> 5.33 us  [forward_pass(): pl.pallas_call(forward, out_shape=tuple((jax.ShapeDtypeStruct(*one) for o...]
    all_to_all x1, blocking collectives: 19.4 us -> 18 us  [spread_sum(): held = lax.all_to_all(held, 'z', 0, 0)]
where the time goes in v8:
time: 98.4 us; the launch traced here: 98 us
  blocking collectives  54.3 us (55%)
  starting transfers between devices  24.2 us (25%)
  Pallas kernels  13.3 us (14%)
  waiting for transfers between devices  4.07 us (4%)
    all_to_all x1, blocking collectives, spread_sum(): held = lax.all_to_all(held, ('y', 'x'), 0, 0)  29.6 us
    all_to_all x1, blocking collectives, spread_sum(): held = lax.all_to_all(held, 'z', 0, 0)  18 us
    ppermute x5, starting transfers between devices, shift(): return lax.ppermute(block, SPACE, route)  17.9 us
    all_to_all x1, blocking collectives, spread_sum(): held = lax.all_to_all(sums, 'core', 0, 0)  6.62 us
    all_to_all x1, starting transfers between devices, spread_sum(): held = lax.all_to_all(held, ('y', 'core'), 0, 0)  6.32 us
    pallas_call x1, Pallas kernels, backward_pass(): pl.pallas_call(backward, out_shape=(jax.ShapeDtypeStruct((FB, XL), BF), j...  5.38 us
    pallas_call x1, Pallas kernels, forward_pass(): pl.pallas_call(forward, out_shape=tuple((jax.ShapeDtypeStruct(*one) for o...  5.33 us
    all_to_all x1, waiting for transfers between devices, spread_sum(): held = lax.all_to_all(held, ('y', 'core'), 0, 0)  4.06 us
  transfers between devices with their start and end apart: 6, of which 1 were waited for; matrix products, arithmetic and copies ran while one was open for 1% of the time, Pallas kernels for 5%

profile of v8, /device:TPU:1, one launch (start us, length us, event | category | flops | bytes accessed | tf_op | source)
XLA Modules:
  0.0 98.0 jit_solution(5553051681012986767)
XLA Ops:
  0.6 0.0 copy-start
  0.6 1.3 %shard_map.111 = (bf16[24,6016]{1,0:T(8,128)(2,1)S(1)}, bf16[24,2304]{1,0:T(8,128)(2,1)S(1)}, bf16[24,2432]{1,0:T(8,128)(2,1)S(1)}) custom-call(s32[1]{0:T(128)} %bitcast.place_ref, bf16[24,4,4,256]{3,2,1,0:T(4,128)(2,1)} %bitcast.10, bf16[24,4,4,256]{3,2,1,0:T(4,128)(2,1)} %bitcast.11, s32[7,1,24]{2,1,0:T(1,128)} %bitcast.12, s32[1,24]{1,0:T(1,128)} %refs_3_.1, ...), custom_call_target="tpu_custom_call" | custom-call | tf_op jit(solution)/shard_map/pallas_call | solution.py:527
  2.0 1.3 %collective-permute-start.1 = (bf16[24,6016]{1,0:T(8,128)(2,1)S(1)}, bf16[24,6016]{1,0:T(8,128)(2,1)S(1)}, u32[]{:S(2)}, u32[]{:S(2)}) collective-permute-start(bf16[24,6016]{1,0:T(8,128)(2,1)S(1)} %get-tuple-element.20.own_ref), channel_id=1, source_target_pairs={{1,0},{2,1},{3,2},{4,3},{5,4},{6,5},{7,6},{8,7},{9,8},{10,9},{11,1... | collective-permute-start | bytes 866312 | tf_op jit(solution)/shard_map/ppermute | solution.py:552
  3.3 5.0 %collective-permute-start = (bf16[24,6016]{1,0:T(8,128)(2,1)S(1)}, bf16[24,6016]{1,0:T(8,128)(2,1)S(1)}, u32[]{:S(2)}, u32[]{:S(2)}) collective-permute-start(bf16[24,6016]{1,0:T(8,128)(2,1)S(1)} %get-tuple-element.20.own_ref), channel_id=1, source_target_pairs={{0,1},{1,2},{2,3},{3,4},{4,5},{5,6},{6,7},{7,8},{8,9},{9,10},{10,1... | collective-permute-start | bytes 866312 | tf_op jit(solution)/shard_map/ppermute | solution.py:552
  8.3 4.9 %collective-permute-start.4 = (bf16[24,2432]{1,0:T(8,128)(2,1)S(1)}, bf16[24,2432]{1,0:T(8,128)(2,1)S(1)}, u32[]{:S(2)}, u32[]{:S(2)}) collective-permute-start(bf16[24,2432]{1,0:T(8,128)(2,1)S(1)} %get-tuple-element.22), channel_id=1, source_target_pairs={{0,2},{1,3},{2,4},{3,5},{4,6},{5,7},{6,8},{7,9},{8,10},{9,11},{10,... | collective-permute-start | bytes 350216 | tf_op jit(solution)/shard_map/ppermute | solution.py:552
  13.2 1.3 %collective-permute-start.3 = (bf16[24,2304]{1,0:T(8,128)(2,1)S(1)}, bf16[24,2304]{1,0:T(8,128)(2,1)S(1)}, u32[]{:S(2)}, u32[]{:S(2)}) collective-permute-start(bf16[24,2304]{1,0:T(8,128)(2,1)S(1)} %get-tuple-element.21.cot_own_ref), channel_id=1, source_target_pairs={{1,0},{2,1},{3,2},{4,3},{5,4},{6,5},{7,6},{8,7},{9,8},{10,9},{11,1... | collective-permute-start | bytes 331784 | tf_op jit(solution)/shard_map/ppermute | solution.py:552
  14.5 5.4 %collective-permute-start.2 = (bf16[24,2304]{1,0:T(8,128)(2,1)S(1)}, bf16[24,2304]{1,0:T(8,128)(2,1)S(1)}, u32[]{:S(2)}, u32[]{:S(2)}) collective-permute-start(bf16[24,2304]{1,0:T(8,128)(2,1)S(1)} %get-tuple-element.21.cot_own_ref), channel_id=1, source_target_pairs={{0,1},{1,2},{2,3},{3,4},{4,5},{5,6},{6,7},{7,8},{8,9},{9,10},{10,1... | collective-permute-start | bytes 331784 | tf_op jit(solution)/shard_map/ppermute | solution.py:552
  19.9 0.0 collective-permute-done.4.far_ref
  19.9 0.0 collective-permute-done.1.next_ref
  19.9 0.0 collective-permute-done.prev_ref
  19.9 5.3 %shard_map.112 = (bf16[4608,256]{1,0:T(8,128)(2,1)S(1)}, bf16[25,32,384]{2,1,0:T(8,128)(2,1)S(1)}, f32[80,128]{1,0:T(8,128)S(1)}, bf16[4,448,128]{2,1,0:T(8,128)...) custom-call(bf16[24,6016]{1,0:T(8,128)(2,1)S(1)} %get-tuple-element., ...), custom_call_target="tpu_custom_call" | custom-call | tf_op jit(solution)/shard_map/pallas_call | solution.py:434
  25.3 0.0 collective-permute-done.3.cot_next_ref
  25.3 0.0 collective-permute-done.2.cot_prev_ref
  25.3 0.0 copy-done
  25.3 5.4 %shard_map.113 = (bf16[24,4096]{1,0:T(8,128)(2,1)S(1)}, bf16[2,4,64,1536]{3,2,1,0:T(8,128)(2,1)S(1)}) custom-call(bf16[24,6016]{1,0:T(8,128)(2,1)S(1)} %get-tuple-element.20.own_ref, bf16[24,6016]{1,0:T(8,128)(2,1)S(1)} %collective-permute-done.prev_ref, bf16[24,6016]{1,0:T(8,128)(2,1)S(1)} %collective-permute-done.1.next_ref, ...), custom_call_target="tpu_custom_call" | custom-call | tf_op jit(solution)/shard_map/pallas_call | solution.py:456
  30.7 6.6 %all_to_all.20 = bf16[2,4,64,1536]{3,2,1,0:T(8,128)(2,1)S(1)} all-to-all(bf16[2,4,64,1536]{3,2,1,0:T(8,128)(2,1)S(1)} %get-tuple-element.32), channel_id=1, replica_groups=mesh['y'=4,'core'=2,'x'=4,'z'=16] {'core'}, dimensions={0} | all-to-all | bytes 3145728 | tf_op jit(solution)/shard_map/all_to_all | solution.py:569
  37.3 0.3 reduce_sum.24
  37.7 29.6 %all_to_all.21 = bf16[16,16,1536]{2,1,0:T(8,128)(2,1)S(1)} all-to-all(bf16[16,16,1536]{2,1,0:T(8,128)(2,1)S(1)} %bitcast.9), channel_id=1, replica_groups=mesh['y'=4,'core'=2,'x'=4,'z'=16] {'y','x'}, dimensions={0} | all-to-all | bytes 1572864 | tf_op jit(solution)/shard_map/all_to_all | solution.py:572
  67.3 0.1 reduce_sum.25
  67.4 0.1 reshape.32
  67.5 18.0 %all_to_all.22.in_ref = bf16[16,12,128]{2,1,0:T(8,128)(2,1)S(1)} all-to-all(bf16[16,12,128]{2,1,0:T(8,128)(2,1)S(1)} %reshape.32), channel_id=1, replica_groups=mesh['y'=4,'core'=2,'x'=4,'z'=16] {'z'}, dimensions={0} | all-to-all | bytes 98304 | tf_op jit(solution)/shard_map/all_to_all | solution.py:575
  85.5 0.7 shard_map.114
  86.1 6.3 %all-to-all-start.3 = ((f32[8,12,128]{2,1,0:T(8,128)}), f32[8,12,128]{2,1,0:T(8,128)S(1)}, u32[]{:S(2)}, u32[]{:S(2)}) async-start(f32[8,12,128]{2,1,0:T(8,128)} %shard_map.114), calls=%async_computation.3 | async-start | bytes 131072 | tf_op jit(solution)/shard_map/all_to_all | solution.py:581
  92.5 0.8 reshape.30
  93.3 4.1 %all-to-all-done.3.in_ref = f32[8,12,128]{2,1,0:T(8,128)S(1)} async-done(((f32[8,12,128]{2,1,0:T(8,128)}), f32[8,12,128]{2,1,0:T(8,128)S(1)}, u32[]{:S(2)}, u32[]{:S(2)}) %all-to-all-start.3) | async-done | bytes 49184 | tf_op jit(solution)/shard_map/all_to_all | solution.py:581
  97.3 0.6 shard_map.115
Async XLA Ops:
  0.6 24.6 %copy-start = (bf16[128,512]{1,0:T(8,128)(2,1)S(1)}, bf16[128,512]{1,0:T(8,128)(2,1)}, u32[]{:S(2)}) copy-start(bf16[128,512]{1,0:T(8,128)(2,1)} %wu_ref.1) | copy-start | bytes 393220
  2.0 17.9 %collective-permute-start.1 = (bf16[24,6016]{1,0:T(8,128)(2,1)S(1)}, bf16[24,6016]{1,0:T(8,128)(2,1)S(1)}, u32[]{:S(2)}, u32[]{:S(2)}) collective-permute-start(bf16[24,6016]{1,0:T(8,128)(2,1)S(1)} %get-tuple-element.20.own_ref), channel_id=1, source_target_pairs={{1,0},{2,1},{3,2},{4,3},{5,4},{6,5},{7,6},{8,7},{9,8},{10,9},{11,1... | collective-permute-start | bytes 866312 | tf_op jit(solution)/shard_map/ppermute | solution.py:552
  3.3 16.6 %collective-permute-start = (bf16[24,6016]{1,0:T(8,128)(2,1)S(1)}, bf16[24,6016]{1,0:T(8,128)(2,1)S(1)}, u32[]{:S(2)}, u32[]{:S(2)}) collective-permute-start(bf16[24,6016]{1,0:T(8,128)(2,1)S(1)} %get-tuple-element.20.own_ref), channel_id=1, source_target_pairs={{0,1},{1,2},{2,3},{3,4},{4,5},{5,6},{6,7},{7,8},{8,9},{9,10},{10,1... | collective-permute-start | bytes 866312 | tf_op jit(solution)/shard_map/ppermute | solution.py:552
  8.3 11.6 %collective-permute-start.4 = (bf16[24,2432]{1,0:T(8,128)(2,1)S(1)}, bf16[24,2432]{1,0:T(8,128)(2,1)S(1)}, u32[]{:S(2)}, u32[]{:S(2)}) collective-permute-start(bf16[24,2432]{1,0:T(8,128)(2,1)S(1)} %get-tuple-element.22), channel_id=1, source_target_pairs={{0,2},{1,3},{2,4},{3,5},{4,6},{5,7},{6,8},{7,9},{8,10},{9,11},{10,... | collective-permute-start | bytes 350216 | tf_op jit(solution)/shard_map/ppermute | solution.py:552
  13.2 12.1 %collective-permute-start.3 = (bf16[24,2304]{1,0:T(8,128)(2,1)S(1)}, bf16[24,2304]{1,0:T(8,128)(2,1)S(1)}, u32[]{:S(2)}, u32[]{:S(2)}) collective-permute-start(bf16[24,2304]{1,0:T(8,128)(2,1)S(1)} %get-tuple-element.21.cot_own_ref), channel_id=1, source_target_pairs={{1,0},{2,1},{3,2},{4,3},{5,4},{6,5},{7,6},{8,7},{9,8},{10,9},{11,1... | collective-permute-start | bytes 331784 | tf_op jit(solution)/shard_map/ppermute | solution.py:552
  14.5 10.8 %collective-permute-start.2 = (bf16[24,2304]{1,0:T(8,128)(2,1)S(1)}, bf16[24,2304]{1,0:T(8,128)(2,1)S(1)}, u32[]{:S(2)}, u32[]{:S(2)}) collective-permute-start(bf16[24,2304]{1,0:T(8,128)(2,1)S(1)} %get-tuple-element.21.cot_own_ref), channel_id=1, source_target_pairs={{0,1},{1,2},{2,3},{3,4},{4,5},{5,6},{6,7},{7,8},{8,9},{9,10},{10,1... | collective-permute-start | bytes 331784 | tf_op jit(solution)/shard_map/ppermute | solution.py:552
  86.1 11.2 %all-to-all-start.3 = ((f32[8,12,128]{2,1,0:T(8,128)}), f32[8,12,128]{2,1,0:T(8,128)S(1)}, u32[]{:S(2)}, u32[]{:S(2)}) async-start(f32[8,12,128]{2,1,0:T(8,128)} %shard_map.114), calls=%async_computation.3 | async-start | bytes 131072 | tf_op jit(solution)/shard_map/all_to_all | solution.py:581
